TPU v7x, 32 devices: a whole 2x2x4 slice. The times are simulated.
32 devices in a mesh: lon: 8 (over y, x, core), lat: 4 (over z).
Axes of the slice: x: 2, y: 2, z: 4, core: 2. Of those that a mesh axis runs over, the one named last changes fastest.
Arguments:
- velocity: float32 [2, 256, 2048], P(None, 'lat', 'lon'), may hold values from -4 to 4
- stress: float32 [3, 256, 2048], P(None, 'lat', 'lon'), may hold values from -4 to 4
- thickness: float32 [6, 256, 2048], P(None, 'lat', 'lon'), may hold values from 0.1 to 5
- concentration: float32 [6, 256, 2048], P(None, 'lat', 'lon'), may hold values from 0.02 to 0.16
- land_mask: int32 [256, 2048], P('lat', 'lon'), may hold values 0 or 1
- covered: int32 [4, 16], P('lat'), may hold values 0 or 1
- ocean_current: bfloat16 [2, 2, 256, 2048], P(None, None, 'lat', 'lon'), may hold values from -6 to 6
- wind_stress: bfloat16 [2, 2, 256, 2048], P(None, None, 'lat', 'lon'), may hold values from -6 to 6
- regrid_weights: bfloat16 [256, 128], P('lat'), may hold values from -0.5 to 0.5
- tile_offset: int32 [256], P('lat'), may hold values from -1 to 1, as said below
Outputs:
- velocity_out: float32 [2, 256, 2048], P(None, 'lat', 'lon')
- stress_out: float32 [3, 256, 2048], P(None, 'lat', 'lon')
- thickness_out: float32 [6, 256, 2048], P(None, 'lat', 'lon')
Inputs may be any that keep to these rules, and one draw needn't show every extreme that they name: `tile_offset`: never 0; rows of the first tile have +1 and rows of the last tile have -1, so every row reads a tile of the grid.
All inputs are finite; a program needn't handle non-finite values. No bound on the sum of `land_mask` or of `covered` on one device may be relied on, other than what follows from the above.
Results may differ from a plain program's by a relative error of at most 0.0015.
Values may be sent and summed in bfloat16 or wider, within the bound.
No kernel may reach another device: no remote copies, remote signals or barrier semaphores. Data moves between devices by JAX's collectives and lax.ppermute only.
A program may use at most 64 MiB of HBM per device.

v0:
```python
import jax
import jax.numpy as jnp
from jax import lax
from jax.sharding import PartitionSpec as P

BPD = 2
SUB = 4


relax_rate = 0.5
strain_offset = 0.5
time_step = 0.5
water_drag = 1.0
growth_rate = 0.3
mixing_rate = 0.3


def padded(x, sides, width, wrap):
    for axis, dim in sides:
        devices, length = (lax.axis_size(axis), x.shape[dim])
        up = [(i, (i + 1) % devices) for i in range(devices if wrap else devices - 1)]
        down = [(j, i) for i, j in up]
        last = lax.slice_in_dim(x, length - width, length, axis=dim)
        leading = lax.slice_in_dim(x, 0, width, axis=dim)
        before = lax.ppermute(last, axis, up)
        after = lax.ppermute(leading, axis, down)
        x = jnp.concatenate([before, x, after], axis=dim)
    return x


def growth(thick_now, conc_now):
    ice_area = jnp.sum(conc_now, axis=0)
    mean_thick = jnp.sum(conc_now * thick_now, axis=0) / ice_area
    return thick_now + growth_rate / (0.5 + thick_now) + mixing_rate * (mean_thick - thick_now)


def keep_thick(thick_now, conc_now):
    return thick_now


def grow_block(thick_block, conc_block, live):
    return lax.cond(live, growth, keep_thick, thick_block, conc_block)


def forcing(thick_now, conc_now):
    volume = jnp.sum(conc_now * thick_now, axis=0)
    ice_area = jnp.sum(conc_now, axis=0)
    strength = volume * jnp.exp(-2.0 * (1.0 - ice_area))
    return (strength, volume + 0.5)


def new_stress(
    east_u,
    west_u,
    north_u,
    south_u,
    east_v,
    west_v,
    north_v,
    south_v,
    stresses,
    strength,
    open_mask,
):
    stretch_x = (east_u - west_u) / 2.0
    stretch_y = (north_v - south_v) / 2.0
    shear_half = (north_u - south_u + (east_v - west_v)) / 4.0
    divergence = stretch_x + stretch_y
    tension = stretch_x - stretch_y
    shearing = 2.0 * shear_half
    deformation = jnp.sqrt(
        divergence * divergence
        + (tension * tension + shearing * shearing) / 4.0
        + strain_offset * strain_offset
    )
    bulk_stress = (
        (stresses[0] + relax_rate * strength * (divergence / deformation - 1.0))
        / (1.0 + relax_rate)
        * open_mask
    )
    tension_stress = (
        (stresses[1] + relax_rate * strength * tension / (4.0 * deformation))
        / (1.0 + relax_rate)
        * open_mask
    )
    shear_stress = (
        (stresses[2] + relax_rate * strength * shearing / (8.0 * deformation))
        / (1.0 + relax_rate)
        * open_mask
    )
    return jnp.stack([bulk_stress, tension_stress, shear_stress])


def new_velocity(
    sxx_east,
    sxx_west,
    syy_north,
    syy_south,
    sxy_east,
    sxy_west,
    sxy_north,
    sxy_south,
    velocity_now,
    ice_mass,
    current,
    wind_now,
    open_mask,
):
    force_x = (sxx_east - sxx_west) / 2.0 + (sxy_north - sxy_south) / 2.0
    force_y = (sxy_east - sxy_west) / 2.0 + (syy_north - syy_south) / 2.0
    damping = 1.0 + time_step * water_drag / ice_mass
    u = (
        (velocity_now[0] + time_step * (force_x + wind_now[0] + water_drag * current[0]) / ice_mass)
        / damping
        * open_mask
    )
    v = (
        (velocity_now[1] + time_step * (force_y + wind_now[1] + water_drag * current[1]) / ice_mass)
        / damping
        * open_mask
    )
    return jnp.stack([u, v])


def stress_from(wide_velocity, stresses, strength, open_mask):
    u = wide_velocity[0]
    v = wide_velocity[1]
    return new_stress(
        u[1:-1, 2:],
        u[1:-1, :-2],
        u[2:, 1:-1],
        u[:-2, 1:-1],
        v[1:-1, 2:],
        v[1:-1, :-2],
        v[2:, 1:-1],
        v[:-2, 1:-1],
        stresses,
        strength,
        open_mask,
    )


def velocity_from(wide_stress, velocity_now, ice_mass, current, wind_now, open_mask):
    sigma_xx = (wide_stress[0] + wide_stress[1]) / 2.0
    sigma_yy = (wide_stress[0] - wide_stress[1]) / 2.0
    sigma_xy = wide_stress[2]
    return new_velocity(
        sigma_xx[1:-1, 2:],
        sigma_xx[1:-1, :-2],
        sigma_yy[2:, 1:-1],
        sigma_yy[:-2, 1:-1],
        sigma_xy[1:-1, 2:],
        sigma_xy[1:-1, :-2],
        sigma_xy[2:, 1:-1],
        sigma_xy[:-2, 1:-1],
        velocity_now,
        ice_mass,
        current,
        wind_now,
        open_mask,
    )


def trim(field, amount):
    return field[..., amount : field.shape[-2] - amount, amount : field.shape[-1] - amount]


def local(
    velocity,
    stress,
    thickness,
    concentration,
    land_mask,
    covered,
    ocean_current,
    wind_stress,
    regrid_weights,
    tile_offset,
):
    row_count = velocity.shape[1]
    col_count = velocity.shape[2]
    blocks = BPD
    block_cols = col_count // blocks
    lon_pos = lax.axis_index("lon")
    lat_count = lax.axis_size("lat")
    lat_pos = lax.axis_index("lat")
    open_mask = land_mask.astype(jnp.float32)
    beside_all = padded(ocean_current, (("lat", 2),), row_count, False)
    side_weights = regrid_weights[:, row_count:]
    currents = jnp.einsum(
        "ij,wcjx->wcix",
        regrid_weights[:, :row_count],
        ocean_current,
        preferred_element_type=jnp.float32,
    )
    from_lower = jnp.einsum(
        "ij,wcjx->wcix",
        side_weights,
        beside_all[:, :, :row_count],
        preferred_element_type=jnp.float32,
    )
    from_upper = jnp.einsum(
        "ij,wcjx->wcix",
        side_weights,
        beside_all[:, :, 2 * row_count :],
        preferred_element_type=jnp.float32,
    )
    upward = (tile_offset > 0)[:, None]
    currents = currents + jnp.where(upward, from_upper, from_lower)
    own_flags = lax.dynamic_slice_in_dim(covered[0], lon_pos * blocks, blocks)
    thick_now = thickness
    velocity_now = velocity
    stresses = stress
    for window in range(wind_stress.shape[0]):
        pieces = []
        for number in range(blocks):
            columns = slice(number * block_cols, (number + 1) * block_cols)
            pieces.append(
                grow_block(
                    thick_now[:, :, columns], concentration[:, :, columns], own_flags[number] > 0
                )
            )
        thick_now = jnp.concatenate(pieces, axis=2)
        strength, ice_mass = forcing(thick_now, concentration)
        wind_now = wind_stress[window].astype(jnp.float32)
        current = currents[window]
        margin = 2 * SUB
        bundle = jnp.concatenate(
            [
                velocity_now,
                stresses,
                open_mask[None],
                strength[None],
                ice_mass[None],
                current,
                wind_now,
            ],
            axis=0,
        )
        wide = padded(bundle, (("lon", 2), ("lat", 1)), margin, True)
        total_rows = row_count + 2 * margin
        numbers = jnp.arange(total_rows)[:, None]
        outside = (numbers < margin) & (lat_pos == 0) | (numbers >= total_rows - margin) & (
            lat_pos == lat_count - 1
        )
        keep = jnp.where(outside, 0.0, 1.0).astype(jnp.float32)
        wide_velocity = wide[0:2] * keep
        wide_stress = wide[2:5] * keep
        wide_mask = wide[5] * keep
        wide_strength = wide[6]
        wide_mass = wide[7]
        wide_current = wide[8:10]
        wide_wind = wide[10:12]
        have_velocity = margin
        have_stress = margin
        for substep in range(SUB):
            target = have_velocity - 1
            wide_stress = stress_from(
                wide_velocity,
                trim(wide_stress, have_stress - target),
                trim(wide_strength, margin - target),
                trim(wide_mask, margin - target),
            )
            have_stress = target
            target = have_stress - 1
            wide_velocity = velocity_from(
                wide_stress,
                trim(wide_velocity, have_velocity - target),
                trim(wide_mass, margin - target),
                trim(wide_current, margin - target),
                trim(wide_wind, margin - target),
                trim(wide_mask, margin - target),
            )
            have_velocity = target
        velocity_now = wide_velocity
        stresses = trim(wide_stress, have_stress)
    return (velocity_now, stresses, thick_now)


def solution(mesh):
    return jax.shard_map(
        local,
        mesh=mesh,
        in_specs=(
            P(None, "lat", "lon"),
            P(None, "lat", "lon"),
            P(None, "lat", "lon"),
            P(None, "lat", "lon"),
            P("lat", "lon"),
            P("lat", None),
            P(None, None, "lat", "lon"),
            P(None, None, "lat", "lon"),
            P("lat", None),
            P("lat"),
        ),
        out_specs=(P(None, "lat", "lon"), P(None, "lat", "lon"), P(None, "lat", "lon")),
        check_vma=False,
    )
```

profile of v0, /device:TPU:0, one launch (start us, length us, event | category | flops | bytes accessed | tf_op | source)
XLA Modules:
  0.0 69.6 jit_solution(11294176343706646115)
XLA Ops:
  0.6 4.9 %collective-permute-start.1 = (bf16[2,2,64,256]{3,2,1,0:T(8,128)(2,1)}, bf16[2,2,64,256]{3,2,1,0:T(8,128)(2,1)S(1)}, u32[]{:S(2)}, u32[]{:S(2)}) collective-permute-start(bf16[2,2,64,256]{3,2,1,0:T(8,128)(2,1)} %param.24), channel_id=1, source_target_pairs={{0,1},{1,2},{2,3},{4,5},{5,6},{6,7},{8,9},{9,10},{10,11},{12,13},{... | collective-permute-start | bytes 393224 | tf_op jit(solution)/shard_map/ppermute | solution.py:25
  5.6 1.3 %collective-permute-start = (bf16[2,2,64,256]{3,2,1,0:T(8,128)(2,1)}, bf16[2,2,64,256]{3,2,1,0:T(8,128)(2,1)S(1)}, u32[]{:S(2)}, u32[]{:S(2)}) collective-permute-start(bf16[2,2,64,256]{3,2,1,0:T(8,128)(2,1)} %param.24), channel_id=1, source_target_pairs={{1,0},{2,1},{3,2},{5,4},{6,5},{7,6},{9,8},{10,9},{11,10},{13,12},{... | collective-permute-start | bytes 393224 | tf_op jit(solution)/shard_map/ppermute | solution.py:26
  7.0 0.6 fusion.330
  8.2 1.3 %fusion.328 = (f32[6,64,128]{2,1,0:T(8,128)S(1)}, f32[6,64,128]{2,1,0:T(8,128)S(1)}, f32[6,64,128]{2,1,0:T(8,128)S(1)}, f32[6,64,128]{2,1,0:T(8,128)S(1)}) fusion(f32[6,64,256]{2,1,0:T(8,128)} %param.21, f32[6,64,256]{2,1,0:T(8,128)} %param.20), kind=kLoop, calls=%fused_computation.523 | loop fusion | bytes 1572864 | tf_op jit(solution)/shard_map/slice | solution.py:220
  10.7 0.8 %multiply_reduce_fusion.4 = (f32[64,256]{1,0:T(8,128)S(1)}, f32[64,256]{1,0:T(8,128)S(1)}, f32[64,256]{1,0:T(8,128)S(1)}, f32[6,64,256]{2,1,0:T(8,128)}) fusion(f32[6,64,256]{2,1,0:T(8,128)S(1)} %copy-done.1, f32[6,64,128]{2,1,0:T(8,128)S(1)} %get-tuple-element.144, f32[6,64,128]{2,1,0:T(8,128)S(1)} %get-tuple-element.143, ...), kind=kLoop, calls=%fused_computation.16 | loop fusion | flops 638976 | bytes 1769472 | tf_op jit(solution)/shard_map/reduce_sum | solution.py:46
  12.0 0.6 collective-permute-done
  13.2 2.6 %collective-permute-start.3 = (f32[12,64,8]{2,1,0:T(8,128)S(1)}, f32[12,64,8]{2,1,0:T(8,128)S(1)}, u32[]{:S(2)}, u32[]{:S(2)}) collective-permute-start(f32[12,64,8]{2,1,0:T(8,128)S(1)} %get-tuple-element.126), channel_id=1, source_target_pairs={{4,0},{8,4},{12,8},{16,12},{20,16},{24,20},{28,24},{0,28},{5,1},{9... | collective-permute-start | bytes 73736 | tf_op jit(solution)/shard_map/ppermute | solution.py:26
  15.8 7.7 %collective-permute-done.2 = f32[12,64,8]{2,1,0:T(8,128)S(1)} collective-permute-done((f32[12,64,8]{2,1,0:T(8,128)S(1)}, f32[12,64,8]{2,1,0:T(8,128)S(1)}, u32[]{:S(2)}, u32[]{:S(2)}) %collective-permute-start.2) | collective-permute-done | bytes 24608 | tf_op jit(solution)/shard_map/ppermute | solution.py:25
  23.8 2.6 %collective-permute-start.4 = (f32[12,8,272]{2,1,0:T(8,128)S(1)}, f32[12,8,272]{2,1,0:T(8,128)S(1)}, u32[]{:S(2)}, u32[]{:S(2)}) collective-permute-start(f32[12,8,272]{2,1,0:T(8,128)S(1)} %get-tuple-element.117), channel_id=1, source_target_pairs={{0,1},{1,2},{2,3},{3,0},{4,5},{5,6},{6,7},{7,4},{8,9},{9,10},{10,1... | collective-permute-start | bytes 313352 | tf_op jit(solution)/shard_map/ppermute | solution.py:25
  26.4 1.8 %collective-permute-start.5 = (f32[12,8,272]{2,1,0:T(8,128)S(1)}, f32[12,8,272]{2,1,0:T(8,128)S(1)}, u32[]{:S(2)}, u32[]{:S(2)}) collective-permute-start(f32[12,8,272]{2,1,0:T(8,128)S(1)} %get-tuple-element.118), channel_id=1, source_target_pairs={{1,0},{2,1},{3,2},{0,3},{5,4},{6,5},{7,6},{4,7},{9,8},{10,9},{11,1... | collective-permute-start | bytes 313352 | tf_op jit(solution)/shard_map/ppermute | solution.py:26
  28.2 3.8 %collective-permute-done.4 = f32[12,8,272]{2,1,0:T(8,128)S(1)} collective-permute-done((f32[12,8,272]{2,1,0:T(8,128)S(1)}, f32[12,8,272]{2,1,0:T(8,128)S(1)}, u32[]{:S(2)}, u32[]{:S(2)}) %collective-permute-start.4) | collective-permute-done | bytes 104480 | tf_op jit(solution)/shard_map/ppermute | solution.py:25
  32.0 3.9 %collective-permute-done.5 = f32[12,8,272]{2,1,0:T(8,128)S(1)} collective-permute-done((f32[12,8,272]{2,1,0:T(8,128)S(1)}, f32[12,8,272]{2,1,0:T(8,128)S(1)}, u32[]{:S(2)}, u32[]{:S(2)}) %collective-permute-start.5) | collective-permute-done | bytes 104480 | tf_op jit(solution)/shard_map/ppermute | solution.py:26
  37.4 0.6 fusion.78
  38.6 0.5 fusion.216
  39.7 0.5 fusion.185
  41.8 2.5 %collective-permute-start.7 = (f32[12,64,8]{2,1,0:T(8,128)S(1)}, f32[12,64,8]{2,1,0:T(8,128)S(1)}, u32[]{:S(2)}, u32[]{:S(2)}) collective-permute-start(f32[12,64,8]{2,1,0:T(8,128)S(1)} %get-tuple-element.124), channel_id=1, source_target_pairs={{4,0},{8,4},{12,8},{16,12},{20,16},{24,20},{28,24},{0,28},{5,1},{9... | collective-permute-start | bytes 73736 | tf_op jit(solution)/shard_map/ppermute | solution.py:26
  44.3 8.6 %collective-permute-done.6 = f32[12,64,8]{2,1,0:T(8,128)S(1)} collective-permute-done((f32[12,64,8]{2,1,0:T(8,128)S(1)}, f32[12,64,8]{2,1,0:T(8,128)S(1)}, u32[]{:S(2)}, u32[]{:S(2)}) %collective-permute-start.6) | collective-permute-done | bytes 24608 | tf_op jit(solution)/shard_map/ppermute | solution.py:25
  53.1 3.8 %collective-permute-start.9 = (f32[12,8,272]{2,1,0:T(8,128)S(1)}, f32[12,8,272]{2,1,0:T(8,128)S(1)}, u32[]{:S(2)}, u32[]{:S(2)}) collective-permute-start(f32[12,8,272]{2,1,0:T(8,128)S(1)} %get-tuple-element.116), channel_id=1, source_target_pairs={{1,0},{2,1},{3,2},{0,3},{5,4},{6,5},{7,6},{4,7},{9,8},{10,9},{11,1... | collective-permute-start | bytes 313352 | tf_op jit(solution)/shard_map/ppermute | solution.py:26
  56.9 4.8 %collective-permute-done.8 = f32[12,8,272]{2,1,0:T(8,128)S(1)} collective-permute-done((f32[12,8,272]{2,1,0:T(8,128)S(1)}, f32[12,8,272]{2,1,0:T(8,128)S(1)}, u32[]{:S(2)}, u32[]{:S(2)}) %collective-permute-start.8) | collective-permute-done | bytes 104480 | tf_op jit(solution)/shard_map/ppermute | solution.py:25
  61.7 1.2 %collective-permute-done.9 = f32[12,8,272]{2,1,0:T(8,128)S(1)} collective-permute-done((f32[12,8,272]{2,1,0:T(8,128)S(1)}, f32[12,8,272]{2,1,0:T(8,128)S(1)}, u32[]{:S(2)}, u32[]{:S(2)}) %collective-permute-start.9) | collective-permute-done | bytes 104480 | tf_op jit(solution)/shard_map/ppermute | solution.py:26
  64.4 0.6 fusion.33
  65.6 0.5 fusion.154
  68.1 0.7 pad_maximum_fusion.13
  68.8 0.8 %pad_maximum_fusion.3 = f32[3,64,256]{2,1,0:T(8,128)} fusion(f32[1,66,258]{2,1,0:T(8,128)S(1)} %bitcast.745, f32[1,66,258]{2,1,0:T(8,128)S(1)} %bitcast.754, f32[1,66,258]{2,1,0:T(8,128)S(1)} %bitcast.755), kind=kLoop, calls=%fused_computation.21 | loop fusion | flops 98304 | bytes 400944 | tf_op jit(solution)/shard_map/stack | solution.py:91
  (94 shorter events, 9.9 us)
Async XLA Ops:
  0.6 6.3 %copy-start = (s32[1,16]{1,0:T(1,128)S(1)}, s32[1,16]{1,0:T(1,128)}, u32[]{:S(2)}) copy-start(s32[1,16]{1,0:T(1,128)} %param.23) | copy-start | bytes 196
  0.6 11.1 %collective-permute-start.1 = (bf16[2,2,64,256]{3,2,1,0:T(8,128)(2,1)}, bf16[2,2,64,256]{3,2,1,0:T(8,128)(2,1)S(1)}, u32[]{:S(2)}, u32[]{:S(2)}) collective-permute-start(bf16[2,2,64,256]{3,2,1,0:T(8,128)(2,1)} %param.24), channel_id=1, source_target_pairs={{0,1},{1,2},{2,3},{4,5},{5,6},{6,7},{8,9},{9,10},{10,11},{12,13},{... | collective-permute-start | bytes 393224 | tf_op jit(solution)/shard_map/ppermute | solution.py:25
  5.6 7.1 %collective-permute-start = (bf16[2,2,64,256]{3,2,1,0:T(8,128)(2,1)}, bf16[2,2,64,256]{3,2,1,0:T(8,128)(2,1)S(1)}, u32[]{:S(2)}, u32[]{:S(2)}) collective-permute-start(bf16[2,2,64,256]{3,2,1,0:T(8,128)(2,1)} %param.24), channel_id=1, source_target_pairs={{1,0},{2,1},{3,2},{5,4},{6,5},{7,6},{9,8},{10,9},{11,10},{13,12},{... | collective-permute-start | bytes 393224 | tf_op jit(solution)/shard_map/ppermute | solution.py:26
  9.6 0.9 %copy-start.7 = (f32[2,64,256]{2,1,0:T(8,128)S(1)}, f32[2,64,256]{2,1,0:T(8,128)}, u32[]{:S(2)}) copy-start(f32[2,64,256]{2,1,0:T(8,128)} %param.18) | copy-start | bytes 393220
  9.6 1.1 %copy-start.1 = (f32[6,64,256]{2,1,0:T(8,128)S(1)}, f32[6,64,256]{2,1,0:T(8,128)}, u32[]{:S(2)}) copy-start(f32[6,64,256]{2,1,0:T(8,128)} %param.21) | copy-start | bytes 1179652
  10.3 1.2 %copy-start.4 = (f32[3,64,256]{2,1,0:T(8,128)S(1)}, f32[3,64,256]{2,1,0:T(8,128)}, u32[]{:S(2)}) copy-start(f32[3,64,256]{2,1,0:T(8,128)} %param.19) | copy-start | bytes 589828
  10.4 1.1 %copy-start.3 = (s32[64,256]{1,0:T(8,128)S(1)}, s32[64,256]{1,0:T(8,128)}, u32[]{:S(2)}) copy-start(s32[64,256]{1,0:T(8,128)} %param.22) | copy-start | bytes 196612
  10.4 1.2 %copy-start.5 = (bf16[64,128]{1,0:T(8,128)(2,1)S(1)}, bf16[64,128]{1,0:T(8,128)(2,1)}, u32[]{:S(2)}) copy-start(bf16[64,128]{1,0:T(8,128)(2,1)} %param.26) | copy-start | bytes 49156
  10.4 1.2 %copy-start.6 = (bf16[2,2,64,256]{3,2,1,0:T(8,128)(2,1)S(1)}, bf16[2,2,64,256]{3,2,1,0:T(8,128)(2,1)}, u32[]{:S(2)}) copy-start(bf16[2,2,64,256]{3,2,1,0:T(8,128)(2,1)} %param.24) | copy-start | bytes 393220
  10.7 1.1 %copy-start.8 = (s32[64]{0:T(128)S(1)}, s32[64]{0:T(128)}, u32[]{:S(2)}) copy-start(s32[64]{0:T(128)} %param.27) | copy-start | bytes 772
  11.5 1.4 %copy-start.2 = (bf16[2,2,64,256]{3,2,1,0:T(8,128)(2,1)S(1)}, bf16[2,2,64,256]{3,2,1,0:T(8,128)(2,1)}, u32[]{:S(2)}) copy-start(bf16[2,2,64,256]{3,2,1,0:T(8,128)(2,1)} %param.25) | copy-start | bytes 393220
  13.1 10.5 %collective-permute-start.2 = (f32[12,64,8]{2,1,0:T(8,128)S(1)}, f32[12,64,8]{2,1,0:T(8,128)S(1)}, u32[]{:S(2)}, u32[]{:S(2)}) collective-permute-start(f32[12,64,8]{2,1,0:T(8,128)S(1)} %get-tuple-element.125), channel_id=1, source_target_pairs={{0,4},{4,8},{8,12},{12,16},{16,20},{20,24},{24,28},{28,0},{1,5},{5... | collective-permute-start | bytes 73736 | tf_op jit(solution)/shard_map/ppermute | solution.py:25
  13.2 10.4 %collective-permute-start.3 = (f32[12,64,8]{2,1,0:T(8,128)S(1)}, f32[12,64,8]{2,1,0:T(8,128)S(1)}, u32[]{:S(2)}, u32[]{:S(2)}) collective-permute-start(f32[12,64,8]{2,1,0:T(8,128)S(1)} %get-tuple-element.126), channel_id=1, source_target_pairs={{4,0},{8,4},{12,8},{16,12},{20,16},{24,20},{28,24},{0,28},{5,1},{9... | collective-permute-start | bytes 73736 | tf_op jit(solution)/shard_map/ppermute | solution.py:26
  23.8 8.2 %collective-permute-start.4 = (f32[12,8,272]{2,1,0:T(8,128)S(1)}, f32[12,8,272]{2,1,0:T(8,128)S(1)}, u32[]{:S(2)}, u32[]{:S(2)}) collective-permute-start(f32[12,8,272]{2,1,0:T(8,128)S(1)} %get-tuple-element.117), channel_id=1, source_target_pairs={{0,1},{1,2},{2,3},{3,0},{4,5},{5,6},{6,7},{7,4},{8,9},{9,10},{10,1... | collective-permute-start | bytes 313352 | tf_op jit(solution)/shard_map/ppermute | solution.py:25
  26.4 9.5 %collective-permute-start.5 = (f32[12,8,272]{2,1,0:T(8,128)S(1)}, f32[12,8,272]{2,1,0:T(8,128)S(1)}, u32[]{:S(2)}, u32[]{:S(2)}) collective-permute-start(f32[12,8,272]{2,1,0:T(8,128)S(1)} %get-tuple-element.118), channel_id=1, source_target_pairs={{1,0},{2,1},{3,2},{0,3},{5,4},{6,5},{7,6},{4,7},{9,8},{10,9},{11,1... | collective-permute-start | bytes 313352 | tf_op jit(solution)/shard_map/ppermute | solution.py:26
  41.6 11.3 %collective-permute-start.6 = (f32[12,64,8]{2,1,0:T(8,128)S(1)}, f32[12,64,8]{2,1,0:T(8,128)S(1)}, u32[]{:S(2)}, u32[]{:S(2)}) collective-permute-start(f32[12,64,8]{2,1,0:T(8,128)S(1)} %get-tuple-element.123), channel_id=1, source_target_pairs={{0,4},{4,8},{8,12},{12,16},{16,20},{20,24},{24,28},{28,0},{1,5},{5... | collective-permute-start | bytes 73736 | tf_op jit(solution)/shard_map/ppermute | solution.py:25
  41.8 11.1 %collective-permute-start.7 = (f32[12,64,8]{2,1,0:T(8,128)S(1)}, f32[12,64,8]{2,1,0:T(8,128)S(1)}, u32[]{:S(2)}, u32[]{:S(2)}) collective-permute-start(f32[12,64,8]{2,1,0:T(8,128)S(1)} %get-tuple-element.124), channel_id=1, source_target_pairs={{4,0},{8,4},{12,8},{16,12},{20,16},{24,20},{28,24},{0,28},{5,1},{9... | collective-permute-start | bytes 73736 | tf_op jit(solution)/shard_map/ppermute | solution.py:26
  53.0 8.7 %collective-permute-start.8 = (f32[12,8,272]{2,1,0:T(8,128)S(1)}, f32[12,8,272]{2,1,0:T(8,128)S(1)}, u32[]{:S(2)}, u32[]{:S(2)}) collective-permute-start(f32[12,8,272]{2,1,0:T(8,128)S(1)} %get-tuple-element.115), channel_id=1, source_target_pairs={{0,1},{1,2},{2,3},{3,0},{4,5},{5,6},{6,7},{7,4},{8,9},{9,10},{10,1... | collective-permute-start | bytes 313352 | tf_op jit(solution)/shard_map/ppermute | solution.py:25
  53.1 9.8 %collective-permute-start.9 = (f32[12,8,272]{2,1,0:T(8,128)S(1)}, f32[12,8,272]{2,1,0:T(8,128)S(1)}, u32[]{:S(2)}, u32[]{:S(2)}) collective-permute-start(f32[12,8,272]{2,1,0:T(8,128)S(1)} %get-tuple-element.116), channel_id=1, source_target_pairs={{1,0},{2,1},{3,2},{0,3},{5,4},{6,5},{7,6},{4,7},{9,8},{10,9},{11,1... | collective-permute-start | bytes 313352 | tf_op jit(solution)/shard_map/ppermute | solution.py:26
where the time goes:
time: 70.2 us; the launch traced here: 69.6 us
  waiting for transfers between devices  30.7 us (44%)
  starting transfers between devices  19.9 us (28%)
  other arithmetic  13 us (19%)
  local copies, waits for them, and re-layouts  2.71 us (4%)
  between operations  2.58 us (4%)
    ppermute x5, waiting for transfers between devices, padded(): before = lax.ppermute(last, axis, up)  24.9 us
    ppermute x5, starting transfers between devices, padded(): after = lax.ppermute(leading, axis, down)  12 us
    ppermute x5, starting transfers between devices, padded(): before = lax.ppermute(last, axis, up)  7.85 us
    ppermute x5, waiting for transfers between devices, padded(): after = lax.ppermute(leading, axis, down)  5.78 us
    mul x6, other arithmetic, new_velocity(): (velocity_now[0] + time_step * (force_x + wind_now[0] + water_drag * curr...  3.19 us
    div x8, other arithmetic, velocity_from(): sigma_yy = (wide_stress[0] - wide_stress[1]) / 2.0  1.74 us
    div x8, other arithmetic, velocity_from(): sigma_xx = (wide_stress[0] + wide_stress[1]) / 2.0  1.74 us
  transfers between devices with their start and end apart: 10, of which 7 were waited for; matrix products, arithmetic and copies ran while one was open for 5% of the time, Pallas kernels for 0%

commit v1 on v0

v1 whole, which is shorter than its diff:
```python
import jax
import jax.numpy as jnp
from jax import lax
from jax.experimental import pallas as pl
from jax.experimental.pallas import tpu as pltpu
from jax.sharding import PartitionSpec as P

BLK = 128
SUB = 4
LANES = 128
PAD = 8
STATE = 5
COEF = 4
VMEM_LIMIT = 16 * 1024 * 1024

growth_rate = 0.3
mixing_rate = 0.3


def total(terms):
    result = terms[0]
    for term in terms[1:]:
        result = result + term
    return result


def growth_kernel(covered_ref, thick_ref, conc_ref, mask_ref, thick_out_ref, coef_ref):
    cats, rows, cols = thick_ref.shape
    blocks = cols // BLK
    first = lax.axis_index("lon") * blocks
    step = 16
    for block in range(blocks):
        live = covered_ref[0, first + block] > 0
        lanes = slice(block * BLK, (block + 1) * BLK)
        for row in range(0, rows, step):
            at = slice(row, row + step)
            conc = [conc_ref[c, at, lanes] for c in range(cats)]
            thick = [thick_ref[c, at, lanes] for c in range(cats)]
            mask = mask_ref[at, lanes].astype(jnp.float32)
            area = total(conc)
            inverse = 1.0 / area
            factor = jnp.exp(-2.0 * (1.0 - area)) * (mask * (1.0 / 3.0))
            half = 0.5 * mask
            volume = total([c * h for c, h in zip(conc, thick)])
            for window in range(coef_ref.shape[0] // 2):
                mean = volume * inverse
                grown = [h + growth_rate / (0.5 + h) + mixing_rate * (mean - h) for h in thick]
                thick = [jnp.where(live, g, h) for g, h in zip(grown, thick)]
                volume = total([c * h for c, h in zip(conc, thick)])
                coef_ref[2 * window, at, lanes] = volume * factor
                coef_ref[2 * window + 1, at, lanes] = half / (volume + 1.0)
            for c in range(cats):
                thick_out_ref[c, at, lanes] = thick[c]


def slots(depth):
    return LANES // depth


def message_plan(margin, windows):
    plan = [(f, margin) for f in range(STATE)]
    for window in range(windows):
        plan += [(STATE + COEF * window + k, margin - 2 * SUB * window) for k in range(COEF)]
    return plan


def pack_kernel(
    offset_ref,
    weights_ref,
    own_ref,
    lower_ref,
    upper_ref,
    wind_ref,
    coef_ref,
    velocity_ref,
    stress_ref,
    mask_ref,
    fields_ref,
    east_ref,
    west_ref,
    north_ref,
    south_ref,
):
    windows, _, rows, cols = own_ref.shape
    margin = 2 * SUB * windows
    up = offset_ref[...] > 0
    square = (rows, rows)
    diagonal = lax.broadcasted_iota(jnp.int32, square, 0) == lax.broadcasted_iota(
        jnp.int32, square, 1
    )
    upward = jnp.where(diagonal & up, 1.0, 0.0).astype(jnp.bfloat16)
    downward = jnp.where(diagonal & jnp.logical_not(up), 1.0, 0.0).astype(jnp.bfloat16)
    own_weights = weights_ref[:, :rows]
    side = weights_ref[:, rows:]

    def dot(a, b):
        return jnp.dot(a, b, preferred_element_type=jnp.float32)

    up_weights = dot(upward, side).astype(jnp.bfloat16)
    down_weights = dot(downward, side).astype(jnp.bfloat16)
    mask = mask_ref[...].astype(jnp.float32)
    fields_ref[0] = velocity_ref[0]
    fields_ref[1] = velocity_ref[1]
    fields_ref[2] = (stress_ref[0] + stress_ref[1]) * mask
    fields_ref[3] = (stress_ref[0] - stress_ref[1]) * mask
    fields_ref[4] = (stress_ref[2] + stress_ref[2]) * mask
    for w in range(windows):
        base = STATE + COEF * w
        fields_ref[base] = coef_ref[2 * w]
        b = coef_ref[2 * w + 1]
        fields_ref[base + 1] = b
        for k in range(2):
            current = (
                dot(own_weights, own_ref[w, k])
                + dot(up_weights, upper_ref[w, k])
                + dot(down_weights, lower_ref[w, k])
            )
            fields_ref[base + 2 + k] = b * (wind_ref[w, k].astype(jnp.float32) + current)

    count = fields_ref.shape[0]
    per = slots(margin)
    lane = lax.broadcasted_iota(jnp.int32, (rows, LANES), 1) // margin
    for group in range(-(-count // per)):
        eastward = jnp.zeros((rows, LANES), jnp.float32)
        westward = jnp.zeros((rows, LANES), jnp.float32)
        for slot in range(min(per, count - group * per)):
            field = group * per + slot
            last = fields_ref[field, :, cols - LANES :]
            leading = fields_ref[field, :, :LANES]
            here = lane == slot
            shift = slot * margin
            last = pltpu.roll(last, (shift + margin) % LANES, 1)
            leading = pltpu.roll(leading, shift, 1) if shift else leading
            eastward = jnp.where(here, last, eastward)
            westward = jnp.where(here, leading, westward)
        lanes = slice(group * LANES, (group + 1) * LANES)
        east_ref[:, lanes] = eastward.astype(jnp.bfloat16)
        west_ref[:, lanes] = westward.astype(jnp.bfloat16)

    row, held_north, held_south, held = 0, [], [], 0
    for field, depth in message_plan(margin, windows):
        held_north.append(fields_ref[field, rows - depth :, :])
        held_south.append(fields_ref[field, :depth, :])
        held += depth
        if held % 16 == 0:
            join = (lambda x: x[0] if len(x) == 1 else jnp.concatenate(x, axis=0))
            north_ref[row : row + held] = join(held_north).astype(jnp.bfloat16)
            south_ref[row : row + held] = join(held_south).astype(jnp.bfloat16)
            row, held_north, held_south, held = row + held, [], [], 0
    tail = north_ref.shape[0] - row
    north_ref[row:] = jnp.zeros((tail, cols), jnp.bfloat16)
    south_ref[row:] = jnp.zeros((tail, cols), jnp.bfloat16)


def dynamics_kernel(
    fields_ref,
    east_ref,
    west_ref,
    north_ref,
    south_ref,
    velocity_ref,
    stress_ref,
    state,
    strength,
    keep,
    push,
    force,
):
    count, rows, cols = fields_ref.shape
    windows = strength.shape[0]
    margin = 2 * SUB * windows
    own_tiles = cols // LANES
    tiles = own_tiles + 1
    per = slots(margin)
    top = PAD + margin
    bottom = top + rows
    lane = lax.broadcasted_iota(jnp.int32, (8, LANES), 1)

    def place(field, tile, row, value):
        at = slice(row, row + value.shape[0])
        if field < STATE:
            state[field, tile, at, :] = value
            return
        window, kind = divmod(field - STATE, COEF)
        if kind == 0:
            strength[window, tile, at, :] = value
        elif kind == 1:
            push[window, tile, at, :] = value
            keep[window, tile, at, :] = jnp.where(value > 0.0, 1.0 - value, 0.0)
        else:
            force[window, kind - 2, tile, at, :] = value

    zero = jnp.zeros((PAD, LANES), jnp.float32)
    for tile in range(tiles):
        for field in range(STATE):
            state[field, tile, 0:PAD, :] = zero
            state[field, tile, bottom + margin : bottom + margin + PAD, :] = zero

    def side_tile(field, east, west, row, depth, skip):
        group, slot = divmod(field, per)
        lanes = slice(group * LANES, (group + 1) * LANES)
        from_east = east[:, lanes].astype(jnp.float32)
        from_west = west[:, lanes].astype(jnp.float32)
        shift = slot * margin
        if shift:
            from_east = pltpu.roll(from_east, LANES - shift, 1)
        back = (LANES - margin - shift) % LANES
        if back:
            from_west = pltpu.roll(from_west, back, 1)
        wide = lax.broadcasted_iota(jnp.int32, from_east.shape, 1)
        value = jnp.where(
            wide < margin, from_east, jnp.where(wide >= LANES - margin, from_west, 0.0)
        )
        place(field, own_tiles, row, value[skip : skip + depth])

    plan = message_plan(margin, windows)
    corner = sum(depth for _, depth in plan)
    for field in range(count):
        for tile in range(own_tiles):
            lanes = slice(tile * LANES, (tile + 1) * LANES)
            place(field, tile, top, fields_ref[field, :, lanes])
        side_tile(field, east_ref[...], west_ref[...], top, rows, 0)
    for ref, is_north in ((north_ref, True), (south_ref, False)):
        row = 0
        east = ref[corner : corner + margin]
        west = ref[corner + margin : corner + 2 * margin]
        for field, depth in plan:
            begin = row // 16 * 16
            value = ref[begin : begin + 16].astype(jnp.float32)
            value = value[row - begin : row - begin + depth]
            to = bottom if is_north else top - depth
            for tile in range(own_tiles):
                lanes = slice(tile * LANES, (tile + 1) * LANES)
                place(field, tile, to, value[:, lanes])
            side_tile(field, east, west, to, depth, 0 if is_north else margin - depth)
            row += depth

    first_lane = lane == 0
    last_lane = lane == LANES - 1

    def across(values):
        ahead = [pltpu.roll(x, LANES - 1, 1) for x in values]
        behind = [pltpu.roll(x, 1, 1) for x in values]
        return [
            jnp.where(last_lane, ahead[(j + 1) % tiles], ahead[j])
            - jnp.where(first_lane, behind[j - 1], behind[j])
            for j in range(tiles)
        ]

    def along(field, tile, row):
        return state[field, tile, row + 1 : row + 9, :] - state[field, tile, row - 1 : row + 7, :]

    every = range(tiles)
    for window in range(windows):
        spare = 2 * SUB * window
        row_list = range(top - margin + spare, bottom + margin - spare, 8)

        def subcycle(_, carry):
            for row in row_list:
                at = slice(row, row + 8)
                u_x = across([state[0, j, at, :] for j in every])
                v_x = across([state[1, j, at, :] for j in every])
                for j in every:
                    u_y = along(0, j, row)
                    v_y = along(1, j, row)
                    shear = u_y + v_x[j]
                    spread = u_x[j] + v_y
                    tension = u_x[j] - v_y
                    tension4 = tension * 0.25
                    shear4 = shear * 0.25
                    squares = spread * spread + tension * tension4 + (shear * shear4 + 1.0)
                    k = strength[window, j, at, :]
                    kr = k * lax.rsqrt(squares)
                    state[2, j, at, :] = state[2, j, at, :] * (2.0 / 3.0) + (
                        kr * (spread + tension4) - k
                    )
                    state[3, j, at, :] = state[3, j, at, :] * (2.0 / 3.0) + (
                        kr * (spread - tension4) - k
                    )
                    state[4, j, at, :] = state[4, j, at, :] * (2.0 / 3.0) + kr * shear4
            for row in row_list:
                at = slice(row, row + 8)
                p_x = across([state[2, j, at, :] for j in every])
                t_x = across([state[4, j, at, :] for j in every])
                for j in every:
                    b = push[window, j, at, :] * 0.25
                    a = keep[window, j, at, :]
                    state[0, j, at, :] = (
                        a * state[0, j, at, :]
                        + b * (p_x[j] + along(4, j, row))
                        + force[window, 0, j, at, :]
                    )
                    state[1, j, at, :] = (
                        a * state[1, j, at, :]
                        + b * (t_x[j] + along(3, j, row))
                        + force[window, 1, j, at, :]
                    )
            return carry

        lax.fori_loop(0, SUB, subcycle, 0)

    for tile in range(own_tiles):
        lanes = slice(tile * LANES, (tile + 1) * LANES)
        for row in range(0, rows, 8):
            at = slice(row, row + 8)
            to = slice(top + row, top + row + 8)
            velocity_ref[0, at, lanes] = state[0, tile, to, :]
            velocity_ref[1, at, lanes] = state[1, tile, to, :]
            p = state[2, tile, to, :]
            q = state[3, tile, to, :]
            stress_ref[0, at, lanes] = (p + q) * 0.5
            stress_ref[1, at, lanes] = (p - q) * 0.5
            stress_ref[2, at, lanes] = state[4, tile, to, :] * 0.5


def params():
    return pltpu.CompilerParams(vmem_limit_bytes=VMEM_LIMIT)


def shift_pairs(axis, step, wrap):
    n = lax.axis_size(axis)
    return [(i, (i + step) % n) for i in range(n) if wrap or 0 <= i + step < n]


def shape(dims, dtype=jnp.float32):
    return jax.ShapeDtypeStruct(dims, dtype)


def local(
    velocity,
    stress,
    thickness,
    concentration,
    land_mask,
    covered,
    ocean_current,
    wind_stress,
    regrid_weights,
    tile_offset,
):
    _, rows, cols = velocity.shape
    windows = wind_stress.shape[0]
    margin = 2 * SUB * windows
    count = STATE + COEF * windows
    tiles = cols // LANES + 1

    lower = lax.ppermute(ocean_current, "lat", shift_pairs("lat", 1, False))
    upper = lax.ppermute(ocean_current, "lat", shift_pairs("lat", -1, False))

    whole = pl.BlockSpec(memory_space=pltpu.VMEM)
    thick_out, coef = pl.pallas_call(
        growth_kernel,
        out_shape=(shape(thickness.shape), shape((2 * windows, rows, cols))),
        in_specs=[pl.BlockSpec(memory_space=pltpu.SMEM)] + [whole] * 3,
        out_specs=(whole, whole),
        compiler_params=params(),
        cost_estimate=pl.CostEstimate(
            flops=100 * thickness.size, bytes_accessed=12 * thickness.size, transcendentals=0
        ),
        name="growth",
    )(covered, thickness, concentration, land_mask)

    plan = message_plan(margin, windows)
    body = sum(depth for _, depth in plan)
    packed = -(-count // slots(margin)) * LANES
    bf16 = jnp.bfloat16
    fields, eastward, westward, northward, southward = pl.pallas_call(
        pack_kernel,
        out_shape=(
            shape((count, rows, cols)),
            shape((rows, packed), bf16),
            shape((rows, packed), bf16),
            shape((body + 2 * margin, cols), bf16),
            shape((body + 2 * margin, cols), bf16),
        ),
        in_specs=[whole] * 10,
        out_specs=(whole,) * 5,
        compiler_params=params(),
        name="pack",
    )(
        tile_offset.reshape(1, rows),
        regrid_weights,
        ocean_current,
        lower,
        upper,
        wind_stress,
        coef,
        velocity,
        stress,
        land_mask,
    )

    from_west = lax.ppermute(eastward, "lon", shift_pairs("lon", 1, True))
    from_east = lax.ppermute(westward, "lon", shift_pairs("lon", -1, True))
    for number, side in enumerate((from_east, from_west)):
        at = body + number * margin
        northward = northward.at[at : at + margin, :packed].set(side[rows - margin :])
        southward = southward.at[at : at + margin, :packed].set(side[:margin])
    from_south = lax.ppermute(northward, "lat", shift_pairs("lat", 1, False))
    from_north = lax.ppermute(southward, "lat", shift_pairs("lat", -1, False))

    height = rows + 2 * margin + 2 * PAD

    def scratch(*lead):
        return pltpu.VMEM((*lead, tiles, height, LANES), jnp.float32)

    velocity_out, stress_out = pl.pallas_call(
        dynamics_kernel,
        out_shape=(shape(velocity.shape), shape(stress.shape)),
        in_specs=[whole] * 5,
        out_specs=(whole, whole),
        scratch_shapes=[
            scratch(STATE),
            scratch(windows),
            scratch(windows),
            scratch(windows),
            scratch(windows, 2),
        ],
        compiler_params=params(),
        name="dynamics",
    )(fields, from_east, from_west, from_north, from_south)
    return (velocity_out, stress_out, thick_out)


def solution(mesh):
    return jax.shard_map(
        local,
        mesh=mesh,
        in_specs=(
            P(None, "lat", "lon"),
            P(None, "lat", "lon"),
            P(None, "lat", "lon"),
            P(None, "lat", "lon"),
            P("lat", "lon"),
            P("lat", None),
            P(None, None, "lat", "lon"),
            P(None, None, "lat", "lon"),
            P("lat", None),
            P("lat"),
        ),
        out_specs=(P(None, "lat", "lon"), P(None, "lat", "lon"), P(None, "lat", "lon")),
        check_vma=False,
    )
```

time: 70.2 us -> 34.2 us (0.49)
  waiting for transfers between devices: 30.7 us -> 10.2 us
  other arithmetic: 13 us -> 0 us
  starting transfers between devices: 19.9 us -> 12.8 us
  Pallas kernels: 0 us -> 5.98 us
  between operations: 2.58 us -> 0.74 us
  local copies, waits for them, and re-layouts: 2.71 us -> 4.12 us
    ppermute x10 -> x6, waiting for transfers between devices: 30.7 us -> 10.2 us  [the longest x1 4.33 us: local(): from_north = lax.ppermute(southward, 'lat', shift_pairs('lat', -1, False))]
    ppermute x10 -> x6, starting transfers between devices: 19.9 us -> 12.8 us  [the longest x1 4.93 us: local(): lower = lax.ppermute(ocean_current, 'lat', shift_pairs('lat', 1, False))]
    pallas_call x0 -> x3, Pallas kernels: none -> 5.98 us  [the longest x1 3.88 us: local(): pl.pallas_call(dynamics_kernel, out_shape=(shape(velocity.shape), shape(s...]
    mul x20 -> x0, other arithmetic: 5.1 us -> none  [the longest x6 3.19 us: new_velocity(): (velocity_now[0] + time_step * (force_x + wind_now[0] + water_drag * curr...]
    unnamed x22, local copies, waits for them, and re-layouts: 0.34 us -> 4.12 us
    div x16 -> x0, other arithmetic: 3.48 us -> none  [the longest x8 1.74 us: velocity_from(): sigma_yy = (wide_stress[0] - wide_stress[1]) / 2.0]
    slice x4 -> x0, local copies, waits for them, and re-layouts: 2.2 us -> none  [the longest x1 1.28 us: local(): concentration[:, :, columns]]
    another operation x3 -> x0, other arithmetic: 1.72 us -> none  [the longest x2 0.92 us: new_velocity(): return jnp.stack([u, v])]
  transfers between devices with their start and end apart: 10 -> 6, of which waited for: 7 -> 5; matrix products, arithmetic and copies ran while one was open for 5% -> 0% of each run, Pallas kernels for 0% -> 5%
where the time goes in v1:
time: 34.2 us; the launch traced here: 33.8 us
  starting transfers between devices  12.8 us (37%)
  waiting for transfers between devices  10.2 us (30%)
  Pallas kernels  5.98 us (17%)
  local copies, waits for them, and re-layouts  4.12 us (12%)
  between operations  0.74 us (2%)
    ppermute x1, starting transfers between devices, local(): lower = lax.ppermute(ocean_current, 'lat', shift_pairs('lat', 1, False))  4.93 us
    ppermute x1, waiting for transfers between devices, local(): from_north = lax.ppermute(southward, 'lat', shift_pairs('lat', -1, False))  4.33 us
    ppermute x1, starting transfers between devices, local(): from_south = lax.ppermute(northward, 'lat', shift_pairs('lat', 1, False))  4.26 us
    unnamed x22, local copies, waits for them, and re-layouts  4.12 us
    pallas_call x1, Pallas kernels, local(): pl.pallas_call(dynamics_kernel, out_shape=(shape(velocity.shape), shape(s...  3.88 us
    ppermute x1, waiting for transfers between devices, local(): from_west = lax.ppermute(eastward, 'lon', shift_pairs('lon', 1, True))  2.48 us
    ppermute x1, waiting for transfers between devices, local(): from_east = lax.ppermute(westward, 'lon', shift_pairs('lon', -1, True))  1.75 us
    pallas_call x1, Pallas kernels, local(): pl.pallas_call(growth_kernel, out_shape=(shape(thickness.shape), shape((2...  1.59 us
  transfers between devices with their start and end apart: 6, of which 5 were waited for; matrix products, arithmetic and copies ran while one was open for 0% of the time, Pallas kernels for 5%

profile of v1, /device:TPU:0, one launch (start us, length us, event | category | flops | bytes accessed | tf_op | source)
XLA Modules:
  0.0 33.8 jit_solution(13742099076273788221)
XLA Ops:
  0.6 4.9 %collective-permute-start = (bf16[2,2,64,256]{3,2,1,0:T(8,128)(2,1)}, bf16[2,2,64,256]{3,2,1,0:T(8,128)(2,1)S(1)}, u32[]{:S(2)}, u32[]{:S(2)}) collective-permute-start(bf16[2,2,64,256]{3,2,1,0:T(8,128)(2,1)} %own_ref.1), channel_id=1, source_target_pairs={{0,1},{1,2},{2,3},{4,5},{5,6},{6,7},{8,9},{9,10},{10,11},{12,13},{... | collective-permute-start | bytes 393224 | tf_op jit(solution)/shard_map/ppermute | solution.py:347
  5.6 1.3 %collective-permute-start.1 = (bf16[2,2,64,256]{3,2,1,0:T(8,128)(2,1)}, bf16[2,2,64,256]{3,2,1,0:T(8,128)(2,1)S(1)}, u32[]{:S(2)}, u32[]{:S(2)}) collective-permute-start(bf16[2,2,64,256]{3,2,1,0:T(8,128)(2,1)} %own_ref.1), channel_id=1, source_target_pairs={{1,0},{2,1},{3,2},{5,4},{6,5},{7,6},{9,8},{10,9},{11,10},{13,12},{... | collective-permute-start | bytes 393224 | tf_op jit(solution)/shard_map/ppermute | solution.py:348
  6.9 0.0 copy-start
  6.9 1.0 %copy-done = f32[6,64,256]{2,1,0:T(8,128)S(1)} copy-done((f32[6,64,256]{2,1,0:T(8,128)S(1)}, f32[6,64,256]{2,1,0:T(8,128)}, u32[]{:S(2)}) %copy-start) | copy-done | bytes 393240
  7.9 1.0 %copy-done.1 = f32[6,64,256]{2,1,0:T(8,128)S(1)} copy-done((f32[6,64,256]{2,1,0:T(8,128)S(1)}, f32[6,64,256]{2,1,0:T(8,128)}, u32[]{:S(2)}) %copy-start.1) | copy-done | bytes 393240
  8.9 0.8 %copy-done.2 = s32[64,256]{1,0:T(8,128)S(1)} copy-done((s32[64,256]{1,0:T(8,128)S(1)}, s32[64,256]{1,0:T(8,128)}, u32[]{:S(2)}) %copy-start.2) | copy-done | bytes 65560
  9.7 0.7 %copy-done.9 = s32[1,16]{1,0:T(1,128)S(1)} copy-done((s32[1,16]{1,0:T(1,128)S(1)}, s32[1,16]{1,0:T(1,128)}, u32[]{:S(2)}) %copy-start.9) | copy-done | bytes 88
  10.4 0.0 copy-start.7
  10.4 0.0 copy-start.8
  10.4 1.6 %growth.1 = (f32[6,64,256]{2,1,0:T(8,128)}, f32[4,64,256]{2,1,0:T(8,128)S(1)}) custom-call(s32[1,16]{1,0:T(1,128)S(1)} %copy-done.9, f32[6,64,256]{2,1,0:T(8,128)S(1)} %copy-done, f32[6,64,256]{2,1,0:T(8,128)S(1)} %copy-done.1, s32[64,256]{1,0:T(8,128)S(1)} %copy-done.2), custom_call_target="tpu_custom_call" | custom-call | flops 9830400 | bytes 1179648 | tf_op jit(solution)/shard_map/growth/pallas_call | solution.py:351
  12.0 0.0 collective-permute-done.lower_ref
  12.0 0.7 %collective-permute-done.1.upper_ref = bf16[2,2,64,256]{3,2,1,0:T(8,128)(2,1)S(1)} collective-permute-done((bf16[2,2,64,256]{3,2,1,0:T(8,128)(2,1)}, bf16[2,2,64,256]{3,2,1,0:T(8,128)(2,1)S(1)}, u32[]{:S(2)}, u32[]{:S(2)}) %collective-permute-start.1) | collective-permute-done | bytes 131104 | tf_op jit(solution)/shard_map/ppermute | solution.py:348
  12.6 0.0 copy-done.3
  12.7 0.6 %copy-done.10 = s32[64]{0:T(128)S(1)} copy-done((s32[64]{0:T(128)S(1)}, s32[64]{0:T(128)}, u32[]{:S(2)}) %copy-start.10) | copy-done | bytes 280
  13.3 0.5 %pack.1 = (f32[13,64,256]{2,1,0:T(8,128)S(1)}, bf16[64,256]{1,0:T(8,128)(2,1)S(1)}, bf16[64,256]{1,0:T(8,128)(2,1)S(1)}, bf16[208,256]{1,0:T(8,128)(2,1)S(1)}, bf16[208,256]{1,0:T(8,128)(2,1)S(1)}) custom-call(s32[1,64]{1,0:T(1,128)S(1)} %bitcast.1, bf16[64,128]{1,0:T(8,128)(2,1)S(1)} %copy-done.8, bf16[2,2,64,256]{3,2,1,0:T(8,128)(2,1)S(1)} %copy-done.5, ...), custom_call_target="tpu_custom_call" | custom-call | tf_op jit(solution)/shard_map/pack/pallas_call | solution.py:367
  13.8 1.0 %collective-permute-start.2 = (bf16[64,256]{1,0:T(8,128)(2,1)S(1)}, bf16[64,256]{1,0:T(8,128)(2,1)S(1)}, u32[]{:S(2)}, u32[]{:S(2)}) collective-permute-start(bf16[64,256]{1,0:T(8,128)(2,1)S(1)} %get-tuple-element.62), channel_id=1, source_target_pairs={{0,28},{4,0},{8,4},{12,8},{16,12},{20,16},{24,20},{28,24},{1,29},{... | collective-permute-start | bytes 98312 | tf_op jit(solution)/shard_map/ppermute | solution.py:394
  14.8 0.0 collective-permute-start.3
  14.8 1.8 %collective-permute-done.2.east_ref = bf16[64,256]{1,0:T(8,128)(2,1)S(1)} collective-permute-done((bf16[64,256]{1,0:T(8,128)(2,1)S(1)}, bf16[64,256]{1,0:T(8,128)(2,1)S(1)}, u32[]{:S(2)}, u32[]{:S(2)}) %collective-permute-start.2) | collective-permute-done | bytes 32800 | tf_op jit(solution)/shard_map/ppermute | solution.py:394
  16.6 2.5 %collective-permute-done.3.west_ref = bf16[64,256]{1,0:T(8,128)(2,1)S(1)} collective-permute-done((bf16[64,256]{1,0:T(8,128)(2,1)S(1)}, bf16[64,256]{1,0:T(8,128)(2,1)S(1)}, u32[]{:S(2)}, u32[]{:S(2)}) %collective-permute-start.3) | collective-permute-done | bytes 32800 | tf_op jit(solution)/shard_map/ppermute | solution.py:393
  19.1 4.3 %collective-permute-start.5 = (bf16[208,256]{1,0:T(8,128)(2,1)S(1)}, bf16[208,256]{1,0:T(8,128)(2,1)S(1)}, u32[]{:S(2)}, u32[]{:S(2)}) collective-permute-start(bf16[208,256]{1,0:T(8,128)(2,1)S(1)} %get-tuple-element.69), channel_id=1, source_target_pairs={{0,1},{1,2},{2,3},{4,5},{5,6},{6,7},{8,9},{9,10},{10,11},{12,13},{... | collective-permute-start | bytes 319496 | tf_op jit(solution)/shard_map/ppermute | solution.py:399
  23.3 1.3 %collective-permute-start.4 = (bf16[208,256]{1,0:T(8,128)(2,1)S(1)}, bf16[208,256]{1,0:T(8,128)(2,1)S(1)}, u32[]{:S(2)}, u32[]{:S(2)}) collective-permute-start(bf16[208,256]{1,0:T(8,128)(2,1)S(1)} %get-tuple-element.70), channel_id=1, source_target_pairs={{1,0},{2,1},{3,2},{5,4},{6,5},{7,6},{9,8},{10,9},{11,10},{13,12},{... | collective-permute-start | bytes 319496 | tf_op jit(solution)/shard_map/ppermute | solution.py:400
  24.6 1.0 %collective-permute-done.5.south_ref = bf16[208,256]{1,0:T(8,128)(2,1)S(1)} collective-permute-done((bf16[208,256]{1,0:T(8,128)(2,1)S(1)}, bf16[208,256]{1,0:T(8,128)(2,1)S(1)}, u32[]{:S(2)}, u32[]{:S(2)}) %collective-permute-start.5) | collective-permute-done | bytes 106528 | tf_op jit(solution)/shard_map/ppermute | solution.py:399
  25.6 4.3 %collective-permute-done.4.north_ref = bf16[208,256]{1,0:T(8,128)(2,1)S(1)} collective-permute-done((bf16[208,256]{1,0:T(8,128)(2,1)S(1)}, bf16[208,256]{1,0:T(8,128)(2,1)S(1)}, u32[]{:S(2)}, u32[]{:S(2)}) %collective-permute-start.4) | collective-permute-done | bytes 106528 | tf_op jit(solution)/shard_map/ppermute | solution.py:400
  29.9 3.9 %dynamics.1 = (f32[2,64,256]{2,1,0:T(8,128)}, f32[3,64,256]{2,1,0:T(8,128)}) custom-call(f32[13,64,256]{2,1,0:T(8,128)S(1)} %get-tuple-element.61.fields_ref, bf16[64,256]{1,0:T(8,128)(2,1)S(1)} %collective-permute-done.2.east_ref, bf16[64,256]{1,0:T(8,128)(2,1)S(1)} %collective-permute-done.3.west_ref, ...), custom_call_target="tpu_custom_call" | custom-call | tf_op jit(solution)/shard_map/dynamics/pallas_call | solution.py:407
  (15 shorter events, 0.0 us)
Async XLA Ops:
  0.6 11.4 %collective-permute-start = (bf16[2,2,64,256]{3,2,1,0:T(8,128)(2,1)}, bf16[2,2,64,256]{3,2,1,0:T(8,128)(2,1)S(1)}, u32[]{:S(2)}, u32[]{:S(2)}) collective-permute-start(bf16[2,2,64,256]{3,2,1,0:T(8,128)(2,1)} %own_ref.1), channel_id=1, source_target_pairs={{0,1},{1,2},{2,3},{4,5},{5,6},{6,7},{8,9},{9,10},{10,11},{12,13},{... | collective-permute-start | bytes 393224 | tf_op jit(solution)/shard_map/ppermute | solution.py:347
  5.6 7.1 %collective-permute-start.1 = (bf16[2,2,64,256]{3,2,1,0:T(8,128)(2,1)}, bf16[2,2,64,256]{3,2,1,0:T(8,128)(2,1)S(1)}, u32[]{:S(2)}, u32[]{:S(2)}) collective-permute-start(bf16[2,2,64,256]{3,2,1,0:T(8,128)(2,1)} %own_ref.1), channel_id=1, source_target_pairs={{1,0},{2,1},{3,2},{5,4},{6,5},{7,6},{9,8},{10,9},{11,10},{13,12},{... | collective-permute-start | bytes 393224 | tf_op jit(solution)/shard_map/ppermute | solution.py:348
  6.9 1.0 %copy-start = (f32[6,64,256]{2,1,0:T(8,128)S(1)}, f32[6,64,256]{2,1,0:T(8,128)}, u32[]{:S(2)}) copy-start(f32[6,64,256]{2,1,0:T(8,128)} %thick_ref.1) | copy-start | bytes 1179652
  7.9 1.0 %copy-start.1 = (f32[6,64,256]{2,1,0:T(8,128)S(1)}, f32[6,64,256]{2,1,0:T(8,128)}, u32[]{:S(2)}) copy-start(f32[6,64,256]{2,1,0:T(8,128)} %conc_ref.1) | copy-start | bytes 1179652
  8.9 0.8 %copy-start.2 = (s32[64,256]{1,0:T(8,128)S(1)}, s32[64,256]{1,0:T(8,128)}, u32[]{:S(2)}) copy-start(s32[64,256]{1,0:T(8,128)} %mask_ref.3) | copy-start | bytes 196612
  9.7 0.7 %copy-start.9 = (s32[1,16]{1,0:T(1,128)S(1)}, s32[1,16]{1,0:T(1,128)}, u32[]{:S(2)}) copy-start(s32[1,16]{1,0:T(1,128)} %covered_ref.1) | copy-start | bytes 196
  10.4 2.3 %copy-start.3 = (s32[64,256]{1,0:T(8,128)S(1)}, s32[64,256]{1,0:T(8,128)}, u32[]{:S(2)}) copy-start(s32[64,256]{1,0:T(8,128)} %mask_ref.3) | copy-start | bytes 196612
  10.4 2.3 %copy-start.4 = (f32[3,64,256]{2,1,0:T(8,128)S(1)}, f32[3,64,256]{2,1,0:T(8,128)}, u32[]{:S(2)}) copy-start(f32[3,64,256]{2,1,0:T(8,128)} %stress_ref.1) | copy-start | bytes 589828
  10.4 2.3 %copy-start.5 = (bf16[2,2,64,256]{3,2,1,0:T(8,128)(2,1)S(1)}, bf16[2,2,64,256]{3,2,1,0:T(8,128)(2,1)}, u32[]{:S(2)}) copy-start(bf16[2,2,64,256]{3,2,1,0:T(8,128)(2,1)} %own_ref.1) | copy-start | bytes 393220
  10.4 2.3 %copy-start.6 = (bf16[2,2,64,256]{3,2,1,0:T(8,128)(2,1)S(1)}, bf16[2,2,64,256]{3,2,1,0:T(8,128)(2,1)}, u32[]{:S(2)}) copy-start(bf16[2,2,64,256]{3,2,1,0:T(8,128)(2,1)} %wind_ref.1) | copy-start | bytes 393220
  10.4 2.3 %copy-start.7 = (f32[2,64,256]{2,1,0:T(8,128)S(1)}, f32[2,64,256]{2,1,0:T(8,128)}, u32[]{:S(2)}) copy-start(f32[2,64,256]{2,1,0:T(8,128)} %velocity_ref.1) | copy-start | bytes 393220
  10.4 2.3 %copy-start.8 = (bf16[64,128]{1,0:T(8,128)(2,1)S(1)}, bf16[64,128]{1,0:T(8,128)(2,1)}, u32[]{:S(2)}) copy-start(bf16[64,128]{1,0:T(8,128)(2,1)} %weights_ref.1) | copy-start | bytes 49156
  12.6 0.7 %copy-start.10 = (s32[64]{0:T(128)S(1)}, s32[64]{0:T(128)}, u32[]{:S(2)}) copy-start(s32[64]{0:T(128)} %param.27) | copy-start | bytes 772
  13.8 2.8 %collective-permute-start.2 = (bf16[64,256]{1,0:T(8,128)(2,1)S(1)}, bf16[64,256]{1,0:T(8,128)(2,1)S(1)}, u32[]{:S(2)}, u32[]{:S(2)}) collective-permute-start(bf16[64,256]{1,0:T(8,128)(2,1)S(1)} %get-tuple-element.62), channel_id=1, source_target_pairs={{0,28},{4,0},{8,4},{12,8},{16,12},{20,16},{24,20},{28,24},{1,29},{... | collective-permute-start | bytes 98312 | tf_op jit(solution)/shard_map/ppermute | solution.py:394
  14.8 4.2 %collective-permute-start.3 = (bf16[64,256]{1,0:T(8,128)(2,1)S(1)}, bf16[64,256]{1,0:T(8,128)(2,1)S(1)}, u32[]{:S(2)}, u32[]{:S(2)}) collective-permute-start(bf16[64,256]{1,0:T(8,128)(2,1)S(1)} %get-tuple-element.63), channel_id=1, source_target_pairs={{0,4},{4,8},{8,12},{12,16},{16,20},{20,24},{24,28},{28,0},{1,5},{5... | collective-permute-start | bytes 98312 | tf_op jit(solution)/shard_map/ppermute | solution.py:393
  19.1 6.5 %collective-permute-start.5 = (bf16[208,256]{1,0:T(8,128)(2,1)S(1)}, bf16[208,256]{1,0:T(8,128)(2,1)S(1)}, u32[]{:S(2)}, u32[]{:S(2)}) collective-permute-start(bf16[208,256]{1,0:T(8,128)(2,1)S(1)} %get-tuple-element.69), channel_id=1, source_target_pairs={{0,1},{1,2},{2,3},{4,5},{5,6},{6,7},{8,9},{9,10},{10,11},{12,13},{... | collective-permute-start | bytes 319496 | tf_op jit(solution)/shard_map/ppermute | solution.py:399
  23.3 6.6 %collective-permute-start.4 = (bf16[208,256]{1,0:T(8,128)(2,1)S(1)}, bf16[208,256]{1,0:T(8,128)(2,1)S(1)}, u32[]{:S(2)}, u32[]{:S(2)}) collective-permute-start(bf16[208,256]{1,0:T(8,128)(2,1)S(1)} %get-tuple-element.70), channel_id=1, source_target_pairs={{1,0},{2,1},{3,2},{5,4},{6,5},{7,6},{9,8},{10,9},{11,10},{13,12},{... | collective-permute-start | bytes 319496 | tf_op jit(solution)/shard_map/ppermute | solution.py:400

commit v2 on v1

v2 whole, which is shorter than its diff:
```python
import functools

import jax
import jax.numpy as jnp
from jax import lax
from jax.experimental import pallas as pl
from jax.experimental.pallas import tpu as pltpu
from jax.sharding import PartitionSpec as P

BLK = 128
SUB = 4
LANES = 128
GROUP = 16
PAD = 8
STATE = 5
VMEM_LIMIT = 16 * 1024 * 1024

growth_rate = 0.3
mixing_rate = 0.3


def total(terms):
    result = terms[0]
    for term in terms[1:]:
        result = result + term
    return result


def field_depths(margin, windows):
    depths = [margin] * STATE
    for copies in (2, 2):
        for window in range(windows):
            depths += [margin - 2 * SUB * window] * copies
    return depths


def message_groups(fields, depths):
    groups, held = [], []
    for field in fields:
        held.append(field)
        if sum(depths[f] for f in held) % GROUP == 0:
            groups.append(held)
            held = []
    return groups + ([held] if held else [])


def even(axis):
    return lax.axis_index(axis) % 2 == 0


def pack_rows(message_ref, row, groups, depths, value_of, northward, rows):
    for group in groups:
        parts = []
        for field in group:
            start = jnp.where(northward, rows - depths[field], 0)
            parts.append(value_of(field, pl.ds(pl.multiple_of(start, 8), depths[field])))
        value = parts[0] if len(parts) == 1 else jnp.concatenate(parts, axis=0)
        message_ref[row : row + value.shape[0]] = value.astype(jnp.bfloat16)
        row += value.shape[0]
    return row


def local_kernel(
    margin,
    covered_hbm,
    offset_hbm,
    weights_hbm,
    thick_hbm,
    conc_hbm,
    mask_hbm,
    velocity_hbm,
    stress_hbm,
    ocean_hbm,
    wind_hbm,
    thick_out_hbm,
    fields_ref,
    current_ref,
    side_ref,
    lon_x_ref,
    lon_y_ref,
    lat_x_ref,
    lat_y_ref,
    covered,
    offset,
    weights,
    thick,
    conc,
    mask_in,
    velocity,
    stress,
    ocean,
    wind,
    in_sems,
    thick_sems,
    conc_sems,
    out_sems,
):
    cats, rows, cols = thick.shape
    windows = wind.shape[0]
    step = GROUP
    chunks = rows // step

    def rows_of(chunk):
        return pl.ds(chunk * step, step)

    small = [
        pltpu.make_async_copy(source, target, in_sems.at[i])
        for i, (source, target) in enumerate(
            (
                (covered_hbm, covered),
                (mask_hbm, mask_in),
                (velocity_hbm, velocity),
                (stress_hbm, stress),
                (ocean_hbm, ocean),
                (wind_hbm, wind),
                (weights_hbm, weights),
                (offset_hbm, offset),
            )
        )
    ]
    pairs = [
        [
            pltpu.make_async_copy(hbm.at[:, rows_of(c)], vmem.at[:, rows_of(c)], sems.at[c])
            for hbm, vmem, sems in ((thick_hbm, thick, thick_sems), (conc_hbm, conc, conc_sems))
        ]
        for c in range(chunks)
    ]
    writes = [
        pltpu.make_async_copy(thick.at[:, rows_of(c)], thick_out_hbm.at[:, rows_of(c)], out_sems.at[c])
        for c in range(chunks)
    ]
    for copy in small[:2] + [copy for pair in pairs for copy in pair] + small[2:]:
        copy.start()

    blocks = cols // BLK
    first = lax.axis_index("lon") * blocks
    small[0].wait()
    live = [covered[0, first + block] > 0 for block in range(blocks)]
    small[1].wait()
    for c in range(chunks):
        at = slice(c * step, (c + 1) * step)
        for copy in pairs[c]:
            copy.wait()
        for block in range(blocks):
            lanes = slice(block * BLK, (block + 1) * BLK)
            part = [conc[k, at, lanes] for k in range(cats)]
            height = [thick[k, at, lanes] for k in range(cats)]
            mask = mask_in[at, lanes].astype(jnp.float32)
            area = total(part)
            inverse = 1.0 / area
            factor = jnp.exp(-2.0 * (1.0 - area)) * (mask * (1.0 / 3.0))
            half = 0.5 * mask
            volume = total([a * h for a, h in zip(part, height)])
            for window in range(windows):
                mean = volume * inverse
                grown = [h + growth_rate / (0.5 + h) + mixing_rate * (mean - h) for h in height]
                height = [jnp.where(live[block], g, h) for g, h in zip(grown, height)]
                volume = total([a * h for a, h in zip(part, height)])
                fields_ref[STATE + 2 * window, at, lanes] = volume * factor
                fields_ref[STATE + 2 * window + 1, at, lanes] = half / (volume + 1.0)
            for k in range(cats):
                thick[k, at, lanes] = height[k]
        writes[c].start()

    small[2].wait()
    small[3].wait()
    for row in range(0, rows, step):
        at = slice(row, row + step)
        mask = mask_in[at].astype(jnp.float32)
        fields_ref[0, at] = velocity[0, at]
        fields_ref[1, at] = velocity[1, at]
        fields_ref[2, at] = (stress[0, at] + stress[1, at]) * mask
        fields_ref[3, at] = (stress[0, at] - stress[1, at]) * mask
        fields_ref[4, at] = (stress[2, at] + stress[2, at]) * mask

    count = fields_ref.shape[0]
    per = LANES // margin
    slot_of_lane = lax.broadcasted_iota(jnp.int32, (rows, LANES), 1) // margin
    eastward = even("lon")
    for group in range(lon_x_ref.shape[1] // LANES):
        east = jnp.zeros((rows, LANES), jnp.float32)
        west = jnp.zeros((rows, LANES), jnp.float32)
        for slot in range(min(per, count - group * per)):
            field = group * per + slot
            east, west = add_slot(
                east, west, fields_ref.at[field], slot_of_lane == slot, slot * margin, margin
            )
        store_sides(lon_x_ref, lon_y_ref, group, east, west, eastward)
    depths = field_depths(margin, windows)
    groups = message_groups(range(count), depths)
    northward = even("lat")

    def value_of(field, at):
        return fields_ref[field, at, :]

    pack_rows(lat_x_ref, 0, groups, depths, value_of, northward, rows)
    pack_rows(lat_y_ref, 0, groups, depths, value_of, jnp.logical_not(northward), rows)

    for copy in small[4:]:
        copy.wait()
    own_weights = weights[:, :rows]
    for w in range(windows):
        for k in range(2):
            current_ref[w, k] = wind[w, k].astype(jnp.float32) + jnp.dot(
                own_weights, ocean[w, k], preferred_element_type=jnp.float32
            )
    square = (rows, rows)
    diagonal = lax.broadcasted_iota(jnp.int32, square, 0) == lax.broadcasted_iota(
        jnp.int32, square, 1
    )
    up = offset[...] > 0
    for number, north in enumerate((northward, jnp.logical_not(northward))):
        wanted = jnp.where(north, up.astype(jnp.int32), 1 - up.astype(jnp.int32)) > 0
        pick = jnp.where(diagonal & wanted, 1.0, 0.0).astype(jnp.bfloat16)
        side_ref[:, number * rows : (number + 1) * rows] = jnp.dot(
            pick, weights[:, rows:], preferred_element_type=jnp.float32
        ).astype(jnp.bfloat16)

    for copy in writes:
        copy.wait()


def add_slot(east, west, field_ref, here, shift, margin):
    cols = field_ref.shape[1]
    last = pltpu.roll(field_ref[:, cols - LANES :], (shift + margin) % LANES, 1)
    leading = field_ref[:, :LANES]
    if shift:
        leading = pltpu.roll(leading, shift, 1)
    return jnp.where(here, last, east), jnp.where(here, leading, west)


def store_sides(x_ref, y_ref, group, east, west, eastward):
    lanes = slice(group * LANES, (group + 1) * LANES)
    x_ref[:, lanes] = jnp.where(eastward, east, west).astype(jnp.bfloat16)
    y_ref[:, lanes] = jnp.where(eastward, west, east).astype(jnp.bfloat16)


def force_kernel(
    margin,
    early,
    side_ref,
    tile_x_ref,
    tile_y_ref,
    current_ref,
    fields_ref,
    lon_x_in,
    lon_y_in,
    lat_x_in,
    lat_y_in,
    force_ref,
    lon_x_ref,
    lon_y_ref,
    lat_x_ref,
    lat_y_ref,
):
    windows, _, rows, cols = current_ref.shape
    side_x = side_ref[:, :rows]
    side_y = side_ref[:, rows:]

    def dot(a, b):
        return jnp.dot(a, b, preferred_element_type=jnp.float32)

    for w in range(windows):
        b = fields_ref[STATE + 2 * w + 1]
        for k in range(2):
            current = dot(side_x, tile_x_ref[w, k]) + dot(side_y, tile_y_ref[w, k])
            force_ref[2 * w + k] = b * (current_ref[w, k] + current)

    per = LANES // margin
    count = early + force_ref.shape[0]
    slot_of_lane = lax.broadcasted_iota(jnp.int32, (rows, LANES), 1) // margin
    eastward = even("lon")
    for group in range(lon_x_ref.shape[1] // LANES):
        lanes = slice(group * LANES, (group + 1) * LANES)
        x = lon_x_in[:, lanes].astype(jnp.float32)
        y = lon_y_in[:, lanes].astype(jnp.float32)
        east, west = jnp.where(eastward, x, y), jnp.where(eastward, y, x)
        for field in range(max(early, group * per), min(count, (group + 1) * per)):
            slot = field - group * per
            east, west = add_slot(
                east, west, force_ref.at[field - early], slot_of_lane == slot, slot * margin, margin
            )
        store_sides(lon_x_ref, lon_y_ref, group, east, west, eastward)

    depths = field_depths(margin, windows)
    groups = message_groups(range(early, count), depths)
    northward = even("lat")

    def value_of(field, at):
        return force_ref[field - early, at, :]

    for old_ref, ref, north in (
        (lat_x_in, lat_x_ref, northward),
        (lat_y_in, lat_y_ref, jnp.logical_not(northward)),
    ):
        row = old_ref.shape[0]
        ref[:row] = old_ref[...]
        row = pack_rows(ref, row, groups, depths, value_of, north, rows)
        ref[row:] = jnp.zeros((ref.shape[0] - row, cols), jnp.bfloat16)


def dynamics_kernel(
    margin,
    lat_count,
    fields_ref,
    force_ref,
    lon_x_ref,
    lon_y_ref,
    lat_x_ref,
    lat_y_ref,
    velocity_ref,
    stress_ref,
    state,
    strength,
    keep,
    push,
    force,
):
    early, rows, cols = fields_ref.shape
    windows = strength.shape[0]
    count = early + force_ref.shape[0]
    own_tiles = cols // LANES
    tiles = own_tiles + 1
    per = LANES // margin
    top = PAD + margin
    bottom = top + rows
    lane = lax.broadcasted_iota(jnp.int32, (8, LANES), 1)

    def place(field, tile, row, value):
        at = pl.ds(row, value.shape[0])
        if field < STATE:
            state[field, tile, at, :] = value
        elif field >= early:
            window, kind = divmod(field - early, 2)
            force[window, kind, tile, at, :] = value
        else:
            window, kind = divmod(field - STATE, 2)
            if kind == 0:
                strength[window, tile, at, :] = value
            else:
                push[window, tile, at, :] = value
                keep[window, tile, at, :] = jnp.where(value > 0.0, 1.0 - value, 0.0)

    zero = jnp.zeros((PAD, LANES), jnp.float32)
    for tile in range(tiles):
        for field in range(STATE):
            state[field, tile, 0:PAD, :] = zero
            state[field, tile, bottom + margin : bottom + margin + PAD, :] = zero

    def side_tiles(x, y, row):
        wide = lax.broadcasted_iota(jnp.int32, (x.shape[0], LANES), 1)
        from_x_is_east = even("lon")
        for group in range(x.shape[1] // LANES):
            lanes = slice(group * LANES, (group + 1) * LANES)
            x_now, y_now = x[:, lanes], y[:, lanes]
            east = jnp.where(from_x_is_east, x_now, y_now)
            west = jnp.where(from_x_is_east, y_now, x_now)
            for slot in range(min(per, count - group * per)):
                shift = slot * margin
                back = (LANES - margin - shift) % LANES
                e = pltpu.roll(east, LANES - shift, 1) if shift else east
                w = pltpu.roll(west, back, 1) if back else west
                value = jnp.where(wide < margin, e, jnp.where(wide >= LANES - margin, w, 0.0))
                place(group * per + slot, own_tiles, row, value)

    for field in range(count):
        for tile in range(own_tiles):
            lanes = slice(tile * LANES, (tile + 1) * LANES)
            own = fields_ref[field, :, lanes] if field < early else force_ref[field - early, :, lanes]
            place(field, tile, top, own)
    side_tiles(lon_x_ref[...].astype(jnp.float32), lon_y_ref[...].astype(jnp.float32), top)

    depths = field_depths(margin, windows)
    groups = message_groups(range(early), depths) + message_groups(range(early, count), depths)
    me = lax.axis_index("lat")
    for ref, north in ((lat_x_ref, even("lat")), (lat_y_ref, jnp.logical_not(even("lat")))):
        exists = jnp.where(north, me < lat_count - 1, me > 0)

        def read(at):
            return jnp.where(exists, ref[at].astype(jnp.float32), 0.0)

        row = 0
        for group in groups:
            height = sum(depths[f] for f in group)
            value = read(slice(row, row + height))
            begin = 0
            for field in group:
                depth = depths[field]
                to = pl.multiple_of(jnp.where(north, bottom, top - depth), 8)
                for tile in range(own_tiles):
                    lanes = slice(tile * LANES, (tile + 1) * LANES)
                    place(field, tile, to, value[begin : begin + depth, lanes])
                begin += depth
            row += height
        to = pl.multiple_of(jnp.where(north, bottom, top - margin), 8)
        packed = lon_x_ref.shape[1]
        side_tiles(
            read(slice(row, row + margin))[:, :packed],
            read(slice(row + margin, row + 2 * margin))[:, :packed],
            to,
        )

    first_lane = lane == 0
    last_lane = lane == LANES - 1

    def across(values):
        ahead = [pltpu.roll(x, LANES - 1, 1) for x in values]
        behind = [pltpu.roll(x, 1, 1) for x in values]
        return [
            jnp.where(last_lane, ahead[(j + 1) % tiles], ahead[j])
            - jnp.where(first_lane, behind[j - 1], behind[j])
            for j in range(tiles)
        ]

    def along(field, tile, row):
        return state[field, tile, row + 1 : row + 9, :] - state[field, tile, row - 1 : row + 7, :]

    every = range(tiles)
    for window in range(windows):
        spare = 2 * SUB * window
        row_list = range(top - margin + spare, bottom + margin - spare, 8)

        def subcycle(_, carry):
            for row in row_list:
                at = slice(row, row + 8)
                u_x = across([state[0, j, at, :] for j in every])
                v_x = across([state[1, j, at, :] for j in every])
                for j in every:
                    u_y = along(0, j, row)
                    v_y = along(1, j, row)
                    shear = u_y + v_x[j]
                    spread = u_x[j] + v_y
                    tension = u_x[j] - v_y
                    tension4 = tension * 0.25
                    shear4 = shear * 0.25
                    squares = spread * spread + tension * tension4 + (shear * shear4 + 1.0)
                    k = strength[window, j, at, :]
                    kr = k * lax.rsqrt(squares)
                    state[2, j, at, :] = state[2, j, at, :] * (2.0 / 3.0) + (
                        kr * (spread + tension4) - k
                    )
                    state[3, j, at, :] = state[3, j, at, :] * (2.0 / 3.0) + (
                        kr * (spread - tension4) - k
                    )
                    state[4, j, at, :] = state[4, j, at, :] * (2.0 / 3.0) + kr * shear4
            for row in row_list:
                at = slice(row, row + 8)
                p_x = across([state[2, j, at, :] for j in every])
                t_x = across([state[4, j, at, :] for j in every])
                for j in every:
                    b = push[window, j, at, :] * 0.25
                    a = keep[window, j, at, :]
                    state[0, j, at, :] = (
                        a * state[0, j, at, :]
                        + b * (p_x[j] + along(4, j, row))
                        + force[window, 0, j, at, :]
                    )
                    state[1, j, at, :] = (
                        a * state[1, j, at, :]
                        + b * (t_x[j] + along(3, j, row))
                        + force[window, 1, j, at, :]
                    )
            return carry

        lax.fori_loop(0, SUB, subcycle, 0)

    for tile in range(own_tiles):
        lanes = slice(tile * LANES, (tile + 1) * LANES)
        for row in range(0, rows, 8):
            at = slice(row, row + 8)
            to = slice(top + row, top + row + 8)
            velocity_ref[0, at, lanes] = state[0, tile, to, :]
            velocity_ref[1, at, lanes] = state[1, tile, to, :]
            p = state[2, tile, to, :]
            q = state[3, tile, to, :]
            stress_ref[0, at, lanes] = (p + q) * 0.5
            stress_ref[1, at, lanes] = (p - q) * 0.5
            stress_ref[2, at, lanes] = state[4, tile, to, :] * 0.5


def params():
    return pltpu.CompilerParams(vmem_limit_bytes=VMEM_LIMIT)


def swaps(axis, first, ring):
    n = lax.axis_size(axis)
    if ring and n % 2:
        raise ValueError("odd ring")
    partner = list(range(n))
    for i in range(first, n if ring else n - 1, 2):
        j = (i + 1) % n
        partner[i], partner[j] = j, i
    return list(enumerate(partner))


def exchange(x, y, axis, ring):
    return (
        lax.ppermute(x, axis, swaps(axis, 0, ring)),
        lax.ppermute(y, axis, swaps(axis, 1, ring)),
    )


def shape(dims, dtype=jnp.float32):
    return jax.ShapeDtypeStruct(dims, dtype)


def local(
    velocity,
    stress,
    thickness,
    concentration,
    land_mask,
    covered,
    ocean_current,
    wind_stress,
    regrid_weights,
    tile_offset,
):
    _, rows, cols = velocity.shape
    windows = wind_stress.shape[0]
    margin = 2 * SUB * windows
    early = STATE + 2 * windows
    count = early + 2 * windows
    tiles = cols // LANES + 1
    packed = -(-count // (LANES // margin)) * LANES
    depths = field_depths(margin, windows)
    early_rows = sum(depths[:early])
    message_rows = sum(depths)
    bf16 = jnp.bfloat16

    tile_x, tile_y = exchange(ocean_current, ocean_current, "lat", False)

    whole = pl.BlockSpec(memory_space=pltpu.VMEM)
    anywhere = pl.BlockSpec(memory_space=pl.ANY)
    chunks = rows // GROUP
    thick_out, fields, current, side, lon_x, lon_y, lat_x, lat_y = pl.pallas_call(
        functools.partial(local_kernel, margin),
        out_shape=(
            shape(thickness.shape),
            shape((early, rows, cols)),
            shape(wind_stress.shape),
            shape((rows, 2 * rows), bf16),
            shape((rows, packed), bf16),
            shape((rows, packed), bf16),
            shape((early_rows, cols), bf16),
            shape((early_rows, cols), bf16),
        ),
        in_specs=[anywhere] * 10,
        out_specs=(anywhere,) + (whole,) * 7,
        scratch_shapes=[
            pltpu.SMEM(covered.shape, jnp.int32),
            pltpu.VMEM((1, rows), jnp.int32),
            pltpu.VMEM(regrid_weights.shape, bf16),
            pltpu.VMEM(thickness.shape, jnp.float32),
            pltpu.VMEM(thickness.shape, jnp.float32),
            pltpu.VMEM(land_mask.shape, jnp.int32),
            pltpu.VMEM(velocity.shape, jnp.float32),
            pltpu.VMEM(stress.shape, jnp.float32),
            pltpu.VMEM(ocean_current.shape, bf16),
            pltpu.VMEM(wind_stress.shape, bf16),
            pltpu.SemaphoreType.DMA((8,)),
            pltpu.SemaphoreType.DMA((chunks,)),
            pltpu.SemaphoreType.DMA((chunks,)),
            pltpu.SemaphoreType.DMA((chunks,)),
        ],
        compiler_params=params(),
        cost_estimate=pl.CostEstimate(
            flops=100 * thickness.size, bytes_accessed=12 * thickness.size, transcendentals=0
        ),
        name="local",
    )(
        covered,
        tile_offset.reshape(1, rows),
        regrid_weights,
        thickness,
        concentration,
        land_mask,
        velocity,
        stress,
        ocean_current,
        wind_stress,
    )

    force, lon_x, lon_y, lat_x, lat_y = pl.pallas_call(
        functools.partial(force_kernel, margin, early),
        out_shape=(
            shape((2 * windows, rows, cols)),
            shape((rows, packed), bf16),
            shape((rows, packed), bf16),
            shape((message_rows + 2 * margin, cols), bf16),
            shape((message_rows + 2 * margin, cols), bf16),
        ),
        in_specs=[whole] * 9,
        out_specs=(whole,) * 5,
        compiler_params=params(),
        name="force",
    )(side, tile_x, tile_y, current, fields, lon_x, lon_y, lat_x, lat_y)

    lon_x, lon_y = exchange(lon_x, lon_y, "lon", True)
    north_end = rows - margin
    start_x = jnp.where(even("lat"), north_end, 0)
    for number, part in enumerate((lon_x, lon_y)):
        at = message_rows + number * margin
        corner_x = lax.dynamic_slice_in_dim(part, start_x, margin, 0)
        corner_y = lax.dynamic_slice_in_dim(part, north_end - start_x, margin, 0)
        lat_x = lat_x.at[at : at + margin, :packed].set(corner_x)
        lat_y = lat_y.at[at : at + margin, :packed].set(corner_y)
    lat_x, lat_y = exchange(lat_x, lat_y, "lat", False)

    height = rows + 2 * margin + 2 * PAD

    def scratch(*lead):
        return pltpu.VMEM((*lead, tiles, height, LANES), jnp.float32)

    velocity_out, stress_out = pl.pallas_call(
        functools.partial(dynamics_kernel, margin, lax.axis_size("lat")),
        out_shape=(shape(velocity.shape), shape(stress.shape)),
        in_specs=[whole] * 6,
        out_specs=(whole, whole),
        scratch_shapes=[
            scratch(STATE),
            scratch(windows),
            scratch(windows),
            scratch(windows),
            scratch(windows, 2),
        ],
        compiler_params=params(),
        name="dynamics",
    )(fields, force, lon_x, lon_y, lat_x, lat_y)
    return (velocity_out, stress_out, thick_out)


def solution(mesh):
    return jax.shard_map(
        local,
        mesh=mesh,
        in_specs=(
            P(None, "lat", "lon"),
            P(None, "lat", "lon"),
            P(None, "lat", "lon"),
            P(None, "lat", "lon"),
            P("lat", "lon"),
            P("lat", None),
            P(None, None, "lat", "lon"),
            P(None, None, "lat", "lon"),
            P("lat", None),
            P("lat"),
        ),
        out_specs=(P(None, "lat", "lon"), P(None, "lat", "lon"), P(None, "lat", "lon")),
        check_vma=False,
    )
```

time: 34.2 us -> 31.1 us (0.909)
  the two profiles are of different devices: /device:TPU:0 before, /device:TPU:11 now
where the time goes in v2:
time: 31.1 us; the launch traced here: 30.7 us
  starting transfers between devices  8.96 us (29%)
  waiting for transfers between devices  7.4 us (24%)
  local copies, waits for them, and re-layouts  7.19 us (23%)
  Pallas kernels  6.43 us (21%)
  between operations  0.73 us (2%)
    ppermute x3, starting transfers between devices, exchange(): lax.ppermute(y, axis, swaps(axis, 1, ring))  7.42 us
    unnamed x20, local copies, waits for them, and re-layouts  7.19 us
    ppermute x3, waiting for transfers between devices, exchange(): lax.ppermute(y, axis, swaps(axis, 1, ring))  4.67 us
    pallas_call x1, Pallas kernels, local(): pl.pallas_call(functools.partial(dynamics_kernel, margin, lax.axis_size('...  3.88 us
    ppermute x3, waiting for transfers between devices, exchange(): lax.ppermute(x, axis, swaps(axis, 0, ring))  2.73 us
    pallas_call x1, Pallas kernels, local(): pl.pallas_call(functools.partial(local_kernel, margin), out_shape=(shape(...  2.21 us
    ppermute x3, starting transfers between devices, exchange(): lax.ppermute(x, axis, swaps(axis, 0, ring))  1.55 us
  transfers between devices with their start and end apart: 6, of which 3 were waited for; matrix products, arithmetic and copies ran while one was open for 0% of the time, Pallas kernels for 7%

profile of v2, /device:TPU:11, one launch (start us, length us, event | category | flops | bytes accessed | tf_op | source)
XLA Modules:
  0.0 30.7 jit_solution(7435242975374691626)
XLA Ops:
  0.6 0.0 copy-start.8
  0.7 0.2 collective-permute-start
  0.9 4.3 %collective-permute-start.1 = (bf16[2,2,64,256]{3,2,1,0:T(8,128)(2,1)}, bf16[2,2,64,256]{3,2,1,0:T(8,128)(2,1)S(1)}, u32[]{:S(2)}, u32[]{:S(2)}) collective-permute-start(bf16[2,2,64,256]{3,2,1,0:T(8,128)(2,1)} %ocean_hbm.1), channel_id=1, source_target_pairs={{0,0},{1,2},{2,1},{3,3},{4,4},{5,6},{6,5},{7,7},{8,8},{9,10},{10,9... | collective-permute-start | bytes 393224 | tf_op jit(solution)/shard_map/ppermute | solution.py:499
  5.2 1.0 %copy-done = f32[6,64,256]{2,1,0:T(8,128)S(1)} copy-done((f32[6,64,256]{2,1,0:T(8,128)S(1)}, f32[6,64,256]{2,1,0:T(8,128)}, u32[]{:S(2)}) %copy-start) | copy-done | bytes 393240
  6.2 1.0 %copy-done.1 = f32[6,64,256]{2,1,0:T(8,128)S(1)} copy-done((f32[6,64,256]{2,1,0:T(8,128)S(1)}, f32[6,64,256]{2,1,0:T(8,128)}, u32[]{:S(2)}) %copy-start.1) | copy-done | bytes 393240
  7.2 0.9 %copy-done.2 = f32[3,64,256]{2,1,0:T(8,128)S(1)} copy-done((f32[3,64,256]{2,1,0:T(8,128)S(1)}, f32[3,64,256]{2,1,0:T(8,128)}, u32[]{:S(2)}) %copy-start.2) | copy-done | bytes 196632
  8.2 0.9 %copy-done.3 = f32[2,64,256]{2,1,0:T(8,128)S(1)} copy-done((f32[2,64,256]{2,1,0:T(8,128)S(1)}, f32[2,64,256]{2,1,0:T(8,128)}, u32[]{:S(2)}) %copy-start.3) | copy-done | bytes 131096
  9.1 0.9 %copy-done.4 = bf16[2,2,64,256]{3,2,1,0:T(8,128)(2,1)S(1)} copy-done((bf16[2,2,64,256]{3,2,1,0:T(8,128)(2,1)S(1)}, bf16[2,2,64,256]{3,2,1,0:T(8,128)(2,1)}, u32[]{:S(2)}) %copy-start.4) | copy-done | bytes 131096
  10.0 0.9 %copy-done.5 = bf16[2,2,64,256]{3,2,1,0:T(8,128)(2,1)S(1)} copy-done((bf16[2,2,64,256]{3,2,1,0:T(8,128)(2,1)S(1)}, bf16[2,2,64,256]{3,2,1,0:T(8,128)(2,1)}, u32[]{:S(2)}) %copy-start.5) | copy-done | bytes 131096
  10.9 0.8 %copy-done.6 = s32[64,256]{1,0:T(8,128)S(1)} copy-done((s32[64,256]{1,0:T(8,128)S(1)}, s32[64,256]{1,0:T(8,128)}, u32[]{:S(2)}) %copy-start.6) | copy-done | bytes 65560
  11.7 0.7 %copy-done.7 = bf16[64,128]{1,0:T(8,128)(2,1)S(1)} copy-done((bf16[64,128]{1,0:T(8,128)(2,1)S(1)}, bf16[64,128]{1,0:T(8,128)(2,1)}, u32[]{:S(2)}) %copy-start.7) | copy-done | bytes 16408
  12.4 2.2 %local.1 = (f32[6,64,256]{2,1,0:T(8,128)}, f32[9,64,256]{2,1,0:T(8,128)S(1)}, f32[2,2,64,256]{3,2,1,0:T(8,128)S(1)}, bf16[64,128]{1,0:T(8,128)(2,1)S(1)}, bf16[6...) custom-call(s32[1,16]{1,0:T(1,128)S(1)} %copy-done.8, ...), custom_call_target="tpu_custom_call" | custom-call | flops 9830400 | bytes 1179648 | tf_op jit(solution)/shard_map/local/pallas_call | solution.py:536
  14.6 0.0 collective-permute-done.tile_x_ref
  14.7 0.0 collective-permute-done.1.tile_y_ref
  14.7 0.3 %force.1 = (f32[4,64,256]{2,1,0:T(8,128)S(1)}, bf16[64,256]{1,0:T(8,128)(2,1)S(1)}, bf16[64,256]{1,0:T(8,128)(2,1)S(1)}, bf16[208,256]{1,0:T(8,128)(2,1)S(1)}, bf16[208,256]{1,0:T(8,128)(2,1)S(1)}) custom-call(bf16[64,128]{1,0:T(8,128)(2,1)S(1)} %get-tuple-element.67.side_ref, bf16[2,2,64,256]{3,2,1,0:T(8,128)(2,1)S(1)} %collective-permute-done.tile_x_ref, ...), custom_call_target="tpu_custom_call" | custom-call | tf_op jit(solution)/shard_map/force/pallas_call | solution.py:584
  15.0 1.3 %collective-permute-start.2 = (bf16[64,256]{1,0:T(8,128)(2,1)S(1)}, bf16[64,256]{1,0:T(8,128)(2,1)S(1)}, u32[]{:S(2)}, u32[]{:S(2)}) collective-permute-start(bf16[64,256]{1,0:T(8,128)(2,1)S(1)} %get-tuple-element.74), channel_id=1, source_target_pairs={{0,4},{4,0},{8,12},{12,8},{16,20},{20,16},{24,28},{28,24},{1,5},{5... | collective-permute-start | bytes 98312 | tf_op jit(solution)/shard_map/ppermute | solution.py:498
  16.3 1.2 %collective-permute-start.3 = (bf16[64,256]{1,0:T(8,128)(2,1)S(1)}, bf16[64,256]{1,0:T(8,128)(2,1)S(1)}, u32[]{:S(2)}, u32[]{:S(2)}) collective-permute-start(bf16[64,256]{1,0:T(8,128)(2,1)S(1)} %get-tuple-element.75), channel_id=1, source_target_pairs={{0,28},{4,8},{8,4},{12,16},{16,12},{20,24},{24,20},{28,0},{1,29},{... | collective-permute-start | bytes 98312 | tf_op jit(solution)/shard_map/ppermute | solution.py:499
  17.5 0.0 collective-permute-done.2.lon_x_ref
  17.5 3.0 %collective-permute-done.3.lon_y_ref = bf16[64,256]{1,0:T(8,128)(2,1)S(1)} collective-permute-done((bf16[64,256]{1,0:T(8,128)(2,1)S(1)}, bf16[64,256]{1,0:T(8,128)(2,1)S(1)}, u32[]{:S(2)}, u32[]{:S(2)}) %collective-permute-start.3) | collective-permute-done | bytes 32800 | tf_op jit(solution)/shard_map/ppermute | solution.py:499
  20.6 0.0 collective-permute-start.4
  20.6 1.9 %collective-permute-start.5 = (bf16[208,256]{1,0:T(8,128)(2,1)S(1)}, bf16[208,256]{1,0:T(8,128)(2,1)S(1)}, u32[]{:S(2)}, u32[]{:S(2)}) collective-permute-start(bf16[208,256]{1,0:T(8,128)(2,1)S(1)} %get-tuple-element.81), channel_id=1, source_target_pairs={{0,0},{1,2},{2,1},{3,3},{4,4},{5,6},{6,5},{7,7},{8,8},{9,10},{10,9... | collective-permute-start | bytes 319496 | tf_op jit(solution)/shard_map/ppermute | solution.py:499
  22.5 2.7 %collective-permute-done.4.lat_x_ref = bf16[208,256]{1,0:T(8,128)(2,1)S(1)} collective-permute-done((bf16[208,256]{1,0:T(8,128)(2,1)S(1)}, bf16[208,256]{1,0:T(8,128)(2,1)S(1)}, u32[]{:S(2)}, u32[]{:S(2)}) %collective-permute-start.4) | collective-permute-done | bytes 106528 | tf_op jit(solution)/shard_map/ppermute | solution.py:498
  25.2 1.6 %collective-permute-done.5.lat_y_ref = bf16[208,256]{1,0:T(8,128)(2,1)S(1)} collective-permute-done((bf16[208,256]{1,0:T(8,128)(2,1)S(1)}, bf16[208,256]{1,0:T(8,128)(2,1)S(1)}, u32[]{:S(2)}, u32[]{:S(2)}) %collective-permute-start.5) | collective-permute-done | bytes 106528 | tf_op jit(solution)/shard_map/ppermute | solution.py:499
  26.8 3.9 %dynamics.1 = (f32[2,64,256]{2,1,0:T(8,128)}, f32[3,64,256]{2,1,0:T(8,128)}) custom-call(f32[9,64,256]{2,1,0:T(8,128)S(1)} %get-tuple-element.66.fields_ref, f32[4,64,256]{2,1,0:T(8,128)S(1)} %get-tuple-element.73.force_ref, bf16[64,256]{1,0:T(8,128)(2,1)S(1)} %collective-permute-done.2.lon_x_ref, bf16[64,256]{1,0:T(8,128)(2,1)S(1)} %collective-permute-done.3.lon_y_ref, ...), custom_call_target="tpu_custom_call" | custom-call | tf_op jit(solution)/shard_map/dynamics/pallas_call | solution.py:615
  (13 shorter events, 0.0 us)
Async XLA Ops:
  0.6 4.6 %copy-start.8 = (s32[1,16]{1,0:T(1,128)S(1)}, s32[1,16]{1,0:T(1,128)}, u32[]{:S(2)}) copy-start(s32[1,16]{1,0:T(1,128)} %covered_hbm.1) | copy-start | bytes 196
  0.6 4.6 %copy-start.9 = (s32[64]{0:T(128)S(1)}, s32[64]{0:T(128)}, u32[]{:S(2)}) copy-start(s32[64]{0:T(128)} %param.27) | copy-start | bytes 772
  0.7 14.0 %collective-permute-start = (bf16[2,2,64,256]{3,2,1,0:T(8,128)(2,1)}, bf16[2,2,64,256]{3,2,1,0:T(8,128)(2,1)S(1)}, u32[]{:S(2)}, u32[]{:S(2)}) collective-permute-start(bf16[2,2,64,256]{3,2,1,0:T(8,128)(2,1)} %ocean_hbm.1), channel_id=1, source_target_pairs={{0,1},{1,0},{2,3},{3,2},{4,5},{5,4},{6,7},{7,6},{8,9},{9,8},{10,11... | collective-permute-start | bytes 393224 | tf_op jit(solution)/shard_map/ppermute | solution.py:498
  0.9 13.8 %collective-permute-start.1 = (bf16[2,2,64,256]{3,2,1,0:T(8,128)(2,1)}, bf16[2,2,64,256]{3,2,1,0:T(8,128)(2,1)S(1)}, u32[]{:S(2)}, u32[]{:S(2)}) collective-permute-start(bf16[2,2,64,256]{3,2,1,0:T(8,128)(2,1)} %ocean_hbm.1), channel_id=1, source_target_pairs={{0,0},{1,2},{2,1},{3,3},{4,4},{5,6},{6,5},{7,7},{8,8},{9,10},{10,9... | collective-permute-start | bytes 393224 | tf_op jit(solution)/shard_map/ppermute | solution.py:499
  5.2 1.0 %copy-start = (f32[6,64,256]{2,1,0:T(8,128)S(1)}, f32[6,64,256]{2,1,0:T(8,128)}, u32[]{:S(2)}) copy-start(f32[6,64,256]{2,1,0:T(8,128)} %thick_hbm.1) | copy-start | bytes 1179652
  6.2 1.0 %copy-start.1 = (f32[6,64,256]{2,1,0:T(8,128)S(1)}, f32[6,64,256]{2,1,0:T(8,128)}, u32[]{:S(2)}) copy-start(f32[6,64,256]{2,1,0:T(8,128)} %conc_hbm.1) | copy-start | bytes 1179652
  7.2 0.9 %copy-start.2 = (f32[3,64,256]{2,1,0:T(8,128)S(1)}, f32[3,64,256]{2,1,0:T(8,128)}, u32[]{:S(2)}) copy-start(f32[3,64,256]{2,1,0:T(8,128)} %stress_hbm.1) | copy-start | bytes 589828
  8.2 0.9 %copy-start.3 = (f32[2,64,256]{2,1,0:T(8,128)S(1)}, f32[2,64,256]{2,1,0:T(8,128)}, u32[]{:S(2)}) copy-start(f32[2,64,256]{2,1,0:T(8,128)} %velocity_hbm.1) | copy-start | bytes 393220
  9.1 0.9 %copy-start.4 = (bf16[2,2,64,256]{3,2,1,0:T(8,128)(2,1)S(1)}, bf16[2,2,64,256]{3,2,1,0:T(8,128)(2,1)}, u32[]{:S(2)}) copy-start(bf16[2,2,64,256]{3,2,1,0:T(8,128)(2,1)} %wind_hbm.1) | copy-start | bytes 393220
  10.0 0.9 %copy-start.5 = (bf16[2,2,64,256]{3,2,1,0:T(8,128)(2,1)S(1)}, bf16[2,2,64,256]{3,2,1,0:T(8,128)(2,1)}, u32[]{:S(2)}) copy-start(bf16[2,2,64,256]{3,2,1,0:T(8,128)(2,1)} %ocean_hbm.1) | copy-start | bytes 393220
  10.9 0.8 %copy-start.6 = (s32[64,256]{1,0:T(8,128)S(1)}, s32[64,256]{1,0:T(8,128)}, u32[]{:S(2)}) copy-start(s32[64,256]{1,0:T(8,128)} %mask_hbm.1) | copy-start | bytes 196612
  11.7 0.7 %copy-start.7 = (bf16[64,128]{1,0:T(8,128)(2,1)S(1)}, bf16[64,128]{1,0:T(8,128)(2,1)}, u32[]{:S(2)}) copy-start(bf16[64,128]{1,0:T(8,128)(2,1)} %weights_hbm.1) | copy-start | bytes 49156
  15.0 2.5 %collective-permute-start.2 = (bf16[64,256]{1,0:T(8,128)(2,1)S(1)}, bf16[64,256]{1,0:T(8,128)(2,1)S(1)}, u32[]{:S(2)}, u32[]{:S(2)}) collective-permute-start(bf16[64,256]{1,0:T(8,128)(2,1)S(1)} %get-tuple-element.74), channel_id=1, source_target_pairs={{0,4},{4,0},{8,12},{12,8},{16,20},{20,16},{24,28},{28,24},{1,5},{5... | collective-permute-start | bytes 98312 | tf_op jit(solution)/shard_map/ppermute | solution.py:498
  16.3 4.2 %collective-permute-start.3 = (bf16[64,256]{1,0:T(8,128)(2,1)S(1)}, bf16[64,256]{1,0:T(8,128)(2,1)S(1)}, u32[]{:S(2)}, u32[]{:S(2)}) collective-permute-start(bf16[64,256]{1,0:T(8,128)(2,1)S(1)} %get-tuple-element.75), channel_id=1, source_target_pairs={{0,28},{4,8},{8,4},{12,16},{16,12},{20,24},{24,20},{28,0},{1,29},{... | collective-permute-start | bytes 98312 | tf_op jit(solution)/shard_map/ppermute | solution.py:499
  20.6 4.6 %collective-permute-start.4 = (bf16[208,256]{1,0:T(8,128)(2,1)S(1)}, bf16[208,256]{1,0:T(8,128)(2,1)S(1)}, u32[]{:S(2)}, u32[]{:S(2)}) collective-permute-start(bf16[208,256]{1,0:T(8,128)(2,1)S(1)} %get-tuple-element.82), channel_id=1, source_target_pairs={{0,1},{1,0},{2,3},{3,2},{4,5},{5,4},{6,7},{7,6},{8,9},{9,8},{10,11... | collective-permute-start | bytes 319496 | tf_op jit(solution)/shard_map/ppermute | solution.py:498
  20.6 6.3 %collective-permute-start.5 = (bf16[208,256]{1,0:T(8,128)(2,1)S(1)}, bf16[208,256]{1,0:T(8,128)(2,1)S(1)}, u32[]{:S(2)}, u32[]{:S(2)}) collective-permute-start(bf16[208,256]{1,0:T(8,128)(2,1)S(1)} %get-tuple-element.81), channel_id=1, source_target_pairs={{0,0},{1,2},{2,1},{3,3},{4,4},{5,6},{6,5},{7,7},{8,8},{9,10},{10,9... | collective-permute-start | bytes 319496 | tf_op jit(solution)/shard_map/ppermute | solution.py:499

commit v3 on v2

--- a/solution.py
+++ b/solution.py
@@ -482,22 +482,32 @@
     return pltpu.CompilerParams(vmem_limit_bytes=VMEM_LIMIT)
 
 
-def swaps(axis, first, ring):
-    n = lax.axis_size(axis)
-    if ring and n % 2:
+def lon_swaps(first):
+    n = lax.axis_size("lon")
+    if n % 2:
         raise ValueError("odd ring")
-    partner = list(range(n))
-    for i in range(first, n if ring else n - 1, 2):
-        j = (i + 1) % n
-        partner[i], partner[j] = j, i
-    return list(enumerate(partner))
-
-
-def exchange(x, y, axis, ring):
-    return (
-        lax.ppermute(x, axis, swaps(axis, 0, ring)),
-        lax.ppermute(y, axis, swaps(axis, 1, ring)),
-    )
+    pairs = [(i, (i + 1) % n) for i in range(first, n, 2)]
+    return pairs + [(j, i) for i, j in pairs]
+
+
+def lat_swaps(first):
+    m, n = lax.axis_size("lat"), lax.axis_size("lon")
+    partner = {}
+    for i in range(m):
+        north = i + 1 if (i - first) % 2 == 0 else i - 1
+        for k in range(n):
+            to = (north, k) if 0 <= north < m else (i, k ^ 1)
+            partner[k * m + i] = to[1] * m + to[0]
+    return list(partner.items())
+
+
+def lon_exchange(x, y):
+    return lax.ppermute(x, "lon", lon_swaps(0)), lax.ppermute(y, "lon", lon_swaps(1))
+
+
+def lat_exchange(x, y):
+    axes = ("lon", "lat")
+    return lax.ppermute(x, axes, lat_swaps(0)), lax.ppermute(y, axes, lat_swaps(1))
 
 
 def shape(dims, dtype=jnp.float32):
@@ -528,7 +538,7 @@
     message_rows = sum(depths)
     bf16 = jnp.bfloat16
 
-    tile_x, tile_y = exchange(ocean_current, ocean_current, "lat", False)
+    tile_x, tile_y = lat_exchange(ocean_current, ocean_current)
 
     whole = pl.BlockSpec(memory_space=pltpu.VMEM)
     anywhere = pl.BlockSpec(memory_space=pl.ANY)
@@ -569,16 +579,21 @@
         ),
         name="local",
     )(
-        covered,
-        tile_offset.reshape(1, rows),
-        regrid_weights,
-        thickness,
-        concentration,
-        land_mask,
-        velocity,
-        stress,
-        ocean_current,
-        wind_stress,
+        *(
+            pltpu.with_memory_space_constraint(x, pltpu.HBM)
+            for x in (
+                covered,
+                tile_offset.reshape(1, rows),
+                regrid_weights,
+                thickness,
+                concentration,
+                land_mask,
+                velocity,
+                stress,
+                ocean_current,
+                wind_stress,
+            )
+        )
     )
 
     force, lon_x, lon_y, lat_x, lat_y = pl.pallas_call(
@@ -596,7 +611,7 @@
         name="force",
     )(side, tile_x, tile_y, current, fields, lon_x, lon_y, lat_x, lat_y)
 
-    lon_x, lon_y = exchange(lon_x, lon_y, "lon", True)
+    lon_x, lon_y = lon_exchange(lon_x, lon_y)
     north_end = rows - margin
     start_x = jnp.where(even("lat"), north_end, 0)
     for number, part in enumerate((lon_x, lon_y)):
@@ -605,7 +620,7 @@
         corner_y = lax.dynamic_slice_in_dim(part, north_end - start_x, margin, 0)
         lat_x = lat_x.at[at : at + margin, :packed].set(corner_x)
         lat_y = lat_y.at[at : at + margin, :packed].set(corner_y)
-    lat_x, lat_y = exchange(lat_x, lat_y, "lat", False)
+    lat_x, lat_y = lat_exchange(lat_x, lat_y)
 
     height = rows + 2 * margin + 2 * PAD
 

time: 31.1 us -> 22.1 us (0.71)
  the two profiles are of different devices: /device:TPU:11 before, /device:TPU:0 now
where the time goes in v3:
time: 22.1 us; the launch traced here: 21.9 us
  starting transfers between devices  8.76 us (40%)
  Pallas kernels  6.56 us (30%)
  waiting for transfers between devices  5.9 us (27%)
  between operations  0.68 us (3%)
    ppermute x2, starting transfers between devices, lat_exchange(): lax.ppermute(x, axes, lat_swaps(0))  5.99 us
    ppermute x2, waiting for transfers between devices, lat_exchange(): lax.ppermute(x, axes, lat_swaps(0))  4.3 us
    pallas_call x1, Pallas kernels, local(): pl.pallas_call(functools.partial(dynamics_kernel, margin, lax.axis_size('...  3.88 us
    ppermute x1, starting transfers between devices, lon_exchange(): lax.ppermute(y, 'lon', lon_swaps(1))  2.7 us
    pallas_call x1, Pallas kernels, local(): pl.pallas_call(functools.partial(local_kernel, margin), out_shape=(shape(...  2.34 us
    ppermute x1, waiting for transfers between devices, lon_exchange(): lax.ppermute(y, 'lon', lon_swaps(1))  1.6 us
  transfers between devices with their start and end apart: 6, of which 3 were waited for; matrix products, arithmetic and copies ran while one was open for 0% of the time, Pallas kernels for 11%

profile of v3, /device:TPU:0, one launch (start us, length us, event | category | flops | bytes accessed | tf_op | source)
XLA Modules:
  0.0 21.9 jit_solution(2494808370302082079)
XLA Ops:
  0.6 3.1 %collective-permute-start = (bf16[2,2,64,256]{3,2,1,0:T(8,128)(2,1)}, bf16[2,2,64,256]{3,2,1,0:T(8,128)(2,1)S(1)}, u32[]{:S(2)}, u32[]{:S(2)}) collective-permute-start(bf16[2,2,64,256]{3,2,1,0:T(8,128)(2,1)} %ocean_hbm.1), channel_id=1, source_target_pairs={{0,1},{4,5},{8,9},{12,13},{16,17},{20,21},{24,25},{28,29},{1,0},{5... | collective-permute-start | bytes 393224 | tf_op jit(solution)/shard_map/ppermute | solution.py:510
  3.7 0.0 collective-permute-start.1
  3.7 2.3 %local.1 = (f32[6,64,256]{2,1,0:T(8,128)}, f32[9,64,256]{2,1,0:T(8,128)S(1)}, f32[2,2,64,256]{3,2,1,0:T(8,128)S(1)}, bf16[64,128]{1,0:T(8,128)(2,1)S(1)}, bf16[6...) custom-call(s32[1,16]{1,0:T(1,128)} %covered_hbm.1, ...), custom_call_target="tpu_custom_call" | custom-call | flops 9830400 | bytes 1179648 | tf_op jit(solution)/shard_map/local/pallas_call | solution.py:546
  6.1 1.4 %collective-permute-done.tile_x_ref = bf16[2,2,64,256]{3,2,1,0:T(8,128)(2,1)S(1)} collective-permute-done((bf16[2,2,64,256]{3,2,1,0:T(8,128)(2,1)}, bf16[2,2,64,256]{3,2,1,0:T(8,128)(2,1)S(1)}, u32[]{:S(2)}, u32[]{:S(2)}) %collective-permute-start) | collective-permute-done | bytes 131104 | tf_op jit(solution)/shard_map/ppermute | solution.py:510
  7.4 0.0 collective-permute-done.1.tile_y_ref
  7.4 0.3 %force.1 = (f32[4,64,256]{2,1,0:T(8,128)S(1)}, bf16[64,256]{1,0:T(8,128)(2,1)S(1)}, bf16[64,256]{1,0:T(8,128)(2,1)S(1)}, bf16[208,256]{1,0:T(8,128)(2,1)S(1)}, bf16[208,256]{1,0:T(8,128)(2,1)S(1)}) custom-call(bf16[64,128]{1,0:T(8,128)(2,1)S(1)} %get-tuple-element.67.side_ref, bf16[2,2,64,256]{3,2,1,0:T(8,128)(2,1)S(1)} %collective-permute-done.tile_x_ref, ...), custom_call_target="tpu_custom_call" | custom-call | tf_op jit(solution)/shard_map/force/pallas_call | solution.py:599
  7.8 0.1 collective-permute-start.2
  7.9 2.7 %collective-permute-start.3 = (bf16[64,256]{1,0:T(8,128)(2,1)S(1)}, bf16[64,256]{1,0:T(8,128)(2,1)S(1)}, u32[]{:S(2)}, u32[]{:S(2)}) collective-permute-start(bf16[64,256]{1,0:T(8,128)(2,1)S(1)} %get-tuple-element.75), channel_id=1, source_target_pairs={{4,8},{12,16},{20,24},{28,0},{8,4},{16,12},{24,20},{0,28},{5,9},{1... | collective-permute-start | bytes 98312 | tf_op jit(solution)/shard_map/ppermute | solution.py:505
  10.6 0.0 collective-permute-done.2.lon_x_ref
  10.6 1.6 %collective-permute-done.3.lon_y_ref = bf16[64,256]{1,0:T(8,128)(2,1)S(1)} collective-permute-done((bf16[64,256]{1,0:T(8,128)(2,1)S(1)}, bf16[64,256]{1,0:T(8,128)(2,1)S(1)}, u32[]{:S(2)}, u32[]{:S(2)}) %collective-permute-start.3) | collective-permute-done | bytes 32800 | tf_op jit(solution)/shard_map/ppermute | solution.py:505
  12.2 2.9 %collective-permute-start.4 = (bf16[208,256]{1,0:T(8,128)(2,1)S(1)}, bf16[208,256]{1,0:T(8,128)(2,1)S(1)}, u32[]{:S(2)}, u32[]{:S(2)}) collective-permute-start(bf16[208,256]{1,0:T(8,128)(2,1)S(1)} %get-tuple-element.82), channel_id=1, source_target_pairs={{0,1},{4,5},{8,9},{12,13},{16,17},{20,21},{24,25},{28,29},{1,0},{5... | collective-permute-start | bytes 319496 | tf_op jit(solution)/shard_map/ppermute | solution.py:510
  15.1 0.0 collective-permute-start.5
  15.1 2.9 %collective-permute-done.4.lat_x_ref = bf16[208,256]{1,0:T(8,128)(2,1)S(1)} collective-permute-done((bf16[208,256]{1,0:T(8,128)(2,1)S(1)}, bf16[208,256]{1,0:T(8,128)(2,1)S(1)}, u32[]{:S(2)}, u32[]{:S(2)}) %collective-permute-start.4) | collective-permute-done | bytes 106528 | tf_op jit(solution)/shard_map/ppermute | solution.py:510
  18.0 0.0 collective-permute-done.5.lat_y_ref
  18.0 3.9 %dynamics.1 = (f32[2,64,256]{2,1,0:T(8,128)}, f32[3,64,256]{2,1,0:T(8,128)}) custom-call(f32[9,64,256]{2,1,0:T(8,128)S(1)} %get-tuple-element.66.fields_ref, f32[4,64,256]{2,1,0:T(8,128)S(1)} %get-tuple-element.73.force_ref, bf16[64,256]{1,0:T(8,128)(2,1)S(1)} %collective-permute-done.2.lon_x_ref, bf16[64,256]{1,0:T(8,128)(2,1)S(1)} %collective-permute-done.3.lon_y_ref, ...), custom_call_target="tpu_custom_call" | custom-call | tf_op jit(solution)/shard_map/dynamics/pallas_call | solution.py:630
  (2 shorter events, 0.0 us)
Async XLA Ops:
  0.6 6.8 %collective-permute-start = (bf16[2,2,64,256]{3,2,1,0:T(8,128)(2,1)}, bf16[2,2,64,256]{3,2,1,0:T(8,128)(2,1)S(1)}, u32[]{:S(2)}, u32[]{:S(2)}) collective-permute-start(bf16[2,2,64,256]{3,2,1,0:T(8,128)(2,1)} %ocean_hbm.1), channel_id=1, source_target_pairs={{0,1},{4,5},{8,9},{12,13},{16,17},{20,21},{24,25},{28,29},{1,0},{5... | collective-permute-start | bytes 393224 | tf_op jit(solution)/shard_map/ppermute | solution.py:510
  3.7 3.7 %collective-permute-start.1 = (bf16[2,2,64,256]{3,2,1,0:T(8,128)(2,1)}, bf16[2,2,64,256]{3,2,1,0:T(8,128)(2,1)S(1)}, u32[]{:S(2)}, u32[]{:S(2)}) collective-permute-start(bf16[2,2,64,256]{3,2,1,0:T(8,128)(2,1)} %ocean_hbm.1), channel_id=1, source_target_pairs={{0,4},{4,0},{8,12},{12,8},{16,20},{20,16},{24,28},{28,24},{1,2},{5... | collective-permute-start | bytes 393224 | tf_op jit(solution)/shard_map/ppermute | solution.py:510
  7.8 2.8 %collective-permute-start.2 = (bf16[64,256]{1,0:T(8,128)(2,1)S(1)}, bf16[64,256]{1,0:T(8,128)(2,1)S(1)}, u32[]{:S(2)}, u32[]{:S(2)}) collective-permute-start(bf16[64,256]{1,0:T(8,128)(2,1)S(1)} %get-tuple-element.74), channel_id=1, source_target_pairs={{0,4},{8,12},{16,20},{24,28},{4,0},{12,8},{20,16},{28,24},{1,5},{9... | collective-permute-start | bytes 98312 | tf_op jit(solution)/shard_map/ppermute | solution.py:505
  7.9 4.3 %collective-permute-start.3 = (bf16[64,256]{1,0:T(8,128)(2,1)S(1)}, bf16[64,256]{1,0:T(8,128)(2,1)S(1)}, u32[]{:S(2)}, u32[]{:S(2)}) collective-permute-start(bf16[64,256]{1,0:T(8,128)(2,1)S(1)} %get-tuple-element.75), channel_id=1, source_target_pairs={{4,8},{12,16},{20,24},{28,0},{8,4},{16,12},{24,20},{0,28},{5,9},{1... | collective-permute-start | bytes 98312 | tf_op jit(solution)/shard_map/ppermute | solution.py:505
  12.2 5.8 %collective-permute-start.4 = (bf16[208,256]{1,0:T(8,128)(2,1)S(1)}, bf16[208,256]{1,0:T(8,128)(2,1)S(1)}, u32[]{:S(2)}, u32[]{:S(2)}) collective-permute-start(bf16[208,256]{1,0:T(8,128)(2,1)S(1)} %get-tuple-element.82), channel_id=1, source_target_pairs={{0,1},{4,5},{8,9},{12,13},{16,17},{20,21},{24,25},{28,29},{1,0},{5... | collective-permute-start | bytes 319496 | tf_op jit(solution)/shard_map/ppermute | solution.py:510
  15.1 2.9 %collective-permute-start.5 = (bf16[208,256]{1,0:T(8,128)(2,1)S(1)}, bf16[208,256]{1,0:T(8,128)(2,1)S(1)}, u32[]{:S(2)}, u32[]{:S(2)}) collective-permute-start(bf16[208,256]{1,0:T(8,128)(2,1)S(1)} %get-tuple-element.81), channel_id=1, source_target_pairs={{0,4},{4,0},{8,12},{12,8},{16,20},{20,16},{24,28},{28,24},{1,2},{5... | collective-permute-start | bytes 319496 | tf_op jit(solution)/shard_map/ppermute | solution.py:510

commit v4 on v3

--- a/solution.py
+++ b/solution.py
@@ -11,7 +11,6 @@
 SUB = 4
 LANES = 128
 GROUP = 16
-PAD = 8
 STATE = 5
 VMEM_LIMIT = 16 * 1024 * 1024
 
@@ -299,79 +298,137 @@
         ref[row:] = jnp.zeros((ref.shape[0] - row, cols), jnp.bfloat16)
 
 
-def dynamics_kernel(
-    margin,
-    lat_count,
-    fields_ref,
-    force_ref,
-    lon_x_ref,
-    lon_y_ref,
-    lat_x_ref,
-    lat_y_ref,
-    velocity_ref,
-    stress_ref,
-    state,
-    strength,
-    keep,
-    push,
-    force,
-):
+def place(refs, early, field, tile, row, value):
+    velocity, stress, strength, keep, push, force = refs
+    at = pl.ds(row, value.shape[0])
+    if field < 2:
+        velocity[0, field, tile, at, :] = value
+    elif field < STATE:
+        stress[0, field - 2, tile, at, :] = value
+    elif field >= early:
+        window, kind = divmod(field - early, 2)
+        force[window, kind, tile, at, :] = value
+    else:
+        window, kind = divmod(field - STATE, 2)
+        if kind == 0:
+            strength[window, tile, at, :] = value
+        else:
+            push[window, tile, at, :] = value * 0.25
+            keep[window, tile, at, :] = jnp.where(value > 0.0, 1.0 - value, 0.0)
+
+
+def place_sides(refs, early, count, margin, x, y, row):
+    last = refs[0].shape[2] - 1
+    per = LANES // margin
+    wide = lax.broadcasted_iota(jnp.int32, (x.shape[0], LANES), 1)
+    from_x_is_east = even("lon")
+    for group in range(x.shape[1] // LANES):
+        lanes = slice(group * LANES, (group + 1) * LANES)
+        x_now, y_now = x[:, lanes], y[:, lanes]
+        east = jnp.where(from_x_is_east, x_now, y_now)
+        west = jnp.where(from_x_is_east, y_now, x_now)
+        for slot in range(min(per, count - group * per)):
+            shift = slot * margin
+            back = (LANES - margin - shift) % LANES
+            e = pltpu.roll(east, LANES - shift, 1) if shift else east
+            w = pltpu.roll(west, back, 1) if back else west
+            value = jnp.where(wide < margin, e, jnp.where(wide >= LANES - margin, w, 0.0))
+            place(refs, early, group * per + slot, last, row, value)
+
+
+def across(values):
+    tiles = len(values)
+    lane = lax.broadcasted_iota(jnp.int32, values[0].shape, 1)
+    ahead = [pltpu.roll(x, LANES - 1, 1) for x in values]
+    behind = [pltpu.roll(x, 1, 1) for x in values]
+    return [
+        jnp.where(lane == LANES - 1, ahead[(j + 1) % tiles], ahead[j])
+        - jnp.where(lane == 0, behind[j - 1], behind[j])
+        for j in range(tiles)
+    ]
+
+
+def stress_rows(refs, step, window, row):
+    velocity, stress, strength, _, _, _ = refs
+    every = range(velocity.shape[2])
+    at, north, south = pl.ds(row, 8), pl.ds(row + 1, 8), pl.ds(row - 1, 8)
+    u_x = across([velocity[step, 0, j, at, :] for j in every])
+    v_x = across([velocity[step, 1, j, at, :] for j in every])
+    for j in every:
+        u_y = velocity[step, 0, j, north, :] - velocity[step, 0, j, south, :]
+        v_y = velocity[step, 1, j, north, :] - velocity[step, 1, j, south, :]
+        shear = u_y + v_x[j]
+        spread = u_x[j] + v_y
+        tension = u_x[j] - v_y
+        tension4 = tension * 0.25
+        shear4 = shear * 0.25
+        squares = spread * spread + tension * tension4 + (shear * shear4 + 1.0)
+        k = strength[window, j, at, :]
+        kr = k * lax.rsqrt(squares)
+        old = [stress[step, i, j, at, :] * (2.0 / 3.0) for i in range(3)]
+        stress[step + 1, 0, j, at, :] = old[0] + (kr * (spread + tension4) - k)
+        stress[step + 1, 1, j, at, :] = old[1] + (kr * (spread - tension4) - k)
+        stress[step + 1, 2, j, at, :] = old[2] + kr * shear4
+
+
+def velocity_rows(refs, step, window, row):
+    velocity, stress, _, keep, push, force = refs
+    every = range(velocity.shape[2])
+    at, north, south = pl.ds(row, 8), pl.ds(row + 1, 8), pl.ds(row - 1, 8)
+    now = step + 1
+    p_x = across([stress[now, 0, j, at, :] for j in every])
+    t_x = across([stress[now, 2, j, at, :] for j in every])
+    for j in every:
+        q_y = stress[now, 1, j, north, :] - stress[now, 1, j, south, :]
+        t_y = stress[now, 2, j, north, :] - stress[now, 2, j, south, :]
+        a = keep[window, j, at, :]
+        b = push[window, j, at, :]
+        velocity[now, 0, j, at, :] = (
+            a * velocity[step, 0, j, at, :] + b * (p_x[j] + t_y) + force[window, 0, j, at, :]
+        )
+        velocity[now, 1, j, at, :] = (
+            a * velocity[step, 1, j, at, :] + b * (t_x[j] + q_y) + force[window, 1, j, at, :]
+        )
+
+
+def interior_kernel(margin, fields_ref, force_ref, lon_x_ref, lon_y_ref, *refs):
     early, rows, cols = fields_ref.shape
-    windows = strength.shape[0]
     count = early + force_ref.shape[0]
-    own_tiles = cols // LANES
-    tiles = own_tiles + 1
-    per = LANES // margin
-    top = PAD + margin
-    bottom = top + rows
-    lane = lax.broadcasted_iota(jnp.int32, (8, LANES), 1)
-
-    def place(field, tile, row, value):
-        at = pl.ds(row, value.shape[0])
-        if field < STATE:
-            state[field, tile, at, :] = value
-        elif field >= early:
-            window, kind = divmod(field - early, 2)
-            force[window, kind, tile, at, :] = value
-        else:
-            window, kind = divmod(field - STATE, 2)
-            if kind == 0:
-                strength[window, tile, at, :] = value
-            else:
-                push[window, tile, at, :] = value
-                keep[window, tile, at, :] = jnp.where(value > 0.0, 1.0 - value, 0.0)
-
-    zero = jnp.zeros((PAD, LANES), jnp.float32)
-    for tile in range(tiles):
-        for field in range(STATE):
-            state[field, tile, 0:PAD, :] = zero
-            state[field, tile, bottom + margin : bottom + margin + PAD, :] = zero
-
-    def side_tiles(x, y, row):
-        wide = lax.broadcasted_iota(jnp.int32, (x.shape[0], LANES), 1)
-        from_x_is_east = even("lon")
-        for group in range(x.shape[1] // LANES):
-            lanes = slice(group * LANES, (group + 1) * LANES)
-            x_now, y_now = x[:, lanes], y[:, lanes]
-            east = jnp.where(from_x_is_east, x_now, y_now)
-            west = jnp.where(from_x_is_east, y_now, x_now)
-            for slot in range(min(per, count - group * per)):
-                shift = slot * margin
-                back = (LANES - margin - shift) % LANES
-                e = pltpu.roll(east, LANES - shift, 1) if shift else east
-                w = pltpu.roll(west, back, 1) if back else west
-                value = jnp.where(wide < margin, e, jnp.where(wide >= LANES - margin, w, 0.0))
-                place(group * per + slot, own_tiles, row, value)
-
+    windows = refs[2].shape[0]
     for field in range(count):
-        for tile in range(own_tiles):
+        for tile in range(cols // LANES):
             lanes = slice(tile * LANES, (tile + 1) * LANES)
             own = fields_ref[field, :, lanes] if field < early else force_ref[field - early, :, lanes]
-            place(field, tile, top, own)
-    side_tiles(lon_x_ref[...].astype(jnp.float32), lon_y_ref[...].astype(jnp.float32), top)
-
+            place(refs, early, field, tile, margin, own)
+    lon_x, lon_y = lon_x_ref[...].astype(jnp.float32), lon_y_ref[...].astype(jnp.float32)
+    place_sides(refs, early, count, margin, lon_x, lon_y, margin)
+    for window in range(windows):
+        lost = 2 * SUB * window
+        row_list = range(margin + lost, margin + rows - lost, 8)
+
+        def subcycle(number, carry):
+            step = window * SUB + number
+            for row in row_list:
+                stress_rows(refs, step, window, row)
+            for row in row_list:
+                velocity_rows(refs, step, window, row)
+            return carry
+
+        lax.fori_loop(0, SUB, subcycle, 0)
+
+
+def rim_kernel(margin, early, count, lat_count, *args):
+    lat_x_ref, lat_y_ref = args[:2]
+    refs = args[2:8]
+    velocity_ref, stress_ref = args[8:10]
+    velocity, stress = refs[:2]
+    windows = refs[2].shape[0]
+    _, rows, cols = velocity_ref.shape
+    own_tiles = cols // LANES
+    bottom = margin + rows
     depths = field_depths(margin, windows)
     groups = message_groups(range(early), depths) + message_groups(range(early, count), depths)
+    packed = -(-count // (LANES // margin)) * LANES
     me = lax.axis_index("lat")
     for ref, north in ((lat_x_ref, even("lat")), (lat_y_ref, jnp.logical_not(even("lat")))):
         exists = jnp.where(north, me < lat_count - 1, me > 0)
@@ -386,96 +443,40 @@
             begin = 0
             for field in group:
                 depth = depths[field]
-                to = pl.multiple_of(jnp.where(north, bottom, top - depth), 8)
+                to = pl.multiple_of(jnp.where(north, bottom, margin - depth), 8)
                 for tile in range(own_tiles):
                     lanes = slice(tile * LANES, (tile + 1) * LANES)
-                    place(field, tile, to, value[begin : begin + depth, lanes])
+                    place(refs, early, field, tile, to, value[begin : begin + depth, lanes])
                 begin += depth
             row += height
-        to = pl.multiple_of(jnp.where(north, bottom, top - margin), 8)
-        packed = lon_x_ref.shape[1]
-        side_tiles(
-            read(slice(row, row + margin))[:, :packed],
-            read(slice(row + margin, row + 2 * margin))[:, :packed],
-            to,
-        )
-
-    first_lane = lane == 0
-    last_lane = lane == LANES - 1
-
-    def across(values):
-        ahead = [pltpu.roll(x, LANES - 1, 1) for x in values]
-        behind = [pltpu.roll(x, 1, 1) for x in values]
-        return [
-            jnp.where(last_lane, ahead[(j + 1) % tiles], ahead[j])
-            - jnp.where(first_lane, behind[j - 1], behind[j])
-            for j in range(tiles)
-        ]
-
-    def along(field, tile, row):
-        return state[field, tile, row + 1 : row + 9, :] - state[field, tile, row - 1 : row + 7, :]
-
-    every = range(tiles)
-    for window in range(windows):
-        spare = 2 * SUB * window
-        row_list = range(top - margin + spare, bottom + margin - spare, 8)
-
-        def subcycle(_, carry):
-            for row in row_list:
-                at = slice(row, row + 8)
-                u_x = across([state[0, j, at, :] for j in every])
-                v_x = across([state[1, j, at, :] for j in every])
-                for j in every:
-                    u_y = along(0, j, row)
-                    v_y = along(1, j, row)
-                    shear = u_y + v_x[j]
-                    spread = u_x[j] + v_y
-                    tension = u_x[j] - v_y
-                    tension4 = tension * 0.25
-                    shear4 = shear * 0.25
-                    squares = spread * spread + tension * tension4 + (shear * shear4 + 1.0)
-                    k = strength[window, j, at, :]
-                    kr = k * lax.rsqrt(squares)
-                    state[2, j, at, :] = state[2, j, at, :] * (2.0 / 3.0) + (
-                        kr * (spread + tension4) - k
-                    )
-                    state[3, j, at, :] = state[3, j, at, :] * (2.0 / 3.0) + (
-                        kr * (spread - tension4) - k
-                    )
-                    state[4, j, at, :] = state[4, j, at, :] * (2.0 / 3.0) + kr * shear4
-            for row in row_list:
-                at = slice(row, row + 8)
-                p_x = across([state[2, j, at, :] for j in every])
-                t_x = across([state[4, j, at, :] for j in every])
-                for j in every:
-                    b = push[window, j, at, :] * 0.25
-                    a = keep[window, j, at, :]
-                    state[0, j, at, :] = (
-                        a * state[0, j, at, :]
-                        + b * (p_x[j] + along(4, j, row))
-                        + force[window, 0, j, at, :]
-                    )
-                    state[1, j, at, :] = (
-                        a * state[1, j, at, :]
-                        + b * (t_x[j] + along(3, j, row))
-                        + force[window, 1, j, at, :]
-                    )
-            return carry
-
-        lax.fori_loop(0, SUB, subcycle, 0)
+        to = pl.multiple_of(jnp.where(north, bottom, 0), 8)
+        east, west = (read(slice(at, at + margin))[:, :packed] for at in (row, row + margin))
+        place_sides(refs, early, count, margin, east, west, to)
+
+    def subcycle(step, carry):
+        window = step // SUB
+        done = 2 * step + 1
+        for half, rows_now in ((0, stress_rows), (1, velocity_rows)):
+            for first in range(0, margin, 8):
+                rows_now(refs, step, window, done + half + first)
+                rows_now(refs, step, window, bottom - done - half + first)
+        return carry
+
+    steps = SUB * windows
+    lax.fori_loop(0, steps, subcycle, 0)
 
     for tile in range(own_tiles):
         lanes = slice(tile * LANES, (tile + 1) * LANES)
         for row in range(0, rows, 8):
             at = slice(row, row + 8)
-            to = slice(top + row, top + row + 8)
-            velocity_ref[0, at, lanes] = state[0, tile, to, :]
-            velocity_ref[1, at, lanes] = state[1, tile, to, :]
-            p = state[2, tile, to, :]
-            q = state[3, tile, to, :]
+            own = slice(margin + row, margin + row + 8)
+            velocity_ref[0, at, lanes] = velocity[steps, 0, tile, own, :]
+            velocity_ref[1, at, lanes] = velocity[steps, 1, tile, own, :]
+            p = stress[steps, 0, tile, own, :]
+            q = stress[steps, 1, tile, own, :]
             stress_ref[0, at, lanes] = (p + q) * 0.5
             stress_ref[1, at, lanes] = (p - q) * 0.5
-            stress_ref[2, at, lanes] = state[4, tile, to, :] * 0.5
+            stress_ref[2, at, lanes] = stress[steps, 2, tile, own, :] * 0.5
 
 
 def params():
@@ -622,26 +623,40 @@
         lat_y = lat_y.at[at : at + margin, :packed].set(corner_y)
     lat_x, lat_y = lat_exchange(lat_x, lat_y)
 
-    height = rows + 2 * margin + 2 * PAD
-
-    def scratch(*lead):
-        return pltpu.VMEM((*lead, tiles, height, LANES), jnp.float32)
+    steps = SUB * windows
+
+    def widened(*lead):
+        return shape((*lead, tiles, rows + 2 * margin, LANES))
+
+    domain = (
+        widened(steps + 1, 2),
+        widened(steps + 1, 3),
+        widened(windows),
+        widened(windows),
+        widened(windows),
+        widened(windows, 2),
+    )
+    refs = pl.pallas_call(
+        functools.partial(interior_kernel, margin),
+        out_shape=domain,
+        in_specs=[whole] * 4,
+        out_specs=(whole,) * 6,
+        compiler_params=params(),
+        cost_estimate=pl.CostEstimate(
+            flops=60 * steps * rows * cols, bytes_accessed=2**22, transcendentals=0
+        ),
+        name="interior",
+    )(fields, force, lon_x, lon_y)
 
     velocity_out, stress_out = pl.pallas_call(
-        functools.partial(dynamics_kernel, margin, lax.axis_size("lat")),
-        out_shape=(shape(velocity.shape), shape(stress.shape)),
-        in_specs=[whole] * 6,
-        out_specs=(whole, whole),
-        scratch_shapes=[
-            scratch(STATE),
-            scratch(windows),
-            scratch(windows),
-            scratch(windows),
-            scratch(windows, 2),
-        ],
+        functools.partial(rim_kernel, margin, early, count, lax.axis_size("lat")),
+        out_shape=(shape(velocity.shape), shape(stress.shape)) + domain,
+        in_specs=[whole] * 8,
+        out_specs=(whole,) * 8,
+        input_output_aliases={2 + i: 2 + i for i in range(6)},
         compiler_params=params(),
-        name="dynamics",
-    )(fields, force, lon_x, lon_y, lat_x, lat_y)
+        name="rim",
+    )(lat_x, lat_y, *refs)[:2]
     return (velocity_out, stress_out, thick_out)
 
 

time: 22.1 us -> 22.1 us (level)
  waiting for transfers between devices: 5.9 us -> 3.36 us
  Pallas kernels: 6.56 us -> 8.08 us
  starting transfers between devices: 8.76 us -> 9.78 us
    ppermute x2, waiting for transfers between devices: 4.3 us -> 1.6 us  [lat_exchange(): lax.ppermute(x, axes, lat_swaps(0))]
    pallas_call x1 -> x2, Pallas kernels: 3.88 us -> 5.4 us  [the longest x1 3.04 us: local(): pl.pallas_call(functools.partial(rim_kernel, margin, early, count, lax.ax...]
    ppermute x2, starting transfers between devices: 5.99 us -> 6.64 us  [lat_exchange(): lax.ppermute(x, axes, lat_swaps(0))]
    ppermute x2, starting transfers between devices: 0.01 us -> 0.52 us  [lat_exchange(): lax.ppermute(y, axes, lat_swaps(1))]
  transfers between devices with their start and end apart: 6 -> 6, of which waited for: 3 -> 3; matrix products, arithmetic and copies ran while one was open for 0% -> 0% of each run, Pallas kernels for 11% -> 22%
where the time goes in v4:
time: 22.1 us; the launch traced here: 21.9 us
  starting transfers between devices  9.78 us (44%)
  Pallas kernels  8.08 us (37%)
  waiting for transfers between devices  3.36 us (15%)
  between operations  0.7 us (3%)
    ppermute x2, starting transfers between devices, lat_exchange(): lax.ppermute(x, axes, lat_swaps(0))  6.64 us
    pallas_call x1, Pallas kernels, local(): pl.pallas_call(functools.partial(rim_kernel, margin, early, count, lax.ax...  3.04 us
    ppermute x1, starting transfers between devices, lon_exchange(): lax.ppermute(y, 'lon', lon_swaps(1))  2.54 us
    pallas_call x1, Pallas kernels, local(): pl.pallas_call(functools.partial(interior_kernel, margin), out_shape=doma...  2.37 us
    pallas_call x1, Pallas kernels, local(): pl.pallas_call(functools.partial(local_kernel, margin), out_shape=(shape(...  2.34 us
    ppermute x1, waiting for transfers between devices, lon_exchange(): lax.ppermute(y, 'lon', lon_swaps(1))  1.76 us
    ppermute x2, waiting for transfers between devices, lat_exchange(): lax.ppermute(x, axes, lat_swaps(0))  1.6 us
    ppermute x2, starting transfers between devices, lat_exchange(): lax.ppermute(y, axes, lat_swaps(1))  0.52 us
  transfers between devices with their start and end apart: 6, of which 3 were waited for; matrix products, arithmetic and copies ran while one was open for 0% of the time, Pallas kernels for 22%

profile of v4, /device:TPU:0, one launch (start us, length us, event | category | flops | bytes accessed | tf_op | source)
XLA Modules:
  0.0 21.9 jit_solution(12302636953173515022)
XLA Ops:
  0.6 0.5 %collective-permute-start.1 = (bf16[2,2,64,256]{3,2,1,0:T(8,128)(2,1)}, bf16[2,2,64,256]{3,2,1,0:T(8,128)(2,1)S(1)}, u32[]{:S(2)}, u32[]{:S(2)}) collective-permute-start(bf16[2,2,64,256]{3,2,1,0:T(8,128)(2,1)} %ocean_hbm.1), channel_id=1, source_target_pairs={{0,4},{4,0},{8,12},{12,8},{16,20},{20,16},{24,28},{28,24},{1,2},{5... | collective-permute-start | bytes 393224 | tf_op jit(solution)/shard_map/ppermute | solution.py:511
  1.2 4.1 %collective-permute-start = (bf16[2,2,64,256]{3,2,1,0:T(8,128)(2,1)}, bf16[2,2,64,256]{3,2,1,0:T(8,128)(2,1)S(1)}, u32[]{:S(2)}, u32[]{:S(2)}) collective-permute-start(bf16[2,2,64,256]{3,2,1,0:T(8,128)(2,1)} %ocean_hbm.1), channel_id=1, source_target_pairs={{0,1},{4,5},{8,9},{12,13},{16,17},{20,21},{24,25},{28,29},{1,0},{5... | collective-permute-start | bytes 393224 | tf_op jit(solution)/shard_map/ppermute | solution.py:511
  5.3 2.3 %local.1 = (f32[6,64,256]{2,1,0:T(8,128)}, f32[9,64,256]{2,1,0:T(8,128)S(1)}, f32[2,2,64,256]{3,2,1,0:T(8,128)S(1)}, bf16[64,128]{1,0:T(8,128)(2,1)S(1)}, bf16[6...) custom-call(s32[1,16]{1,0:T(1,128)} %covered_hbm.1, ...), custom_call_target="tpu_custom_call" | custom-call | flops 9830400 | bytes 1179648 | tf_op jit(solution)/shard_map/local/pallas_call | solution.py:547
  7.6 0.0 collective-permute-done.1.tile_y_ref
  7.7 1.1 %collective-permute-done.tile_x_ref = bf16[2,2,64,256]{3,2,1,0:T(8,128)(2,1)S(1)} collective-permute-done((bf16[2,2,64,256]{3,2,1,0:T(8,128)(2,1)}, bf16[2,2,64,256]{3,2,1,0:T(8,128)(2,1)S(1)}, u32[]{:S(2)}, u32[]{:S(2)}) %collective-permute-start) | collective-permute-done | bytes 131104 | tf_op jit(solution)/shard_map/ppermute | solution.py:511
  8.8 0.3 %force.1 = (f32[4,64,256]{2,1,0:T(8,128)S(1)}, bf16[64,256]{1,0:T(8,128)(2,1)S(1)}, bf16[64,256]{1,0:T(8,128)(2,1)S(1)}, bf16[208,256]{1,0:T(8,128)(2,1)S(1)}, bf16[208,256]{1,0:T(8,128)(2,1)S(1)}) custom-call(bf16[64,128]{1,0:T(8,128)(2,1)S(1)} %get-tuple-element.72.side_ref, bf16[2,2,64,256]{3,2,1,0:T(8,128)(2,1)S(1)} %collective-permute-done.tile_x_ref, ...), custom_call_target="tpu_custom_call" | custom-call | tf_op jit(solution)/shard_map/force/pallas_call | solution.py:600
  9.1 0.1 collective-permute-start.2
  9.2 2.5 %collective-permute-start.3 = (bf16[64,256]{1,0:T(8,128)(2,1)S(1)}, bf16[64,256]{1,0:T(8,128)(2,1)S(1)}, u32[]{:S(2)}, u32[]{:S(2)}) collective-permute-start(bf16[64,256]{1,0:T(8,128)(2,1)S(1)} %get-tuple-element.81), channel_id=1, source_target_pairs={{4,8},{12,16},{20,24},{28,0},{8,4},{16,12},{24,20},{0,28},{5,9},{1... | collective-permute-start | bytes 98312 | tf_op jit(solution)/shard_map/ppermute | solution.py:506
  11.7 0.0 collective-permute-done.2.lon_x_ref
  11.7 1.8 %collective-permute-done.3.lon_y_ref = bf16[64,256]{1,0:T(8,128)(2,1)S(1)} collective-permute-done((bf16[64,256]{1,0:T(8,128)(2,1)S(1)}, bf16[64,256]{1,0:T(8,128)(2,1)S(1)}, u32[]{:S(2)}, u32[]{:S(2)}) %collective-permute-start.3) | collective-permute-done | bytes 32800 | tf_op jit(solution)/shard_map/ppermute | solution.py:506
  13.5 0.0 collective-permute-start.5
  13.5 2.5 %collective-permute-start.4 = (bf16[208,256]{1,0:T(8,128)(2,1)S(1)}, bf16[208,256]{1,0:T(8,128)(2,1)S(1)}, u32[]{:S(2)}, u32[]{:S(2)}) collective-permute-start(bf16[208,256]{1,0:T(8,128)(2,1)S(1)} %get-tuple-element.94), channel_id=1, source_target_pairs={{0,1},{4,5},{8,9},{12,13},{16,17},{20,21},{24,25},{28,29},{1,0},{5... | collective-permute-start | bytes 319496 | tf_op jit(solution)/shard_map/ppermute | solution.py:511
  16.0 2.4 %interior.1 = (f32[9,2,3,96,128]{4,3,2,1,0:T(8,128)S(1)}, f32[9,3,3,96,128]{4,3,2,1,0:T(8,128)S(1)}, f32[2,3,96,128]{3,2,1,0:T(8,128)S(1)}, f32[2,3,96,128]{3,2,...) custom-call(f32[9,64,256]{2,1,0:T(8,128)S(1)} %get-tuple-element.74.fields_ref, ...), custom_call_target="tpu_custom_call" | custom-call | flops 7864320 | bytes 4194304 | tf_op jit(solution)/shard_map/interior/pallas_call | solution.py:639
  18.4 0.0 collective-permute-done.5.args_1_
  18.4 0.5 %collective-permute-done.4.args_0_ = bf16[208,256]{1,0:T(8,128)(2,1)S(1)} collective-permute-done((bf16[208,256]{1,0:T(8,128)(2,1)S(1)}, bf16[208,256]{1,0:T(8,128)(2,1)S(1)}, u32[]{:S(2)}, u32[]{:S(2)}) %collective-permute-start.4) | collective-permute-done | bytes 106528 | tf_op jit(solution)/shard_map/ppermute | solution.py:511
  18.9 3.0 %rim.1 = (f32[2,64,256]{2,1,0:T(8,128)}, f32[3,64,256]{2,1,0:T(8,128)}, f32[9,2,3,96,128]{4,3,2,1,0:T(8,128)S(1)}, f32[9,3,3,96,128]{4,3,2,1,0:T(8,128)S(1)}, f3...) custom-call(bf16[208,256]{1,0:T(8,128)(2,1)S(1)} %collective-permute, ...), custom_call_target="tpu_custom_call", output_to_operand_aliasing={{2}: (2, {}), {3}: (3, {}), {4}: (4, {}), {5}: (5, {}), {6}... | custom-call | tf_op jit(solution)/shard_map/rim/pallas_call | solution.py:651
  (2 shorter events, 0.0 us)
Async XLA Ops:
  0.6 7.0 %collective-permute-start.1 = (bf16[2,2,64,256]{3,2,1,0:T(8,128)(2,1)}, bf16[2,2,64,256]{3,2,1,0:T(8,128)(2,1)S(1)}, u32[]{:S(2)}, u32[]{:S(2)}) collective-permute-start(bf16[2,2,64,256]{3,2,1,0:T(8,128)(2,1)} %ocean_hbm.1), channel_id=1, source_target_pairs={{0,4},{4,0},{8,12},{12,8},{16,20},{20,16},{24,28},{28,24},{1,2},{5... | collective-permute-start | bytes 393224 | tf_op jit(solution)/shard_map/ppermute | solution.py:511
  1.2 7.6 %collective-permute-start = (bf16[2,2,64,256]{3,2,1,0:T(8,128)(2,1)}, bf16[2,2,64,256]{3,2,1,0:T(8,128)(2,1)S(1)}, u32[]{:S(2)}, u32[]{:S(2)}) collective-permute-start(bf16[2,2,64,256]{3,2,1,0:T(8,128)(2,1)} %ocean_hbm.1), channel_id=1, source_target_pairs={{0,1},{4,5},{8,9},{12,13},{16,17},{20,21},{24,25},{28,29},{1,0},{5... | collective-permute-start | bytes 393224 | tf_op jit(solution)/shard_map/ppermute | solution.py:511
  9.1 2.6 %collective-permute-start.2 = (bf16[64,256]{1,0:T(8,128)(2,1)S(1)}, bf16[64,256]{1,0:T(8,128)(2,1)S(1)}, u32[]{:S(2)}, u32[]{:S(2)}) collective-permute-start(bf16[64,256]{1,0:T(8,128)(2,1)S(1)} %get-tuple-element.80), channel_id=1, source_target_pairs={{0,4},{8,12},{16,20},{24,28},{4,0},{12,8},{20,16},{28,24},{1,5},{9... | collective-permute-start | bytes 98312 | tf_op jit(solution)/shard_map/ppermute | solution.py:506
  9.2 4.3 %collective-permute-start.3 = (bf16[64,256]{1,0:T(8,128)(2,1)S(1)}, bf16[64,256]{1,0:T(8,128)(2,1)S(1)}, u32[]{:S(2)}, u32[]{:S(2)}) collective-permute-start(bf16[64,256]{1,0:T(8,128)(2,1)S(1)} %get-tuple-element.81), channel_id=1, source_target_pairs={{4,8},{12,16},{20,24},{28,0},{8,4},{16,12},{24,20},{0,28},{5,9},{1... | collective-permute-start | bytes 98312 | tf_op jit(solution)/shard_map/ppermute | solution.py:506
  13.5 4.9 %collective-permute-start.5 = (bf16[208,256]{1,0:T(8,128)(2,1)S(1)}, bf16[208,256]{1,0:T(8,128)(2,1)S(1)}, u32[]{:S(2)}, u32[]{:S(2)}) collective-permute-start(bf16[208,256]{1,0:T(8,128)(2,1)S(1)} %get-tuple-element.93), channel_id=1, source_target_pairs={{0,4},{4,0},{8,12},{12,8},{16,20},{20,16},{24,28},{28,24},{1,2},{5... | collective-permute-start | bytes 319496 | tf_op jit(solution)/shard_map/ppermute | solution.py:511
  13.5 5.4 %collective-permute-start.4 = (bf16[208,256]{1,0:T(8,128)(2,1)S(1)}, bf16[208,256]{1,0:T(8,128)(2,1)S(1)}, u32[]{:S(2)}, u32[]{:S(2)}) collective-permute-start(bf16[208,256]{1,0:T(8,128)(2,1)S(1)} %get-tuple-element.94), channel_id=1, source_target_pairs={{0,1},{4,5},{8,9},{12,13},{16,17},{20,21},{24,25},{28,29},{1,0},{5... | collective-permute-start | bytes 319496 | tf_op jit(solution)/shard_map/ppermute | solution.py:511

commit v5 on v4

--- a/solution.py
+++ b/solution.py
@@ -391,7 +391,33 @@
         )
 
 
-def interior_kernel(margin, fields_ref, force_ref, lon_x_ref, lon_y_ref, *refs):
+def write_rows(refs, out_hbm, stage, sem, margin, begin, height):
+    velocity, stress = refs[:2]
+    steps = velocity.shape[0] - 1
+    for tile in range(stage.shape[2] // LANES):
+        lanes = slice(tile * LANES, (tile + 1) * LANES)
+        for row in range(0, height, 8):
+            to = slice(row, row + 8)
+            at = slice(margin + begin + row, margin + begin + row + 8)
+            p, q, t = (stress[steps, i, tile, at, :] for i in range(3))
+            stage[0, to, lanes] = velocity[steps, 0, tile, at, :]
+            stage[1, to, lanes] = velocity[steps, 1, tile, at, :]
+            stage[2, to, lanes] = (p + q) * 0.5
+            stage[3, to, lanes] = (p - q) * 0.5
+            stage[4, to, lanes] = t * 0.5
+    copies = [
+        pltpu.make_async_copy(
+            stage.at[first : first + hbm.shape[0]], hbm.at[:, pl.ds(begin, height)], sem.at[i]
+        )
+        for i, (first, hbm) in enumerate(zip((0, 2), out_hbm))
+    ]
+    for copy in copies:
+        copy.start()
+    return copies
+
+
+def interior_kernel(margin, fields_ref, force_ref, lon_x_ref, lon_y_ref, *args):
+    refs, out_hbm, (stage, sem) = args[:6], args[6:8], args[8:]
     early, rows, cols = fields_ref.shape
     count = early + force_ref.shape[0]
     windows = refs[2].shape[0]
@@ -416,14 +442,17 @@
 
         lax.fori_loop(0, SUB, subcycle, 0)
 
+    for copy in write_rows(refs, out_hbm, stage, sem, margin, margin, rows - 2 * margin):
+        copy.wait()
+
 
 def rim_kernel(margin, early, count, lat_count, *args):
     lat_x_ref, lat_y_ref = args[:2]
     refs = args[2:8]
-    velocity_ref, stress_ref = args[8:10]
-    velocity, stress = refs[:2]
+    out_hbm = args[16:18]
+    stages, sems = args[18:20], args[20]
     windows = refs[2].shape[0]
-    _, rows, cols = velocity_ref.shape
+    _, rows, cols = out_hbm[0].shape
     own_tiles = cols // LANES
     bottom = margin + rows
     depths = field_depths(margin, windows)
@@ -453,30 +482,21 @@
         east, west = (read(slice(at, at + margin))[:, :packed] for at in (row, row + margin))
         place_sides(refs, early, count, margin, east, west, to)
 
-    def subcycle(step, carry):
+    for step in range(SUB * windows):
         window = step // SUB
         done = 2 * step + 1
         for half, rows_now in ((0, stress_rows), (1, velocity_rows)):
             for first in range(0, margin, 8):
                 rows_now(refs, step, window, done + half + first)
                 rows_now(refs, step, window, bottom - done - half + first)
-        return carry
-
-    steps = SUB * windows
-    lax.fori_loop(0, steps, subcycle, 0)
-
-    for tile in range(own_tiles):
-        lanes = slice(tile * LANES, (tile + 1) * LANES)
-        for row in range(0, rows, 8):
-            at = slice(row, row + 8)
-            own = slice(margin + row, margin + row + 8)
-            velocity_ref[0, at, lanes] = velocity[steps, 0, tile, own, :]
-            velocity_ref[1, at, lanes] = velocity[steps, 1, tile, own, :]
-            p = stress[steps, 0, tile, own, :]
-            q = stress[steps, 1, tile, own, :]
-            stress_ref[0, at, lanes] = (p + q) * 0.5
-            stress_ref[1, at, lanes] = (p - q) * 0.5
-            stress_ref[2, at, lanes] = stress[steps, 2, tile, own, :] * 0.5
+
+    copies = []
+    for number, begin in enumerate((0, rows - margin)):
+        copies += write_rows(
+            refs, out_hbm, stages[number], sems.at[number], margin, begin, margin
+        )
+    for copy in copies:
+        copy.wait()
 
 
 def params():
@@ -636,11 +656,16 @@
         widened(windows),
         widened(windows, 2),
     )
+    outs = (shape(velocity.shape), shape(stress.shape))
     refs = pl.pallas_call(
         functools.partial(interior_kernel, margin),
-        out_shape=domain,
+        out_shape=domain + outs,
         in_specs=[whole] * 4,
-        out_specs=(whole,) * 6,
+        out_specs=(whole,) * 6 + (anywhere,) * 2,
+        scratch_shapes=[
+            pltpu.VMEM((STATE, rows - 2 * margin, cols), jnp.float32),
+            pltpu.SemaphoreType.DMA((2,)),
+        ],
         compiler_params=params(),
         cost_estimate=pl.CostEstimate(
             flops=60 * steps * rows * cols, bytes_accessed=2**22, transcendentals=0
@@ -650,13 +675,18 @@
 
     velocity_out, stress_out = pl.pallas_call(
         functools.partial(rim_kernel, margin, early, count, lax.axis_size("lat")),
-        out_shape=(shape(velocity.shape), shape(stress.shape)) + domain,
-        in_specs=[whole] * 8,
-        out_specs=(whole,) * 8,
-        input_output_aliases={2 + i: 2 + i for i in range(6)},
+        out_shape=domain + outs,
+        in_specs=[whole] * 8 + [anywhere] * 2,
+        out_specs=(whole,) * 6 + (anywhere,) * 2,
+        input_output_aliases={2 + i: i for i in range(8)},
+        scratch_shapes=[
+            pltpu.VMEM((STATE, margin, cols), jnp.float32),
+            pltpu.VMEM((STATE, margin, cols), jnp.float32),
+            pltpu.SemaphoreType.DMA((2, 2)),
+        ],
         compiler_params=params(),
         name="rim",
-    )(lat_x, lat_y, *refs)[:2]
+    )(lat_x, lat_y, *refs)[6:]
     return (velocity_out, stress_out, thick_out)
 
 

time: 22.1 us -> 21.9 us (level)
  waiting for transfers between devices: 3.36 us -> 2.86 us
  Pallas kernels: 8.08 us -> 8.44 us
    pallas_call x1, Pallas kernels: 2.37 us -> 3.06 us  [local(): pl.pallas_call(functools.partial(interior_kernel, margin), out_shape=doma...]
    ppermute x2, waiting for transfers between devices: 1.6 us -> 1.1 us  [lat_exchange(): lax.ppermute(x, axes, lat_swaps(0))]
    pallas_call x1, Pallas kernels: 3.04 us -> 2.7 us  [local(): pl.pallas_call(functools.partial(rim_kernel, margin, early, count, lax.ax...]
  transfers between devices with their start and end apart: 6 -> 6, of which waited for: 3 -> 2; matrix products, arithmetic and copies ran while one was open for 0% -> 0% of each run, Pallas kernels for 22% -> 25%
where the time goes in v5:
time: 21.9 us; the launch traced here: 21.8 us
  starting transfers between devices  9.78 us (45%)
  Pallas kernels  8.44 us (39%)
  waiting for transfers between devices  2.86 us (13%)
  between operations  0.71 us (3%)
    ppermute x2, starting transfers between devices, lat_exchange(): lax.ppermute(x, axes, lat_swaps(0))  6.64 us
    pallas_call x1, Pallas kernels, local(): pl.pallas_call(functools.partial(interior_kernel, margin), out_shape=doma...  3.06 us
    pallas_call x1, Pallas kernels, local(): pl.pallas_call(functools.partial(rim_kernel, margin, early, count, lax.ax...  2.7 us
    ppermute x1, starting transfers between devices, lon_exchange(): lax.ppermute(y, 'lon', lon_swaps(1))  2.54 us
    pallas_call x1, Pallas kernels, local(): pl.pallas_call(functools.partial(local_kernel, margin), out_shape=(shape(...  2.34 us
    ppermute x1, waiting for transfers between devices, lon_exchange(): lax.ppermute(y, 'lon', lon_swaps(1))  1.76 us
    ppermute x2, waiting for transfers between devices, lat_exchange(): lax.ppermute(x, axes, lat_swaps(0))  1.1 us
    ppermute x2, starting transfers between devices, lat_exchange(): lax.ppermute(y, axes, lat_swaps(1))  0.52 us
  transfers between devices with their start and end apart: 6, of which 2 were waited for; matrix products, arithmetic and copies ran while one was open for 0% of the time, Pallas kernels for 25%

profile of v5, /device:TPU:0, one launch (start us, length us, event | category | flops | bytes accessed | tf_op | source)
XLA Modules:
  0.0 21.8 jit_solution(16712682874257179314)
XLA Ops:
  0.6 0.5 %collective-permute-start.1 = (bf16[2,2,64,256]{3,2,1,0:T(8,128)(2,1)}, bf16[2,2,64,256]{3,2,1,0:T(8,128)(2,1)S(1)}, u32[]{:S(2)}, u32[]{:S(2)}) collective-permute-start(bf16[2,2,64,256]{3,2,1,0:T(8,128)(2,1)} %ocean_hbm.1), channel_id=1, source_target_pairs={{0,4},{4,0},{8,12},{12,8},{16,20},{20,16},{24,28},{28,24},{1,2},{5... | collective-permute-start | bytes 393224 | tf_op jit(solution)/shard_map/ppermute | solution.py:531
  1.2 4.1 %collective-permute-start = (bf16[2,2,64,256]{3,2,1,0:T(8,128)(2,1)}, bf16[2,2,64,256]{3,2,1,0:T(8,128)(2,1)S(1)}, u32[]{:S(2)}, u32[]{:S(2)}) collective-permute-start(bf16[2,2,64,256]{3,2,1,0:T(8,128)(2,1)} %ocean_hbm.1), channel_id=1, source_target_pairs={{0,1},{4,5},{8,9},{12,13},{16,17},{20,21},{24,25},{28,29},{1,0},{5... | collective-permute-start | bytes 393224 | tf_op jit(solution)/shard_map/ppermute | solution.py:531
  5.3 2.3 %local.1 = (f32[6,64,256]{2,1,0:T(8,128)}, f32[9,64,256]{2,1,0:T(8,128)S(1)}, f32[2,2,64,256]{3,2,1,0:T(8,128)S(1)}, bf16[64,128]{1,0:T(8,128)(2,1)S(1)}, bf16[6...) custom-call(s32[1,16]{1,0:T(1,128)} %covered_hbm.1, ...), custom_call_target="tpu_custom_call" | custom-call | flops 9830400 | bytes 1179648 | tf_op jit(solution)/shard_map/local/pallas_call | solution.py:567
  7.6 0.0 collective-permute-done.1.tile_y_ref
  7.7 1.1 %collective-permute-done.tile_x_ref = bf16[2,2,64,256]{3,2,1,0:T(8,128)(2,1)S(1)} collective-permute-done((bf16[2,2,64,256]{3,2,1,0:T(8,128)(2,1)}, bf16[2,2,64,256]{3,2,1,0:T(8,128)(2,1)S(1)}, u32[]{:S(2)}, u32[]{:S(2)}) %collective-permute-start) | collective-permute-done | bytes 131104 | tf_op jit(solution)/shard_map/ppermute | solution.py:531
  8.8 0.3 %force.1 = (f32[4,64,256]{2,1,0:T(8,128)S(1)}, bf16[64,256]{1,0:T(8,128)(2,1)S(1)}, bf16[64,256]{1,0:T(8,128)(2,1)S(1)}, bf16[208,256]{1,0:T(8,128)(2,1)S(1)}, bf16[208,256]{1,0:T(8,128)(2,1)S(1)}) custom-call(bf16[64,128]{1,0:T(8,128)(2,1)S(1)} %get-tuple-element.74.side_ref, bf16[2,2,64,256]{3,2,1,0:T(8,128)(2,1)S(1)} %collective-permute-done.tile_x_ref, ...), custom_call_target="tpu_custom_call" | custom-call | tf_op jit(solution)/shard_map/force/pallas_call | solution.py:620
  9.1 0.1 collective-permute-start.2
  9.2 2.5 %collective-permute-start.3 = (bf16[64,256]{1,0:T(8,128)(2,1)S(1)}, bf16[64,256]{1,0:T(8,128)(2,1)S(1)}, u32[]{:S(2)}, u32[]{:S(2)}) collective-permute-start(bf16[64,256]{1,0:T(8,128)(2,1)S(1)} %get-tuple-element.83), channel_id=1, source_target_pairs={{4,8},{12,16},{20,24},{28,0},{8,4},{16,12},{24,20},{0,28},{5,9},{1... | collective-permute-start | bytes 98312 | tf_op jit(solution)/shard_map/ppermute | solution.py:526
  11.7 0.0 collective-permute-done.2.lon_x_ref
  11.7 1.8 %collective-permute-done.3.lon_y_ref = bf16[64,256]{1,0:T(8,128)(2,1)S(1)} collective-permute-done((bf16[64,256]{1,0:T(8,128)(2,1)S(1)}, bf16[64,256]{1,0:T(8,128)(2,1)S(1)}, u32[]{:S(2)}, u32[]{:S(2)}) %collective-permute-start.3) | collective-permute-done | bytes 32800 | tf_op jit(solution)/shard_map/ppermute | solution.py:526
  13.5 0.0 collective-permute-start.5
  13.5 2.5 %collective-permute-start.4 = (bf16[208,256]{1,0:T(8,128)(2,1)S(1)}, bf16[208,256]{1,0:T(8,128)(2,1)S(1)}, u32[]{:S(2)}, u32[]{:S(2)}) collective-permute-start(bf16[208,256]{1,0:T(8,128)(2,1)S(1)} %get-tuple-element.98), channel_id=1, source_target_pairs={{0,1},{4,5},{8,9},{12,13},{16,17},{20,21},{24,25},{28,29},{1,0},{5... | collective-permute-start | bytes 319496 | tf_op jit(solution)/shard_map/ppermute | solution.py:531
  16.0 3.1 %interior.1 = (f32[9,2,3,96,128]{4,3,2,1,0:T(8,128)S(1)}, f32[9,3,3,96,128]{4,3,2,1,0:T(8,128)S(1)}, f32[2,3,96,128]{3,2,1,0:T(8,128)S(1)}, f32[2,3,96,128]{3,2,...) custom-call(f32[9,64,256]{2,1,0:T(8,128)S(1)} %get-tuple-element.76., ...), custom_call_target="tpu_custom_call" | custom-call | flops 7864320 | bytes 4194304 | tf_op jit(solution)/shard_map/interior/pallas_call | solution.py:660
  19.1 0.0 collective-permute-done.5.args_1_
  19.1 0.0 collective-permute-done.4.args_0_
  19.1 2.7 %rim.1 = (f32[9,2,3,96,128]{4,3,2,1,0:T(8,128)S(1)}, f32[9,3,3,96,128]{4,3,2,1,0:T(8,128)S(1)}, f32[2,3,96,128]{3,2,1,0:T(8,128)S(1)}, f32[2,3,96,128]{3,2,1,0:T...) custom-call(bf16[208,256]{1,0:T(8,128)(2,1)S(1)} %collective-permute, ...), custom_call_target="tpu_custom_call", output_to_operand_aliasing={{0}: (2, {}), {1}: (3, {}), {2}: (4, {}), {3}: (5, {}), {4}... | custom-call | tf_op jit(solution)/shard_map/rim/pallas_call | solution.py:676
  (2 shorter events, 0.0 us)
Async XLA Ops:
  0.6 7.0 %collective-permute-start.1 = (bf16[2,2,64,256]{3,2,1,0:T(8,128)(2,1)}, bf16[2,2,64,256]{3,2,1,0:T(8,128)(2,1)S(1)}, u32[]{:S(2)}, u32[]{:S(2)}) collective-permute-start(bf16[2,2,64,256]{3,2,1,0:T(8,128)(2,1)} %ocean_hbm.1), channel_id=1, source_target_pairs={{0,4},{4,0},{8,12},{12,8},{16,20},{20,16},{24,28},{28,24},{1,2},{5... | collective-permute-start | bytes 393224 | tf_op jit(solution)/shard_map/ppermute | solution.py:531
  1.2 7.6 %collective-permute-start = (bf16[2,2,64,256]{3,2,1,0:T(8,128)(2,1)}, bf16[2,2,64,256]{3,2,1,0:T(8,128)(2,1)S(1)}, u32[]{:S(2)}, u32[]{:S(2)}) collective-permute-start(bf16[2,2,64,256]{3,2,1,0:T(8,128)(2,1)} %ocean_hbm.1), channel_id=1, source_target_pairs={{0,1},{4,5},{8,9},{12,13},{16,17},{20,21},{24,25},{28,29},{1,0},{5... | collective-permute-start | bytes 393224 | tf_op jit(solution)/shard_map/ppermute | solution.py:531
  9.1 2.6 %collective-permute-start.2 = (bf16[64,256]{1,0:T(8,128)(2,1)S(1)}, bf16[64,256]{1,0:T(8,128)(2,1)S(1)}, u32[]{:S(2)}, u32[]{:S(2)}) collective-permute-start(bf16[64,256]{1,0:T(8,128)(2,1)S(1)} %get-tuple-element.82), channel_id=1, source_target_pairs={{0,4},{8,12},{16,20},{24,28},{4,0},{12,8},{20,16},{28,24},{1,5},{9... | collective-permute-start | bytes 98312 | tf_op jit(solution)/shard_map/ppermute | solution.py:526
  9.2 4.3 %collective-permute-start.3 = (bf16[64,256]{1,0:T(8,128)(2,1)S(1)}, bf16[64,256]{1,0:T(8,128)(2,1)S(1)}, u32[]{:S(2)}, u32[]{:S(2)}) collective-permute-start(bf16[64,256]{1,0:T(8,128)(2,1)S(1)} %get-tuple-element.83), channel_id=1, source_target_pairs={{4,8},{12,16},{20,24},{28,0},{8,4},{16,12},{24,20},{0,28},{5,9},{1... | collective-permute-start | bytes 98312 | tf_op jit(solution)/shard_map/ppermute | solution.py:526
  13.5 5.6 %collective-permute-start.5 = (bf16[208,256]{1,0:T(8,128)(2,1)S(1)}, bf16[208,256]{1,0:T(8,128)(2,1)S(1)}, u32[]{:S(2)}, u32[]{:S(2)}) collective-permute-start(bf16[208,256]{1,0:T(8,128)(2,1)S(1)} %get-tuple-element.97), channel_id=1, source_target_pairs={{0,4},{4,0},{8,12},{12,8},{16,20},{20,16},{24,28},{28,24},{1,2},{5... | collective-permute-start | bytes 319496 | tf_op jit(solution)/shard_map/ppermute | solution.py:531
  13.5 5.6 %collective-permute-start.4 = (bf16[208,256]{1,0:T(8,128)(2,1)S(1)}, bf16[208,256]{1,0:T(8,128)(2,1)S(1)}, u32[]{:S(2)}, u32[]{:S(2)}) collective-permute-start(bf16[208,256]{1,0:T(8,128)(2,1)S(1)} %get-tuple-element.98), channel_id=1, source_target_pairs={{0,1},{4,5},{8,9},{12,13},{16,17},{20,21},{24,25},{28,29},{1,0},{5... | collective-permute-start | bytes 319496 | tf_op jit(solution)/shard_map/ppermute | solution.py:531

commit v6 on v5

--- a/solution.py
+++ b/solution.py
@@ -244,8 +244,6 @@
     fields_ref,
     lon_x_in,
     lon_y_in,
-    lat_x_in,
-    lat_y_in,
     force_ref,
     lon_x_ref,
     lon_y_ref,
@@ -288,14 +286,26 @@
     def value_of(field, at):
         return force_ref[field - early, at, :]
 
+    for ref, north in ((lat_x_ref, northward), (lat_y_ref, jnp.logical_not(northward))):
+        pack_rows(ref, 0, groups, depths, value_of, north, rows)
+
+
+def corner_kernel(
+    margin, rows, lat_x_in, lat_y_in, lon_x_ref, lon_y_ref, early_x_ref, early_y_ref, lat_x_ref, lat_y_ref
+):
     for old_ref, ref, north in (
-        (lat_x_in, lat_x_ref, northward),
-        (lat_y_in, lat_y_ref, jnp.logical_not(northward)),
+        (lat_x_in, lat_x_ref, even("lat")),
+        (lat_y_in, lat_y_ref, jnp.logical_not(even("lat"))),
     ):
-        row = old_ref.shape[0]
+        row, cols = old_ref.shape
         ref[:row] = old_ref[...]
-        row = pack_rows(ref, row, groups, depths, value_of, north, rows)
-        ref[row:] = jnp.zeros((ref.shape[0] - row, cols), jnp.bfloat16)
+        start = pl.multiple_of(jnp.where(north, rows - margin, 0), GROUP)
+        for lon_ref in (lon_x_ref, lon_y_ref):
+            packed = lon_ref.shape[1]
+            ref[row : row + margin, :packed] = lon_ref[pl.ds(start, margin), :]
+            if packed < cols:
+                ref[row : row + margin, packed:] = jnp.zeros((margin, cols - packed), ref.dtype)
+            row += margin
 
 
 def place(refs, early, field, tile, row, value):
@@ -416,8 +426,36 @@
     return copies
 
 
-def interior_kernel(margin, fields_ref, force_ref, lon_x_ref, lon_y_ref, *args):
-    refs, out_hbm, (stage, sem) = args[:6], args[6:8], args[8:]
+def place_rows(refs, early, fields, margin, rows, lat_count, x_ref, y_ref):
+    depths = field_depths(margin, refs[2].shape[0])
+    me = lax.axis_index("lat")
+    sides = []
+    for ref, north in ((x_ref, even("lat")), (y_ref, jnp.logical_not(even("lat")))):
+        exists = jnp.where(north, me < lat_count - 1, me > 0)
+
+        def read(at, ref=ref, exists=exists):
+            return jnp.where(exists, ref[at].astype(jnp.float32), 0.0)
+
+        row = 0
+        for group in message_groups(fields, depths):
+            height = sum(depths[f] for f in group)
+            value = read(slice(row, row + height))
+            begin = 0
+            for field in group:
+                depth = depths[field]
+                to = pl.multiple_of(jnp.where(north, margin + rows, margin - depth), 8)
+                for tile in range(refs[0].shape[2] - 1):
+                    lanes = slice(tile * LANES, (tile + 1) * LANES)
+                    place(refs, early, field, tile, to, value[begin : begin + depth, lanes])
+                begin += depth
+            row += height
+        sides.append((north, read, row))
+    return sides
+
+
+def interior_kernel(
+    margin, lat_count, fields_ref, force_ref, lon_x_ref, lon_y_ref, early_x_ref, early_y_ref, *refs
+):
     early, rows, cols = fields_ref.shape
     count = early + force_ref.shape[0]
     windows = refs[2].shape[0]
@@ -428,6 +466,7 @@
             place(refs, early, field, tile, margin, own)
     lon_x, lon_y = lon_x_ref[...].astype(jnp.float32), lon_y_ref[...].astype(jnp.float32)
     place_sides(refs, early, count, margin, lon_x, lon_y, margin)
+    place_rows(refs, early, range(early), margin, rows, lat_count, early_x_ref, early_y_ref)
     for window in range(windows):
         lost = 2 * SUB * window
         row_list = range(margin + lost, margin + rows - lost, 8)
@@ -442,42 +481,22 @@
 
         lax.fori_loop(0, SUB, subcycle, 0)
 
-    for copy in write_rows(refs, out_hbm, stage, sem, margin, margin, rows - 2 * margin):
-        copy.wait()
-
 
 def rim_kernel(margin, early, count, lat_count, *args):
     lat_x_ref, lat_y_ref = args[:2]
     refs = args[2:8]
-    out_hbm = args[16:18]
-    stages, sems = args[18:20], args[20]
+    out_hbm = args[8:10]
+    stages, sems = args[16:19], args[19]
     windows = refs[2].shape[0]
     _, rows, cols = out_hbm[0].shape
-    own_tiles = cols // LANES
+    inner = rows - 2 * margin
+    copies = write_rows(refs, out_hbm, stages[2], sems.at[2], margin, margin, inner)
     bottom = margin + rows
-    depths = field_depths(margin, windows)
-    groups = message_groups(range(early), depths) + message_groups(range(early, count), depths)
     packed = -(-count // (LANES // margin)) * LANES
-    me = lax.axis_index("lat")
-    for ref, north in ((lat_x_ref, even("lat")), (lat_y_ref, jnp.logical_not(even("lat")))):
-        exists = jnp.where(north, me < lat_count - 1, me > 0)
-
-        def read(at):
-            return jnp.where(exists, ref[at].astype(jnp.float32), 0.0)
-
-        row = 0
-        for group in groups:
-            height = sum(depths[f] for f in group)
-            value = read(slice(row, row + height))
-            begin = 0
-            for field in group:
-                depth = depths[field]
-                to = pl.multiple_of(jnp.where(north, bottom, margin - depth), 8)
-                for tile in range(own_tiles):
-                    lanes = slice(tile * LANES, (tile + 1) * LANES)
-                    place(refs, early, field, tile, to, value[begin : begin + depth, lanes])
-                begin += depth
-            row += height
+    late = range(early, count)
+    for north, read, row in place_rows(
+        refs, early, late, margin, rows, lat_count, lat_x_ref, lat_y_ref
+    ):
         to = pl.multiple_of(jnp.where(north, bottom, 0), 8)
         east, west = (read(slice(at, at + margin))[:, :packed] for at in (row, row + margin))
         place_sides(refs, early, count, margin, east, west, to)
@@ -490,7 +509,6 @@
                 rows_now(refs, step, window, done + half + first)
                 rows_now(refs, step, window, bottom - done - half + first)
 
-    copies = []
     for number, begin in enumerate((0, rows - margin)):
         copies += write_rows(
             refs, out_hbm, stages[number], sems.at[number], margin, begin, margin
@@ -556,7 +574,7 @@
     packed = -(-count // (LANES // margin)) * LANES
     depths = field_depths(margin, windows)
     early_rows = sum(depths[:early])
-    message_rows = sum(depths)
+    late_rows = sum(depths[early:])
     bf16 = jnp.bfloat16
 
     tile_x, tile_y = lat_exchange(ocean_current, ocean_current)
@@ -617,30 +635,34 @@
         )
     )
 
+    early_x, early_y = lat_exchange(lat_x, lat_y)
     force, lon_x, lon_y, lat_x, lat_y = pl.pallas_call(
         functools.partial(force_kernel, margin, early),
         out_shape=(
             shape((2 * windows, rows, cols)),
             shape((rows, packed), bf16),
             shape((rows, packed), bf16),
-            shape((message_rows + 2 * margin, cols), bf16),
-            shape((message_rows + 2 * margin, cols), bf16),
+            shape((late_rows, cols), bf16),
+            shape((late_rows, cols), bf16),
         ),
-        in_specs=[whole] * 9,
+        in_specs=[whole] * 7,
         out_specs=(whole,) * 5,
         compiler_params=params(),
+        cost_estimate=pl.CostEstimate(flops=1, bytes_accessed=1, transcendentals=0),
         name="force",
-    )(side, tile_x, tile_y, current, fields, lon_x, lon_y, lat_x, lat_y)
+    )(side, tile_x, tile_y, current, fields, lon_x, lon_y)
 
     lon_x, lon_y = lon_exchange(lon_x, lon_y)
-    north_end = rows - margin
-    start_x = jnp.where(even("lat"), north_end, 0)
-    for number, part in enumerate((lon_x, lon_y)):
-        at = message_rows + number * margin
-        corner_x = lax.dynamic_slice_in_dim(part, start_x, margin, 0)
-        corner_y = lax.dynamic_slice_in_dim(part, north_end - start_x, margin, 0)
-        lat_x = lat_x.at[at : at + margin, :packed].set(corner_x)
-        lat_y = lat_y.at[at : at + margin, :packed].set(corner_y)
+    message = shape((late_rows + 2 * margin, cols), bf16)
+    lat_x, lat_y = pl.pallas_call(
+        functools.partial(corner_kernel, margin, rows),
+        out_shape=(message, message),
+        in_specs=[whole] * 6,
+        out_specs=(whole,) * 2,
+        compiler_params=params(),
+        cost_estimate=pl.CostEstimate(flops=1, bytes_accessed=1, transcendentals=0),
+        name="corner",
+    )(lat_x, lat_y, lon_x, lon_y, early_x, early_y)
     lat_x, lat_y = lat_exchange(lat_x, lat_y)
 
     steps = SUB * windows
@@ -658,35 +680,32 @@
     )
     outs = (shape(velocity.shape), shape(stress.shape))
     refs = pl.pallas_call(
-        functools.partial(interior_kernel, margin),
-        out_shape=domain + outs,
-        in_specs=[whole] * 4,
-        out_specs=(whole,) * 6 + (anywhere,) * 2,
-        scratch_shapes=[
-            pltpu.VMEM((STATE, rows - 2 * margin, cols), jnp.float32),
-            pltpu.SemaphoreType.DMA((2,)),
-        ],
+        functools.partial(interior_kernel, margin, lax.axis_size("lat")),
+        out_shape=domain,
+        in_specs=[whole] * 6,
+        out_specs=(whole,) * 6,
         compiler_params=params(),
         cost_estimate=pl.CostEstimate(
             flops=60 * steps * rows * cols, bytes_accessed=2**22, transcendentals=0
         ),
         name="interior",
-    )(fields, force, lon_x, lon_y)
+    )(fields, force, lon_x, lon_y, early_x, early_y)
 
     velocity_out, stress_out = pl.pallas_call(
         functools.partial(rim_kernel, margin, early, count, lax.axis_size("lat")),
-        out_shape=domain + outs,
-        in_specs=[whole] * 8 + [anywhere] * 2,
-        out_specs=(whole,) * 6 + (anywhere,) * 2,
-        input_output_aliases={2 + i: i for i in range(8)},
+        out_shape=(shape(velocity.shape), shape(stress.shape)) + domain,
+        in_specs=[whole] * 8,
+        out_specs=(anywhere,) * 2 + (whole,) * 6,
+        input_output_aliases={2 + i: 2 + i for i in range(6)},
         scratch_shapes=[
             pltpu.VMEM((STATE, margin, cols), jnp.float32),
             pltpu.VMEM((STATE, margin, cols), jnp.float32),
-            pltpu.SemaphoreType.DMA((2, 2)),
+            pltpu.VMEM((STATE, rows - 2 * margin, cols), jnp.float32),
+            pltpu.SemaphoreType.DMA((3, 2)),
         ],
         compiler_params=params(),
         name="rim",
-    )(lat_x, lat_y, *refs)[6:]
+    )(lat_x, lat_y, *refs)[:2]
     return (velocity_out, stress_out, thick_out)
 
 

time: 21.9 us -> 21.3 us (0.973)
  Pallas kernels: 8.44 us -> 7.83 us
    pallas_call x1 -> x2, Pallas kernels: 3.06 us -> 2.44 us  [the longest x1 2.43 us: local(): pl.pallas_call(functools.partial(interior_kernel, margin, lax.axis_size('...]
    ppermute x1, waiting for transfers between devices: 1.76 us -> 1.5 us  [lon_exchange(): lax.ppermute(y, 'lon', lon_swaps(1))]
    ppermute x2 -> x3, waiting for transfers between devices: 1.1 us -> 1.19 us  [lat_exchange(): lax.ppermute(x, axes, lat_swaps(0))]
    ppermute x2 -> x3, starting transfers between devices: 0.52 us -> 0.59 us  [lat_exchange(): lax.ppermute(y, axes, lat_swaps(1))]
    ppermute x2 -> x3, starting transfers between devices: 6.64 us -> 6.65 us  [lat_exchange(): lax.ppermute(x, axes, lat_swaps(0))]
  transfers between devices with their start and end apart: 6 -> 8, of which waited for: 2 -> 3; matrix products, arithmetic and copies ran while one was open for 0% -> 0% of each run, Pallas kernels for 25% -> 24%
where the time goes in v6:
time: 21.3 us; the launch traced here: 21.1 us
  starting transfers between devices  9.87 us (46%)
  Pallas kernels  7.83 us (37%)
  waiting for transfers between devices  2.69 us (13%)
  between operations  0.71 us (3%)
    ppermute x3, starting transfers between devices, lat_exchange(): lax.ppermute(x, axes, lat_swaps(0))  6.65 us
    pallas_call x1, Pallas kernels, local(): pl.pallas_call(functools.partial(rim_kernel, margin, early, count, lax.ax...  2.71 us
    ppermute x1, starting transfers between devices, lon_exchange(): lax.ppermute(y, 'lon', lon_swaps(1))  2.56 us
    pallas_call x1, Pallas kernels, local(): pl.pallas_call(functools.partial(interior_kernel, margin, lax.axis_size('...  2.43 us
    pallas_call x1, Pallas kernels, local(): pl.pallas_call(functools.partial(local_kernel, margin), out_shape=(shape(...  2.34 us
    ppermute x1, waiting for transfers between devices, lon_exchange(): lax.ppermute(y, 'lon', lon_swaps(1))  1.5 us
    ppermute x3, waiting for transfers between devices, lat_exchange(): lax.ppermute(x, axes, lat_swaps(0))  1.19 us
    ppermute x3, starting transfers between devices, lat_exchange(): lax.ppermute(y, axes, lat_swaps(1))  0.59 us
  transfers between devices with their start and end apart: 8, of which 3 were waited for; matrix products, arithmetic and copies ran while one was open for 0% of the time, Pallas kernels for 24%

profile of v6, /device:TPU:0, one launch (start us, length us, event | category | flops | bytes accessed | tf_op | source)
XLA Modules:
  0.0 21.1 jit_solution(8018910058943157428)
XLA Ops:
  0.6 0.5 %collective-permute-start.1 = (bf16[2,2,64,256]{3,2,1,0:T(8,128)(2,1)}, bf16[2,2,64,256]{3,2,1,0:T(8,128)(2,1)S(1)}, u32[]{:S(2)}, u32[]{:S(2)}) collective-permute-start(bf16[2,2,64,256]{3,2,1,0:T(8,128)(2,1)} %ocean_hbm.1), channel_id=1, source_target_pairs={{0,4},{4,0},{8,12},{12,8},{16,20},{20,16},{24,28},{28,24},{1,2},{5... | collective-permute-start | bytes 393224 | tf_op jit(solution)/shard_map/ppermute | solution.py:549
  1.2 4.1 %collective-permute-start = (bf16[2,2,64,256]{3,2,1,0:T(8,128)(2,1)}, bf16[2,2,64,256]{3,2,1,0:T(8,128)(2,1)S(1)}, u32[]{:S(2)}, u32[]{:S(2)}) collective-permute-start(bf16[2,2,64,256]{3,2,1,0:T(8,128)(2,1)} %ocean_hbm.1), channel_id=1, source_target_pairs={{0,1},{4,5},{8,9},{12,13},{16,17},{20,21},{24,25},{28,29},{1,0},{5... | collective-permute-start | bytes 393224 | tf_op jit(solution)/shard_map/ppermute | solution.py:549
  5.3 2.3 %local.1 = (f32[6,64,256]{2,1,0:T(8,128)}, f32[9,64,256]{2,1,0:T(8,128)S(1)}, f32[2,2,64,256]{3,2,1,0:T(8,128)S(1)}, bf16[64,128]{1,0:T(8,128)(2,1)S(1)}, bf16[6...) custom-call(s32[1,16]{1,0:T(1,128)} %covered_hbm.1, ...), custom_call_target="tpu_custom_call" | custom-call | flops 9830400 | bytes 1179648 | tf_op jit(solution)/shard_map/local/pallas_call | solution.py:585
  7.6 0.1 collective-permute-start.4
  7.7 0.1 collective-permute-start.5
  7.8 0.0 collective-permute-done.1.tile_y_ref
  7.8 0.9 %collective-permute-done.tile_x_ref = bf16[2,2,64,256]{3,2,1,0:T(8,128)(2,1)S(1)} collective-permute-done((bf16[2,2,64,256]{3,2,1,0:T(8,128)(2,1)}, bf16[2,2,64,256]{3,2,1,0:T(8,128)(2,1)S(1)}, u32[]{:S(2)}, u32[]{:S(2)}) %collective-permute-start) | collective-permute-done | bytes 131104 | tf_op jit(solution)/shard_map/ppermute | solution.py:549
  8.8 0.3 %force.1 = (f32[4,64,256]{2,1,0:T(8,128)S(1)}, bf16[64,256]{1,0:T(8,128)(2,1)S(1)}, bf16[64,256]{1,0:T(8,128)(2,1)S(1)}, bf16[48,256]{1,0:T(8,128)(2,1)S(1)}, bf16[48,256]{1,0:T(8,128)(2,1)S(1)}) custom-call(bf16[64,128]{1,0:T(8,128)(2,1)S(1)} %get-tuple-element.26.side_ref, bf16[2,2,64,256]{3,2,1,0:T(8,128)(2,1)S(1)} %collective-permute-done.tile_x_ref, ...), custom_call_target="tpu_custom_call" | custom-call | flops 1 | bytes 1 | tf_op jit(solution)/shard_map/force/pallas_call | solution.py:639
  9.1 0.1 collective-permute-start.2
  9.2 2.6 %collective-permute-start.3 = (bf16[64,256]{1,0:T(8,128)(2,1)S(1)}, bf16[64,256]{1,0:T(8,128)(2,1)S(1)}, u32[]{:S(2)}, u32[]{:S(2)}) collective-permute-start(bf16[64,256]{1,0:T(8,128)(2,1)S(1)} %get-tuple-element.34), channel_id=1, source_target_pairs={{4,8},{12,16},{20,24},{28,0},{8,4},{16,12},{24,20},{0,28},{5,9},{1... | collective-permute-start | bytes 98312 | tf_op jit(solution)/shard_map/ppermute | solution.py:544
  11.7 0.2 %collective-permute-done.4.early_x_ref = bf16[128,256]{1,0:T(8,128)(2,1)S(1)} collective-permute-done((bf16[128,256]{1,0:T(8,128)(2,1)S(1)}, bf16[128,256]{1,0:T(8,128)(2,1)S(1)}, u32[]{:S(2)}, u32[]{:S(2)}) %collective-permute-start.4) | collective-permute-done | bytes 65568 | tf_op jit(solution)/shard_map/ppermute | solution.py:549
  12.0 0.0 collective-permute-done.5.early_y_ref
  12.0 0.0 collective-permute-done.2.lon_x_ref
  12.0 1.5 %collective-permute-done.3.lon_y_ref = bf16[64,256]{1,0:T(8,128)(2,1)S(1)} collective-permute-done((bf16[64,256]{1,0:T(8,128)(2,1)S(1)}, bf16[64,256]{1,0:T(8,128)(2,1)S(1)}, u32[]{:S(2)}, u32[]{:S(2)}) %collective-permute-start.3) | collective-permute-done | bytes 32800 | tf_op jit(solution)/shard_map/ppermute | solution.py:544
  13.5 2.4 %collective-permute-start.6 = (bf16[80,256]{1,0:T(8,128)(2,1)S(1)}, bf16[80,256]{1,0:T(8,128)(2,1)S(1)}, u32[]{:S(2)}, u32[]{:S(2)}) collective-permute-start(bf16[80,256]{1,0:T(8,128)(2,1)S(1)} %get-tuple-element.37), channel_id=1, source_target_pairs={{0,1},{4,5},{8,9},{12,13},{16,17},{20,21},{24,25},{28,29},{1,0},{5... | collective-permute-start | bytes 122888 | tf_op jit(solution)/shard_map/ppermute | solution.py:549
  15.9 0.0 collective-permute-start.7
  15.9 2.4 %interior.1 = (f32[9,2,3,96,128]{4,3,2,1,0:T(8,128)S(1)}, f32[9,3,3,96,128]{4,3,2,1,0:T(8,128)S(1)}, f32[2,3,96,128]{3,2,1,0:T(8,128)S(1)}, f32[2,3,96,128]{3,2,...) custom-call(f32[9,64,256]{2,1,0:T(8,128)S(1)} %get-tuple-element.28.fields_ref, ...), custom_call_target="tpu_custom_call" | custom-call | flops 7864320 | bytes 4194304 | tf_op jit(solution)/shard_map/interior/pallas_call | solution.py:682
  18.4 0.0 collective-permute-done.6.args_0_
  18.4 0.0 collective-permute-done.7.args_1_
  18.4 2.7 %rim.1 = (f32[2,64,256]{2,1,0:T(8,128)}, f32[3,64,256]{2,1,0:T(8,128)}, f32[9,2,3,96,128]{4,3,2,1,0:T(8,128)S(1)}, f32[9,3,3,96,128]{4,3,2,1,0:T(8,128)S(1)}, f3...) custom-call(bf16[80,256]{1,0:T(8,128)(2,1)S(1)} %collective-permute-, ...), custom_call_target="tpu_custom_call", output_to_operand_aliasing={{2}: (2, {}), {3}: (3, {}), {4}: (4, {}), {5}: (5, {}), {6}... | custom-call | tf_op jit(solution)/shard_map/rim/pallas_call | solution.py:694
  (1 shorter events, 0.0 us)
Async XLA Ops:
  0.6 7.2 %collective-permute-start.1 = (bf16[2,2,64,256]{3,2,1,0:T(8,128)(2,1)}, bf16[2,2,64,256]{3,2,1,0:T(8,128)(2,1)S(1)}, u32[]{:S(2)}, u32[]{:S(2)}) collective-permute-start(bf16[2,2,64,256]{3,2,1,0:T(8,128)(2,1)} %ocean_hbm.1), channel_id=1, source_target_pairs={{0,4},{4,0},{8,12},{12,8},{16,20},{20,16},{24,28},{28,24},{1,2},{5... | collective-permute-start | bytes 393224 | tf_op jit(solution)/shard_map/ppermute | solution.py:549
  1.2 7.6 %collective-permute-start = (bf16[2,2,64,256]{3,2,1,0:T(8,128)(2,1)}, bf16[2,2,64,256]{3,2,1,0:T(8,128)(2,1)S(1)}, u32[]{:S(2)}, u32[]{:S(2)}) collective-permute-start(bf16[2,2,64,256]{3,2,1,0:T(8,128)(2,1)} %ocean_hbm.1), channel_id=1, source_target_pairs={{0,1},{4,5},{8,9},{12,13},{16,17},{20,21},{24,25},{28,29},{1,0},{5... | collective-permute-start | bytes 393224 | tf_op jit(solution)/shard_map/ppermute | solution.py:549
  7.6 4.3 %collective-permute-start.4 = (bf16[128,256]{1,0:T(8,128)(2,1)S(1)}, bf16[128,256]{1,0:T(8,128)(2,1)S(1)}, u32[]{:S(2)}, u32[]{:S(2)}) collective-permute-start(bf16[128,256]{1,0:T(8,128)(2,1)S(1)} %get-tuple-element.35), channel_id=1, source_target_pairs={{0,1},{4,5},{8,9},{12,13},{16,17},{20,21},{24,25},{28,29},{1,0},{5... | collective-permute-start | bytes 196616 | tf_op jit(solution)/shard_map/ppermute | solution.py:549
  7.7 4.3 %collective-permute-start.5 = (bf16[128,256]{1,0:T(8,128)(2,1)S(1)}, bf16[128,256]{1,0:T(8,128)(2,1)S(1)}, u32[]{:S(2)}, u32[]{:S(2)}) collective-permute-start(bf16[128,256]{1,0:T(8,128)(2,1)S(1)} %get-tuple-element.36), channel_id=1, source_target_pairs={{0,4},{4,0},{8,12},{12,8},{16,20},{20,16},{24,28},{28,24},{1,2},{5... | collective-permute-start | bytes 196616 | tf_op jit(solution)/shard_map/ppermute | solution.py:549
  9.1 2.9 %collective-permute-start.2 = (bf16[64,256]{1,0:T(8,128)(2,1)S(1)}, bf16[64,256]{1,0:T(8,128)(2,1)S(1)}, u32[]{:S(2)}, u32[]{:S(2)}) collective-permute-start(bf16[64,256]{1,0:T(8,128)(2,1)S(1)} %get-tuple-element.33), channel_id=1, source_target_pairs={{0,4},{8,12},{16,20},{24,28},{4,0},{12,8},{20,16},{28,24},{1,5},{9... | collective-permute-start | bytes 98312 | tf_op jit(solution)/shard_map/ppermute | solution.py:544
  9.2 4.3 %collective-permute-start.3 = (bf16[64,256]{1,0:T(8,128)(2,1)S(1)}, bf16[64,256]{1,0:T(8,128)(2,1)S(1)}, u32[]{:S(2)}, u32[]{:S(2)}) collective-permute-start(bf16[64,256]{1,0:T(8,128)(2,1)S(1)} %get-tuple-element.34), channel_id=1, source_target_pairs={{4,8},{12,16},{20,24},{28,0},{8,4},{16,12},{24,20},{0,28},{5,9},{1... | collective-permute-start | bytes 98312 | tf_op jit(solution)/shard_map/ppermute | solution.py:544
  13.5 4.9 %collective-permute-start.6 = (bf16[80,256]{1,0:T(8,128)(2,1)S(1)}, bf16[80,256]{1,0:T(8,128)(2,1)S(1)}, u32[]{:S(2)}, u32[]{:S(2)}) collective-permute-start(bf16[80,256]{1,0:T(8,128)(2,1)S(1)} %get-tuple-element.37), channel_id=1, source_target_pairs={{0,1},{4,5},{8,9},{12,13},{16,17},{20,21},{24,25},{28,29},{1,0},{5... | collective-permute-start | bytes 122888 | tf_op jit(solution)/shard_map/ppermute | solution.py:549
  15.9 2.5 %collective-permute-start.7 = (bf16[80,256]{1,0:T(8,128)(2,1)S(1)}, bf16[80,256]{1,0:T(8,128)(2,1)S(1)}, u32[]{:S(2)}, u32[]{:S(2)}) collective-permute-start(bf16[80,256]{1,0:T(8,128)(2,1)S(1)} %get-tuple-element.38), channel_id=1, source_target_pairs={{0,4},{4,0},{8,12},{12,8},{16,20},{20,16},{24,28},{28,24},{1,2},{5... | collective-permute-start | bytes 122888 | tf_op jit(solution)/shard_map/ppermute | solution.py:549

commit v7 on v6

--- a/solution.py
+++ b/solution.py
@@ -401,29 +401,27 @@
         )
 
 
-def write_rows(refs, out_hbm, stage, sem, margin, begin, height):
-    velocity, stress = refs[:2]
-    steps = velocity.shape[0] - 1
+def write_rows(refs, out_hbm, stage, sem, margin, begin, height, which):
+    values = refs[which]
+    last = values.shape[0] - 1
+    first = 2 * which
     for tile in range(stage.shape[2] // LANES):
         lanes = slice(tile * LANES, (tile + 1) * LANES)
         for row in range(0, height, 8):
             to = slice(row, row + 8)
             at = slice(margin + begin + row, margin + begin + row + 8)
-            p, q, t = (stress[steps, i, tile, at, :] for i in range(3))
-            stage[0, to, lanes] = velocity[steps, 0, tile, at, :]
-            stage[1, to, lanes] = velocity[steps, 1, tile, at, :]
-            stage[2, to, lanes] = (p + q) * 0.5
-            stage[3, to, lanes] = (p - q) * 0.5
-            stage[4, to, lanes] = t * 0.5
-    copies = [
-        pltpu.make_async_copy(
-            stage.at[first : first + hbm.shape[0]], hbm.at[:, pl.ds(begin, height)], sem.at[i]
-        )
-        for i, (first, hbm) in enumerate(zip((0, 2), out_hbm))
-    ]
-    for copy in copies:
-        copy.start()
-    return copies
+            now = [values[last, i, tile, at, :] for i in range(values.shape[1])]
+            if which:
+                now = [(now[0] + now[1]) * 0.5, (now[0] - now[1]) * 0.5, now[2] * 0.5]
+            for i, value in enumerate(now):
+                stage[first + i, to, lanes] = value
+    copy = pltpu.make_async_copy(
+        stage.at[first : first + values.shape[1]],
+        out_hbm[which].at[:, pl.ds(begin, height)],
+        sem.at[which],
+    )
+    copy.start()
+    return [copy]
 
 
 def place_rows(refs, early, fields, margin, rows, lat_count, x_ref, y_ref):
@@ -469,10 +467,13 @@
     place_rows(refs, early, range(early), margin, rows, lat_count, early_x_ref, early_y_ref)
     for window in range(windows):
         lost = 2 * SUB * window
-        row_list = range(margin + lost, margin + rows - lost, 8)
 
         def subcycle(number, carry):
             step = window * SUB + number
+            base = step // (SUB * windows) * 8
+            row_list = [
+                pl.multiple_of(base + row, 8) for row in range(margin + lost, margin + rows - lost, 8)
+            ]
             for row in row_list:
                 stress_rows(refs, step, window, row)
             for row in row_list:
@@ -490,7 +491,9 @@
     windows = refs[2].shape[0]
     _, rows, cols = out_hbm[0].shape
     inner = rows - 2 * margin
-    copies = write_rows(refs, out_hbm, stages[2], sems.at[2], margin, margin, inner)
+    copies = []
+    for which in range(2):
+        copies += write_rows(refs, out_hbm, stages[2], sems.at[2], margin, margin, inner, which)
     bottom = margin + rows
     packed = -(-count // (LANES // margin)) * LANES
     late = range(early, count)
@@ -501,18 +504,31 @@
         east, west = (read(slice(at, at + margin))[:, :packed] for at in (row, row + margin))
         place_sides(refs, early, count, margin, east, west, to)
 
-    for step in range(SUB * windows):
-        window = step // SUB
-        done = 2 * step + 1
-        for half, rows_now in ((0, stress_rows), (1, velocity_rows)):
-            for first in range(0, margin, 8):
-                rows_now(refs, step, window, done + half + first)
-                rows_now(refs, step, window, bottom - done - half + first)
-
-    for number, begin in enumerate((0, rows - margin)):
-        copies += write_rows(
-            refs, out_hbm, stages[number], sems.at[number], margin, begin, margin
-        )
+    def half_step(step, half):
+        done = 2 * step + 1 + half
+        rows_now = velocity_rows if half else stress_rows
+        for first in range(0, margin, 8):
+            rows_now(refs, step, step // SUB, done + first)
+            rows_now(refs, step, step // SUB, bottom - done + first)
+
+    def subcycles(number, carry):
+        for step in (2 * number, 2 * number + 1):
+            half_step(step, 0)
+            half_step(step, 1)
+        return carry
+
+    last = SUB * windows - 1
+    lax.fori_loop(0, last // 2, subcycles, 0)
+    for step in range(last // 2 * 2, last):
+        half_step(step, 0)
+        half_step(step, 1)
+    half_step(last, 0)
+    ends = list(enumerate((0, rows - margin)))
+    for number, begin in ends:
+        copies += write_rows(refs, out_hbm, stages[number], sems.at[number], margin, begin, margin, 1)
+    half_step(last, 1)
+    for number, begin in ends:
+        copies += write_rows(refs, out_hbm, stages[number], sems.at[number], margin, begin, margin, 0)
     for copy in copies:
         copy.wait()
 

time: 21.3 us -> 21.8 us (1.023)
  Pallas kernels: 7.83 us -> 8.3 us
    pallas_call x1, Pallas kernels: 2.71 us -> 2.96 us  [local(): pl.pallas_call(functools.partial(rim_kernel, margin, early, count, lax.ax...]
    pallas_call x1, Pallas kernels: 2.43 us -> 2.66 us  [local(): pl.pallas_call(functools.partial(interior_kernel, margin, lax.axis_size('...]
  transfers between devices with their start and end apart: 8 -> 8, of which waited for: 3 -> 3; matrix products, arithmetic and copies ran while one was open for 0% -> 0% of each run, Pallas kernels for 24% -> 25%
where the time goes in v7:
time: 21.8 us; the launch traced here: 21.6 us
  starting transfers between devices  9.87 us (45%)
  Pallas kernels  8.3 us (38%)
  waiting for transfers between devices  2.69 us (12%)
  between operations  0.71 us (3%)
    ppermute x3, starting transfers between devices, lat_exchange(): lax.ppermute(x, axes, lat_swaps(0))  6.65 us
    pallas_call x1, Pallas kernels, local(): pl.pallas_call(functools.partial(rim_kernel, margin, early, count, lax.ax...  2.96 us
    pallas_call x1, Pallas kernels, local(): pl.pallas_call(functools.partial(interior_kernel, margin, lax.axis_size('...  2.66 us
    ppermute x1, starting transfers between devices, lon_exchange(): lax.ppermute(y, 'lon', lon_swaps(1))  2.56 us
    pallas_call x1, Pallas kernels, local(): pl.pallas_call(functools.partial(local_kernel, margin), out_shape=(shape(...  2.34 us
    ppermute x1, waiting for transfers between devices, lon_exchange(): lax.ppermute(y, 'lon', lon_swaps(1))  1.5 us
    ppermute x3, waiting for transfers between devices, lat_exchange(): lax.ppermute(x, axes, lat_swaps(0))  1.19 us
    ppermute x3, starting transfers between devices, lat_exchange(): lax.ppermute(y, axes, lat_swaps(1))  0.59 us
  transfers between devices with their start and end apart: 8, of which 3 were waited for; matrix products, arithmetic and copies ran while one was open for 0% of the time, Pallas kernels for 25%

profile of v7, /device:TPU:0, one launch (start us, length us, event | category | flops | bytes accessed | tf_op | source)
XLA Modules:
  0.0 21.6 jit_solution(13440249564473991190)
XLA Ops:
  0.6 0.5 %collective-permute-start.1 = (bf16[2,2,64,256]{3,2,1,0:T(8,128)(2,1)}, bf16[2,2,64,256]{3,2,1,0:T(8,128)(2,1)S(1)}, u32[]{:S(2)}, u32[]{:S(2)}) collective-permute-start(bf16[2,2,64,256]{3,2,1,0:T(8,128)(2,1)} %ocean_hbm.1), channel_id=1, source_target_pairs={{0,4},{4,0},{8,12},{12,8},{16,20},{20,16},{24,28},{28,24},{1,2},{5... | collective-permute-start | bytes 393224 | tf_op jit(solution)/shard_map/ppermute | solution.py:565
  1.2 4.1 %collective-permute-start = (bf16[2,2,64,256]{3,2,1,0:T(8,128)(2,1)}, bf16[2,2,64,256]{3,2,1,0:T(8,128)(2,1)S(1)}, u32[]{:S(2)}, u32[]{:S(2)}) collective-permute-start(bf16[2,2,64,256]{3,2,1,0:T(8,128)(2,1)} %ocean_hbm.1), channel_id=1, source_target_pairs={{0,1},{4,5},{8,9},{12,13},{16,17},{20,21},{24,25},{28,29},{1,0},{5... | collective-permute-start | bytes 393224 | tf_op jit(solution)/shard_map/ppermute | solution.py:565
  5.3 2.3 %local.1 = (f32[6,64,256]{2,1,0:T(8,128)}, f32[9,64,256]{2,1,0:T(8,128)S(1)}, f32[2,2,64,256]{3,2,1,0:T(8,128)S(1)}, bf16[64,128]{1,0:T(8,128)(2,1)S(1)}, bf16[6...) custom-call(s32[1,16]{1,0:T(1,128)} %covered_hbm.1, ...), custom_call_target="tpu_custom_call" | custom-call | flops 9830400 | bytes 1179648 | tf_op jit(solution)/shard_map/local/pallas_call | solution.py:601
  7.6 0.1 collective-permute-start.4
  7.7 0.1 collective-permute-start.5
  7.8 0.0 collective-permute-done.1.tile_y_ref
  7.8 0.9 %collective-permute-done.tile_x_ref = bf16[2,2,64,256]{3,2,1,0:T(8,128)(2,1)S(1)} collective-permute-done((bf16[2,2,64,256]{3,2,1,0:T(8,128)(2,1)}, bf16[2,2,64,256]{3,2,1,0:T(8,128)(2,1)S(1)}, u32[]{:S(2)}, u32[]{:S(2)}) %collective-permute-start) | collective-permute-done | bytes 131104 | tf_op jit(solution)/shard_map/ppermute | solution.py:565
  8.8 0.3 %force.1 = (f32[4,64,256]{2,1,0:T(8,128)S(1)}, bf16[64,256]{1,0:T(8,128)(2,1)S(1)}, bf16[64,256]{1,0:T(8,128)(2,1)S(1)}, bf16[48,256]{1,0:T(8,128)(2,1)S(1)}, bf16[48,256]{1,0:T(8,128)(2,1)S(1)}) custom-call(bf16[64,128]{1,0:T(8,128)(2,1)S(1)} %get-tuple-element.26.side_ref, bf16[2,2,64,256]{3,2,1,0:T(8,128)(2,1)S(1)} %collective-permute-done.tile_x_ref, ...), custom_call_target="tpu_custom_call" | custom-call | flops 1 | bytes 1 | tf_op jit(solution)/shard_map/force/pallas_call | solution.py:655
  9.1 0.1 collective-permute-start.2
  9.2 2.6 %collective-permute-start.3 = (bf16[64,256]{1,0:T(8,128)(2,1)S(1)}, bf16[64,256]{1,0:T(8,128)(2,1)S(1)}, u32[]{:S(2)}, u32[]{:S(2)}) collective-permute-start(bf16[64,256]{1,0:T(8,128)(2,1)S(1)} %get-tuple-element.34), channel_id=1, source_target_pairs={{4,8},{12,16},{20,24},{28,0},{8,4},{16,12},{24,20},{0,28},{5,9},{1... | collective-permute-start | bytes 98312 | tf_op jit(solution)/shard_map/ppermute | solution.py:560
  11.7 0.2 %collective-permute-done.4.early_x_ref = bf16[128,256]{1,0:T(8,128)(2,1)S(1)} collective-permute-done((bf16[128,256]{1,0:T(8,128)(2,1)S(1)}, bf16[128,256]{1,0:T(8,128)(2,1)S(1)}, u32[]{:S(2)}, u32[]{:S(2)}) %collective-permute-start.4) | collective-permute-done | bytes 65568 | tf_op jit(solution)/shard_map/ppermute | solution.py:565
  12.0 0.0 collective-permute-done.5.early_y_ref
  12.0 0.0 collective-permute-done.2.lon_x_ref
  12.0 1.5 %collective-permute-done.3.lon_y_ref = bf16[64,256]{1,0:T(8,128)(2,1)S(1)} collective-permute-done((bf16[64,256]{1,0:T(8,128)(2,1)S(1)}, bf16[64,256]{1,0:T(8,128)(2,1)S(1)}, u32[]{:S(2)}, u32[]{:S(2)}) %collective-permute-start.3) | collective-permute-done | bytes 32800 | tf_op jit(solution)/shard_map/ppermute | solution.py:560
  13.5 2.4 %collective-permute-start.6 = (bf16[80,256]{1,0:T(8,128)(2,1)S(1)}, bf16[80,256]{1,0:T(8,128)(2,1)S(1)}, u32[]{:S(2)}, u32[]{:S(2)}) collective-permute-start(bf16[80,256]{1,0:T(8,128)(2,1)S(1)} %get-tuple-element.37), channel_id=1, source_target_pairs={{0,1},{4,5},{8,9},{12,13},{16,17},{20,21},{24,25},{28,29},{1,0},{5... | collective-permute-start | bytes 122888 | tf_op jit(solution)/shard_map/ppermute | solution.py:565
  15.9 0.0 collective-permute-start.7
  15.9 2.7 %interior.1 = (f32[9,2,3,96,128]{4,3,2,1,0:T(8,128)S(1)}, f32[9,3,3,96,128]{4,3,2,1,0:T(8,128)S(1)}, f32[2,3,96,128]{3,2,1,0:T(8,128)S(1)}, f32[2,3,96,128]{3,2,...) custom-call(f32[9,64,256]{2,1,0:T(8,128)S(1)} %get-tuple-element.28.fields_ref, ...), custom_call_target="tpu_custom_call" | custom-call | flops 7864320 | bytes 4194304 | tf_op jit(solution)/shard_map/interior/pallas_call | solution.py:698
  18.6 0.0 collective-permute-done.6.args_0_
  18.6 0.0 collective-permute-done.7.args_1_
  18.6 3.0 %rim.1 = (f32[2,64,256]{2,1,0:T(8,128)}, f32[3,64,256]{2,1,0:T(8,128)}, f32[9,2,3,96,128]{4,3,2,1,0:T(8,128)S(1)}, f32[9,3,3,96,128]{4,3,2,1,0:T(8,128)S(1)}, f3...) custom-call(bf16[80,256]{1,0:T(8,128)(2,1)S(1)} %collective-permute-, ...), custom_call_target="tpu_custom_call", output_to_operand_aliasing={{2}: (2, {}), {3}: (3, {}), {4}: (4, {}), {5}: (5, {}), {6}... | custom-call | tf_op jit(solution)/shard_map/rim/pallas_call | solution.py:710
  (1 shorter events, 0.0 us)
Async XLA Ops:
  0.6 7.2 %collective-permute-start.1 = (bf16[2,2,64,256]{3,2,1,0:T(8,128)(2,1)}, bf16[2,2,64,256]{3,2,1,0:T(8,128)(2,1)S(1)}, u32[]{:S(2)}, u32[]{:S(2)}) collective-permute-start(bf16[2,2,64,256]{3,2,1,0:T(8,128)(2,1)} %ocean_hbm.1), channel_id=1, source_target_pairs={{0,4},{4,0},{8,12},{12,8},{16,20},{20,16},{24,28},{28,24},{1,2},{5... | collective-permute-start | bytes 393224 | tf_op jit(solution)/shard_map/ppermute | solution.py:565
  1.2 7.6 %collective-permute-start = (bf16[2,2,64,256]{3,2,1,0:T(8,128)(2,1)}, bf16[2,2,64,256]{3,2,1,0:T(8,128)(2,1)S(1)}, u32[]{:S(2)}, u32[]{:S(2)}) collective-permute-start(bf16[2,2,64,256]{3,2,1,0:T(8,128)(2,1)} %ocean_hbm.1), channel_id=1, source_target_pairs={{0,1},{4,5},{8,9},{12,13},{16,17},{20,21},{24,25},{28,29},{1,0},{5... | collective-permute-start | bytes 393224 | tf_op jit(solution)/shard_map/ppermute | solution.py:565
  7.6 4.3 %collective-permute-start.4 = (bf16[128,256]{1,0:T(8,128)(2,1)S(1)}, bf16[128,256]{1,0:T(8,128)(2,1)S(1)}, u32[]{:S(2)}, u32[]{:S(2)}) collective-permute-start(bf16[128,256]{1,0:T(8,128)(2,1)S(1)} %get-tuple-element.35), channel_id=1, source_target_pairs={{0,1},{4,5},{8,9},{12,13},{16,17},{20,21},{24,25},{28,29},{1,0},{5... | collective-permute-start | bytes 196616 | tf_op jit(solution)/shard_map/ppermute | solution.py:565
  7.7 4.3 %collective-permute-start.5 = (bf16[128,256]{1,0:T(8,128)(2,1)S(1)}, bf16[128,256]{1,0:T(8,128)(2,1)S(1)}, u32[]{:S(2)}, u32[]{:S(2)}) collective-permute-start(bf16[128,256]{1,0:T(8,128)(2,1)S(1)} %get-tuple-element.36), channel_id=1, source_target_pairs={{0,4},{4,0},{8,12},{12,8},{16,20},{20,16},{24,28},{28,24},{1,2},{5... | collective-permute-start | bytes 196616 | tf_op jit(solution)/shard_map/ppermute | solution.py:565
  9.1 2.9 %collective-permute-start.2 = (bf16[64,256]{1,0:T(8,128)(2,1)S(1)}, bf16[64,256]{1,0:T(8,128)(2,1)S(1)}, u32[]{:S(2)}, u32[]{:S(2)}) collective-permute-start(bf16[64,256]{1,0:T(8,128)(2,1)S(1)} %get-tuple-element.33), channel_id=1, source_target_pairs={{0,4},{8,12},{16,20},{24,28},{4,0},{12,8},{20,16},{28,24},{1,5},{9... | collective-permute-start | bytes 98312 | tf_op jit(solution)/shard_map/ppermute | solution.py:560
  9.2 4.3 %collective-permute-start.3 = (bf16[64,256]{1,0:T(8,128)(2,1)S(1)}, bf16[64,256]{1,0:T(8,128)(2,1)S(1)}, u32[]{:S(2)}, u32[]{:S(2)}) collective-permute-start(bf16[64,256]{1,0:T(8,128)(2,1)S(1)} %get-tuple-element.34), channel_id=1, source_target_pairs={{4,8},{12,16},{20,24},{28,0},{8,4},{16,12},{24,20},{0,28},{5,9},{1... | collective-permute-start | bytes 98312 | tf_op jit(solution)/shard_map/ppermute | solution.py:560
  13.5 5.1 %collective-permute-start.6 = (bf16[80,256]{1,0:T(8,128)(2,1)S(1)}, bf16[80,256]{1,0:T(8,128)(2,1)S(1)}, u32[]{:S(2)}, u32[]{:S(2)}) collective-permute-start(bf16[80,256]{1,0:T(8,128)(2,1)S(1)} %get-tuple-element.37), channel_id=1, source_target_pairs={{0,1},{4,5},{8,9},{12,13},{16,17},{20,21},{24,25},{28,29},{1,0},{5... | collective-permute-start | bytes 122888 | tf_op jit(solution)/shard_map/ppermute | solution.py:565
  15.9 2.7 %collective-permute-start.7 = (bf16[80,256]{1,0:T(8,128)(2,1)S(1)}, bf16[80,256]{1,0:T(8,128)(2,1)S(1)}, u32[]{:S(2)}, u32[]{:S(2)}) collective-permute-start(bf16[80,256]{1,0:T(8,128)(2,1)S(1)} %get-tuple-element.38), channel_id=1, source_target_pairs={{0,4},{4,0},{8,12},{12,8},{16,20},{20,16},{24,28},{28,24},{1,2},{5... | collective-permute-start | bytes 122888 | tf_op jit(solution)/shard_map/ppermute | solution.py:565

commit v8 on v7

--- a/solution.py
+++ b/solution.py
@@ -244,11 +244,13 @@
     fields_ref,
     lon_x_in,
     lon_y_in,
+    early_y_in,
     force_ref,
     lon_x_ref,
     lon_y_ref,
     lat_x_ref,
     lat_y_ref,
+    early_y_ref,
 ):
     windows, _, rows, cols = current_ref.shape
     side_x = side_ref[:, :rows]
@@ -288,10 +290,11 @@
 
     for ref, north in ((lat_x_ref, northward), (lat_y_ref, jnp.logical_not(northward))):
         pack_rows(ref, 0, groups, depths, value_of, north, rows)
+    early_y_ref[...] = early_y_in[...]
 
 
 def corner_kernel(
-    margin, rows, lat_x_in, lat_y_in, lon_x_ref, lon_y_ref, early_x_ref, early_y_ref, lat_x_ref, lat_y_ref
+    margin, rows, lat_x_in, lat_y_in, lon_x_ref, lon_y_ref, early_x_ref, lat_x_ref, lat_y_ref
 ):
     for old_ref, ref, north in (
         (lat_x_in, lat_x_ref, even("lat")),
@@ -467,13 +470,10 @@
     place_rows(refs, early, range(early), margin, rows, lat_count, early_x_ref, early_y_ref)
     for window in range(windows):
         lost = 2 * SUB * window
+        row_list = range(margin + lost, margin + rows - lost, 8)
 
         def subcycle(number, carry):
             step = window * SUB + number
-            base = step // (SUB * windows) * 8
-            row_list = [
-                pl.multiple_of(base + row, 8) for row in range(margin + lost, margin + rows - lost, 8)
-            ]
             for row in row_list:
                 stress_rows(refs, step, window, row)
             for row in row_list:
@@ -511,15 +511,8 @@
             rows_now(refs, step, step // SUB, done + first)
             rows_now(refs, step, step // SUB, bottom - done + first)
 
-    def subcycles(number, carry):
-        for step in (2 * number, 2 * number + 1):
-            half_step(step, 0)
-            half_step(step, 1)
-        return carry
-
     last = SUB * windows - 1
-    lax.fori_loop(0, last // 2, subcycles, 0)
-    for step in range(last // 2 * 2, last):
+    for step in range(last):
         half_step(step, 0)
         half_step(step, 1)
     half_step(last, 0)
@@ -560,9 +553,8 @@
     return lax.ppermute(x, "lon", lon_swaps(0)), lax.ppermute(y, "lon", lon_swaps(1))
 
 
-def lat_exchange(x, y):
-    axes = ("lon", "lat")
-    return lax.ppermute(x, axes, lat_swaps(0)), lax.ppermute(y, axes, lat_swaps(1))
+def lat_exchange(x, first):
+    return lax.ppermute(x, ("lon", "lat"), lat_swaps(first))
 
 
 def shape(dims, dtype=jnp.float32):
@@ -593,7 +585,7 @@
     late_rows = sum(depths[early:])
     bf16 = jnp.bfloat16
 
-    tile_x, tile_y = lat_exchange(ocean_current, ocean_current)
+    tile_x, tile_y = lat_exchange(ocean_current, 0), lat_exchange(ocean_current, 1)
 
     whole = pl.BlockSpec(memory_space=pltpu.VMEM)
     anywhere = pl.BlockSpec(memory_space=pl.ANY)
@@ -651,8 +643,8 @@
         )
     )
 
-    early_x, early_y = lat_exchange(lat_x, lat_y)
-    force, lon_x, lon_y, lat_x, lat_y = pl.pallas_call(
+    early_x = lat_exchange(lat_x, 0)
+    force, lon_x, lon_y, late_x, late_y, lat_y = pl.pallas_call(
         functools.partial(force_kernel, margin, early),
         out_shape=(
             shape((2 * windows, rows, cols)),
@@ -660,26 +652,28 @@
             shape((rows, packed), bf16),
             shape((late_rows, cols), bf16),
             shape((late_rows, cols), bf16),
+            shape((early_rows, cols), bf16),
         ),
-        in_specs=[whole] * 7,
-        out_specs=(whole,) * 5,
+        in_specs=[whole] * 8,
+        out_specs=(whole,) * 6,
         compiler_params=params(),
         cost_estimate=pl.CostEstimate(flops=1, bytes_accessed=1, transcendentals=0),
         name="force",
-    )(side, tile_x, tile_y, current, fields, lon_x, lon_y)
+    )(side, tile_x, tile_y, current, fields, lon_x, lon_y, lat_y)
 
     lon_x, lon_y = lon_exchange(lon_x, lon_y)
+    early_y = lat_exchange(lat_y, 1)
     message = shape((late_rows + 2 * margin, cols), bf16)
-    lat_x, lat_y = pl.pallas_call(
+    late_x, late_y = pl.pallas_call(
         functools.partial(corner_kernel, margin, rows),
         out_shape=(message, message),
-        in_specs=[whole] * 6,
+        in_specs=[whole] * 5,
         out_specs=(whole,) * 2,
         compiler_params=params(),
         cost_estimate=pl.CostEstimate(flops=1, bytes_accessed=1, transcendentals=0),
         name="corner",
-    )(lat_x, lat_y, lon_x, lon_y, early_x, early_y)
-    lat_x, lat_y = lat_exchange(lat_x, lat_y)
+    )(late_x, late_y, lon_x, lon_y, early_x)
+    late_x, late_y = lat_exchange(late_x, 0), lat_exchange(late_y, 1)
 
     steps = SUB * windows
 
@@ -721,7 +715,7 @@
         ],
         compiler_params=params(),
         name="rim",
-    )(lat_x, lat_y, *refs)[:2]
+    )(late_x, late_y, *refs)[:2]
     return (velocity_out, stress_out, thick_out)
 
 

time: 21.8 us -> 21.3 us (0.977)
  Pallas kernels: 8.3 us -> 7.81 us
    pallas_call x1, Pallas kernels: 2.96 us -> 2.69 us  [local(): pl.pallas_call(functools.partial(rim_kernel, margin, early, count, lax.ax...]
    pallas_call x1, Pallas kernels: 2.66 us -> 2.43 us  [local(): pl.pallas_call(functools.partial(interior_kernel, margin, lax.axis_size('...]
  transfers between devices with their start and end apart: 8 -> 8, of which waited for: 3 -> 3; matrix products, arithmetic and copies ran while one was open for 0% -> 0% of each run, Pallas kernels for 25% -> 24%
where the time goes in v8:
time: 21.3 us; the launch traced here: 21.1 us
  starting transfers between devices  9.8 us (46%)
  Pallas kernels  7.81 us (37%)
  waiting for transfers between devices  2.77 us (13%)
  between operations  0.7 us (3%)
    ppermute x6, starting transfers between devices, lat_exchange(): return lax.ppermute(x, ('lon', 'lat'), lat_swaps(first))  7.17 us
    pallas_call x1, Pallas kernels, local(): pl.pallas_call(functools.partial(rim_kernel, margin, early, count, lax.ax...  2.69 us
    ppermute x1, starting transfers between devices, lon_exchange(): lax.ppermute(y, 'lon', lon_swaps(1))  2.56 us
    pallas_call x1, Pallas kernels, local(): pl.pallas_call(functools.partial(interior_kernel, margin, lax.axis_size('...  2.43 us
    pallas_call x1, Pallas kernels, local(): pl.pallas_call(functools.partial(local_kernel, margin), out_shape=(shape(...  2.34 us
    ppermute x1, waiting for transfers between devices, lon_exchange(): lax.ppermute(y, 'lon', lon_swaps(1))  1.5 us
    ppermute x6, waiting for transfers between devices, lat_exchange(): return lax.ppermute(x, ('lon', 'lat'), lat_swaps(first))  1.27 us
  transfers between devices with their start and end apart: 8, of which 3 were waited for; matrix products, arithmetic and copies ran while one was open for 0% of the time, Pallas kernels for 24%

profile of v8, /device:TPU:0, one launch (start us, length us, event | category | flops | bytes accessed | tf_op | source)
XLA Modules:
  0.0 21.1 jit_solution(8951947053027077492)
XLA Ops:
  0.6 0.5 %collective-permute-start.1 = (bf16[2,2,64,256]{3,2,1,0:T(8,128)(2,1)}, bf16[2,2,64,256]{3,2,1,0:T(8,128)(2,1)S(1)}, u32[]{:S(2)}, u32[]{:S(2)}) collective-permute-start(bf16[2,2,64,256]{3,2,1,0:T(8,128)(2,1)} %ocean_hbm.1), channel_id=1, source_target_pairs={{0,4},{4,0},{8,12},{12,8},{16,20},{20,16},{24,28},{28,24},{1,2},{5... | collective-permute-start | bytes 393224 | tf_op jit(solution)/shard_map/ppermute | solution.py:557
  1.2 4.1 %collective-permute-start = (bf16[2,2,64,256]{3,2,1,0:T(8,128)(2,1)}, bf16[2,2,64,256]{3,2,1,0:T(8,128)(2,1)S(1)}, u32[]{:S(2)}, u32[]{:S(2)}) collective-permute-start(bf16[2,2,64,256]{3,2,1,0:T(8,128)(2,1)} %ocean_hbm.1), channel_id=1, source_target_pairs={{0,1},{4,5},{8,9},{12,13},{16,17},{20,21},{24,25},{28,29},{1,0},{5... | collective-permute-start | bytes 393224 | tf_op jit(solution)/shard_map/ppermute | solution.py:557
  5.3 2.3 %local.1 = (f32[6,64,256]{2,1,0:T(8,128)}, f32[9,64,256]{2,1,0:T(8,128)S(1)}, f32[2,2,64,256]{3,2,1,0:T(8,128)S(1)}, bf16[64,128]{1,0:T(8,128)(2,1)S(1)}, bf16[6...) custom-call(s32[1,16]{1,0:T(1,128)} %covered_hbm.1, ...), custom_call_target="tpu_custom_call" | custom-call | flops 9830400 | bytes 1179648 | tf_op jit(solution)/shard_map/local/pallas_call | solution.py:593
  7.6 0.1 collective-permute-start.4
  7.7 0.0 collective-permute-done.1.tile_y_ref
  7.7 1.0 %collective-permute-done.tile_x_ref = bf16[2,2,64,256]{3,2,1,0:T(8,128)(2,1)S(1)} collective-permute-done((bf16[2,2,64,256]{3,2,1,0:T(8,128)(2,1)}, bf16[2,2,64,256]{3,2,1,0:T(8,128)(2,1)S(1)}, u32[]{:S(2)}, u32[]{:S(2)}) %collective-permute-start) | collective-permute-done | bytes 131104 | tf_op jit(solution)/shard_map/ppermute | solution.py:557
  8.8 0.3 %force.1 = (f32[4,64,256]{2,1,0:T(8,128)S(1)}, bf16[64,256]{1,0:T(8,128)(2,1)S(1)}, bf16[64,256]{1,0:T(8,128)(2,1)S(1)}, bf16[48,256]{1,0:T(8,128)(2,1)S(1)}, bf...) custom-call(bf16[64,128]{1,0:T(8,128)(2,1)S(1)} %get-tuple-element.27.side_ref, ...), custom_call_target="tpu_custom_call" | custom-call | flops 1 | bytes 1 | tf_op jit(solution)/shard_map/force/pallas_call | solution.py:647
  9.1 0.1 collective-permute-start.2
  9.2 2.6 %collective-permute-start.3 = (bf16[64,256]{1,0:T(8,128)(2,1)S(1)}, bf16[64,256]{1,0:T(8,128)(2,1)S(1)}, u32[]{:S(2)}, u32[]{:S(2)}) collective-permute-start(bf16[64,256]{1,0:T(8,128)(2,1)S(1)} %get-tuple-element.36), channel_id=1, source_target_pairs={{4,8},{12,16},{20,24},{28,0},{8,4},{16,12},{24,20},{0,28},{5,9},{1... | collective-permute-start | bytes 98312 | tf_op jit(solution)/shard_map/ppermute | solution.py:553
  11.7 0.0 collective-permute-start.7
  11.7 0.2 %collective-permute-done.4.early_x_ref = bf16[128,256]{1,0:T(8,128)(2,1)S(1)} collective-permute-done((bf16[128,256]{1,0:T(8,128)(2,1)S(1)}, bf16[128,256]{1,0:T(8,128)(2,1)S(1)}, u32[]{:S(2)}, u32[]{:S(2)}) %collective-permute-start.4) | collective-permute-done | bytes 65568 | tf_op jit(solution)/shard_map/ppermute | solution.py:557
  12.0 0.0 collective-permute-done.2.lon_x_ref
  12.0 1.5 %collective-permute-done.3.lon_y_ref = bf16[64,256]{1,0:T(8,128)(2,1)S(1)} collective-permute-done((bf16[64,256]{1,0:T(8,128)(2,1)S(1)}, bf16[64,256]{1,0:T(8,128)(2,1)S(1)}, u32[]{:S(2)}, u32[]{:S(2)}) %collective-permute-start.3) | collective-permute-done | bytes 32800 | tf_op jit(solution)/shard_map/ppermute | solution.py:553
  13.5 2.4 %collective-permute-start.5 = (bf16[80,256]{1,0:T(8,128)(2,1)S(1)}, bf16[80,256]{1,0:T(8,128)(2,1)S(1)}, u32[]{:S(2)}, u32[]{:S(2)}) collective-permute-start(bf16[80,256]{1,0:T(8,128)(2,1)S(1)} %get-tuple-element.38), channel_id=1, source_target_pairs={{0,1},{4,5},{8,9},{12,13},{16,17},{20,21},{24,25},{28,29},{1,0},{5... | collective-permute-start | bytes 122888 | tf_op jit(solution)/shard_map/ppermute | solution.py:557
  15.9 0.0 collective-permute-start.6
  15.9 0.0 collective-permute-done.7.early_y_ref
  15.9 2.4 %interior.1 = (f32[9,2,3,96,128]{4,3,2,1,0:T(8,128)S(1)}, f32[9,3,3,96,128]{4,3,2,1,0:T(8,128)S(1)}, f32[2,3,96,128]{3,2,1,0:T(8,128)S(1)}, f32[2,3,96,128]{3,2,...) custom-call(f32[9,64,256]{2,1,0:T(8,128)S(1)} %get-tuple-element.29.fields_ref, ...), custom_call_target="tpu_custom_call" | custom-call | flops 7864320 | bytes 4194304 | tf_op jit(solution)/shard_map/interior/pallas_call | solution.py:692
  18.4 0.0 collective-permute-done.5.args_0_
  18.4 0.0 collective-permute-done.6.args_1_
  18.4 2.7 %rim.1 = (f32[2,64,256]{2,1,0:T(8,128)}, f32[3,64,256]{2,1,0:T(8,128)}, f32[9,2,3,96,128]{4,3,2,1,0:T(8,128)S(1)}, f32[9,3,3,96,128]{4,3,2,1,0:T(8,128)S(1)}, f3...) custom-call(bf16[80,256]{1,0:T(8,128)(2,1)S(1)} %collective-permute-, ...), custom_call_target="tpu_custom_call", output_to_operand_aliasing={{2}: (2, {}), {3}: (3, {}), {4}: (4, {}), {5}: (5, {}), {6}... | custom-call | tf_op jit(solution)/shard_map/rim/pallas_call | solution.py:704
  (1 shorter events, 0.0 us)
Async XLA Ops:
  0.6 7.1 %collective-permute-start.1 = (bf16[2,2,64,256]{3,2,1,0:T(8,128)(2,1)}, bf16[2,2,64,256]{3,2,1,0:T(8,128)(2,1)S(1)}, u32[]{:S(2)}, u32[]{:S(2)}) collective-permute-start(bf16[2,2,64,256]{3,2,1,0:T(8,128)(2,1)} %ocean_hbm.1), channel_id=1, source_target_pairs={{0,4},{4,0},{8,12},{12,8},{16,20},{20,16},{24,28},{28,24},{1,2},{5... | collective-permute-start | bytes 393224 | tf_op jit(solution)/shard_map/ppermute | solution.py:557
  1.2 7.6 %collective-permute-start = (bf16[2,2,64,256]{3,2,1,0:T(8,128)(2,1)}, bf16[2,2,64,256]{3,2,1,0:T(8,128)(2,1)S(1)}, u32[]{:S(2)}, u32[]{:S(2)}) collective-permute-start(bf16[2,2,64,256]{3,2,1,0:T(8,128)(2,1)} %ocean_hbm.1), channel_id=1, source_target_pairs={{0,1},{4,5},{8,9},{12,13},{16,17},{20,21},{24,25},{28,29},{1,0},{5... | collective-permute-start | bytes 393224 | tf_op jit(solution)/shard_map/ppermute | solution.py:557
  7.6 4.3 %collective-permute-start.4 = (bf16[128,256]{1,0:T(8,128)(2,1)S(1)}, bf16[128,256]{1,0:T(8,128)(2,1)S(1)}, u32[]{:S(2)}, u32[]{:S(2)}) collective-permute-start(bf16[128,256]{1,0:T(8,128)(2,1)S(1)} %get-tuple-element.37), channel_id=1, source_target_pairs={{0,1},{4,5},{8,9},{12,13},{16,17},{20,21},{24,25},{28,29},{1,0},{5... | collective-permute-start | bytes 196616 | tf_op jit(solution)/shard_map/ppermute | solution.py:557
  9.1 2.9 %collective-permute-start.2 = (bf16[64,256]{1,0:T(8,128)(2,1)S(1)}, bf16[64,256]{1,0:T(8,128)(2,1)S(1)}, u32[]{:S(2)}, u32[]{:S(2)}) collective-permute-start(bf16[64,256]{1,0:T(8,128)(2,1)S(1)} %get-tuple-element.35), channel_id=1, source_target_pairs={{0,4},{8,12},{16,20},{24,28},{4,0},{12,8},{20,16},{28,24},{1,5},{9... | collective-permute-start | bytes 98312 | tf_op jit(solution)/shard_map/ppermute | solution.py:553
  9.2 4.3 %collective-permute-start.3 = (bf16[64,256]{1,0:T(8,128)(2,1)S(1)}, bf16[64,256]{1,0:T(8,128)(2,1)S(1)}, u32[]{:S(2)}, u32[]{:S(2)}) collective-permute-start(bf16[64,256]{1,0:T(8,128)(2,1)S(1)} %get-tuple-element.36), channel_id=1, source_target_pairs={{4,8},{12,16},{20,24},{28,0},{8,4},{16,12},{24,20},{0,28},{5,9},{1... | collective-permute-start | bytes 98312 | tf_op jit(solution)/shard_map/ppermute | solution.py:553
  11.7 4.2 %collective-permute-start.7 = (bf16[128,256]{1,0:T(8,128)(2,1)S(1)}, bf16[128,256]{1,0:T(8,128)(2,1)S(1)}, u32[]{:S(2)}, u32[]{:S(2)}) collective-permute-start(bf16[128,256]{1,0:T(8,128)(2,1)S(1)} %get-tuple-element.41), channel_id=1, source_target_pairs={{0,4},{4,0},{8,12},{12,8},{16,20},{20,16},{24,28},{28,24},{1,2},{5... | collective-permute-start | bytes 196616 | tf_op jit(solution)/shard_map/ppermute | solution.py:557
  13.5 4.9 %collective-permute-start.5 = (bf16[80,256]{1,0:T(8,128)(2,1)S(1)}, bf16[80,256]{1,0:T(8,128)(2,1)S(1)}, u32[]{:S(2)}, u32[]{:S(2)}) collective-permute-start(bf16[80,256]{1,0:T(8,128)(2,1)S(1)} %get-tuple-element.38), channel_id=1, source_target_pairs={{0,1},{4,5},{8,9},{12,13},{16,17},{20,21},{24,25},{28,29},{1,0},{5... | collective-permute-start | bytes 122888 | tf_op jit(solution)/shard_map/ppermute | solution.py:557
  15.9 2.5 %collective-permute-start.6 = (bf16[80,256]{1,0:T(8,128)(2,1)S(1)}, bf16[80,256]{1,0:T(8,128)(2,1)S(1)}, u32[]{:S(2)}, u32[]{:S(2)}) collective-permute-start(bf16[80,256]{1,0:T(8,128)(2,1)S(1)} %get-tuple-element.39), channel_id=1, source_target_pairs={{0,4},{4,0},{8,12},{12,8},{16,20},{20,16},{24,28},{28,24},{1,2},{5... | collective-permute-start | bytes 122888 | tf_op jit(solution)/shard_map/ppermute | solution.py:557

commit v9 on v8

--- a/solution.py
+++ b/solution.py
@@ -234,12 +234,21 @@
     y_ref[:, lanes] = jnp.where(eastward, west, east).astype(jnp.bfloat16)
 
 
+def side_kernel(side_ref, tile_ref, current_ref, sum_ref):
+    windows, parts, rows, _ = current_ref.shape
+    weights = side_ref[:, :rows]
+    for w in range(windows):
+        for k in range(parts):
+            sum_ref[w, k] = current_ref[w, k] + jnp.dot(
+                weights, tile_ref[w, k], preferred_element_type=jnp.float32
+            )
+
+
 def force_kernel(
     margin,
     early,
     side_ref,
-    tile_x_ref,
-    tile_y_ref,
+    tile_ref,
     current_ref,
     fields_ref,
     lon_x_in,
@@ -253,16 +262,11 @@
     early_y_ref,
 ):
     windows, _, rows, cols = current_ref.shape
-    side_x = side_ref[:, :rows]
-    side_y = side_ref[:, rows:]
-
-    def dot(a, b):
-        return jnp.dot(a, b, preferred_element_type=jnp.float32)
-
+    weights = side_ref[:, rows:]
     for w in range(windows):
         b = fields_ref[STATE + 2 * w + 1]
         for k in range(2):
-            current = dot(side_x, tile_x_ref[w, k]) + dot(side_y, tile_y_ref[w, k])
+            current = jnp.dot(weights, tile_ref[w, k], preferred_element_type=jnp.float32)
             force_ref[2 * w + k] = b * (current_ref[w, k] + current)
 
     per = LANES // margin
@@ -644,6 +648,15 @@
     )
 
     early_x = lat_exchange(lat_x, 0)
+    current = pl.pallas_call(
+        side_kernel,
+        out_shape=shape(wind_stress.shape),
+        in_specs=[whole] * 3,
+        out_specs=whole,
+        compiler_params=params(),
+        cost_estimate=pl.CostEstimate(flops=1, bytes_accessed=1, transcendentals=0),
+        name="side",
+    )(side, tile_x, current)
     force, lon_x, lon_y, late_x, late_y, lat_y = pl.pallas_call(
         functools.partial(force_kernel, margin, early),
         out_shape=(
@@ -654,12 +667,12 @@
             shape((late_rows, cols), bf16),
             shape((early_rows, cols), bf16),
         ),
-        in_specs=[whole] * 8,
+        in_specs=[whole] * 7,
         out_specs=(whole,) * 6,
         compiler_params=params(),
         cost_estimate=pl.CostEstimate(flops=1, bytes_accessed=1, transcendentals=0),
         name="force",
-    )(side, tile_x, tile_y, current, fields, lon_x, lon_y, lat_y)
+    )(side, tile_y, current, fields, lon_x, lon_y, lat_y)
 
     lon_x, lon_y = lon_exchange(lon_x, lon_y)
     early_y = lat_exchange(lat_y, 1)

time: 21.3 us -> 21.1 us (level)
  waiting for transfers between devices: 2.77 us -> 2.45 us
    ppermute x6, waiting for transfers between devices: 1.27 us -> 0.71 us  [lat_exchange(): return lax.ppermute(x, ('lon', 'lat'), lat_swaps(first))]
    ppermute x1, waiting for transfers between devices: 1.5 us -> 1.74 us  [lon_exchange(): lax.ppermute(y, 'lon', lon_swaps(1))]
  transfers between devices with their start and end apart: 8 -> 8, of which waited for: 3 -> 2; matrix products, arithmetic and copies ran while one was open for 0% -> 0% of each run, Pallas kernels for 24% -> 25%
where the time goes in v9:
time: 21.1 us; the launch traced here: 20.9 us
  starting transfers between devices  9.85 us (47%)
  Pallas kernels  7.93 us (38%)
  waiting for transfers between devices  2.45 us (12%)
  between operations  0.69 us (3%)
    ppermute x6, starting transfers between devices, lat_exchange(): return lax.ppermute(x, ('lon', 'lat'), lat_swaps(first))  7.23 us
    pallas_call x1, Pallas kernels, local(): pl.pallas_call(functools.partial(rim_kernel, margin, early, count, lax.ax...  2.67 us
    ppermute x1, starting transfers between devices, lon_exchange(): lax.ppermute(y, 'lon', lon_swaps(1))  2.55 us
    pallas_call x1, Pallas kernels, local(): pl.pallas_call(functools.partial(interior_kernel, margin, lax.axis_size('...  2.43 us
    pallas_call x1, Pallas kernels, local(): pl.pallas_call(functools.partial(local_kernel, margin), out_shape=(shape(...  2.34 us
    ppermute x1, waiting for transfers between devices, lon_exchange(): lax.ppermute(y, 'lon', lon_swaps(1))  1.74 us
    ppermute x6, waiting for transfers between devices, lat_exchange(): return lax.ppermute(x, ('lon', 'lat'), lat_swaps(first))  0.71 us
  transfers between devices with their start and end apart: 8, of which 2 were waited for; matrix products, arithmetic and copies ran while one was open for 0% of the time, Pallas kernels for 25%

profile of v9, /device:TPU:0, one launch (start us, length us, event | category | flops | bytes accessed | tf_op | source)
XLA Modules:
  0.0 20.9 jit_solution(9958042708266198174)
XLA Ops:
  0.6 3.1 %collective-permute-start.1 = (bf16[2,2,64,256]{3,2,1,0:T(8,128)(2,1)}, bf16[2,2,64,256]{3,2,1,0:T(8,128)(2,1)S(1)}, u32[]{:S(2)}, u32[]{:S(2)}) collective-permute-start(bf16[2,2,64,256]{3,2,1,0:T(8,128)(2,1)} %ocean_hbm.1), channel_id=1, source_target_pairs={{0,1},{4,5},{8,9},{12,13},{16,17},{20,21},{24,25},{28,29},{1,0},{5... | collective-permute-start | bytes 393224 | tf_op jit(solution)/shard_map/ppermute | solution.py:561
  3.7 0.0 collective-permute-start
  3.7 2.3 %local.1 = (f32[6,64,256]{2,1,0:T(8,128)}, f32[9,64,256]{2,1,0:T(8,128)S(1)}, f32[2,2,64,256]{3,2,1,0:T(8,128)S(1)}, bf16[64,128]{1,0:T(8,128)(2,1)S(1)}, bf16[6...) custom-call(s32[1,16]{1,0:T(1,128)} %covered_hbm.1, ...), custom_call_target="tpu_custom_call" | custom-call | flops 9830400 | bytes 1179648 | tf_op jit(solution)/shard_map/local/pallas_call | solution.py:597
  6.1 3.2 %collective-permute-start.4 = (bf16[128,256]{1,0:T(8,128)(2,1)S(1)}, bf16[128,256]{1,0:T(8,128)(2,1)S(1)}, u32[]{:S(2)}, u32[]{:S(2)}) collective-permute-start(bf16[128,256]{1,0:T(8,128)(2,1)S(1)} %get-tuple-element.37), channel_id=1, source_target_pairs={{0,1},{4,5},{8,9},{12,13},{16,17},{20,21},{24,25},{28,29},{1,0},{5... | collective-permute-start | bytes 196616 | tf_op jit(solution)/shard_map/ppermute | solution.py:561
  9.3 0.0 collective-permute-done.1.tile_ref
  9.3 0.2 side.1.current_ref
  9.5 0.0 collective-permute-done.tile_ref
  9.5 0.3 %force.1 = (f32[4,64,256]{2,1,0:T(8,128)S(1)}, bf16[64,256]{1,0:T(8,128)(2,1)S(1)}, bf16[64,256]{1,0:T(8,128)(2,1)S(1)}, bf16[48,256]{1,0:T(8,128)(2,1)S(1)}, bf...) custom-call(bf16[64,128]{1,0:T(8,128)(2,1)S(1)} %get-tuple-element.27.side_ref, ...), custom_call_target="tpu_custom_call" | custom-call | flops 1 | bytes 1 | tf_op jit(solution)/shard_map/force/pallas_call | solution.py:660
  9.8 0.1 collective-permute-start.2
  9.9 2.5 %collective-permute-start.3 = (bf16[64,256]{1,0:T(8,128)(2,1)S(1)}, bf16[64,256]{1,0:T(8,128)(2,1)S(1)}, u32[]{:S(2)}, u32[]{:S(2)}) collective-permute-start(bf16[64,256]{1,0:T(8,128)(2,1)S(1)} %get-tuple-element.36), channel_id=1, source_target_pairs={{4,8},{12,16},{20,24},{28,0},{8,4},{16,12},{24,20},{0,28},{5,9},{1... | collective-permute-start | bytes 98312 | tf_op jit(solution)/shard_map/ppermute | solution.py:557
  12.4 0.0 collective-permute-start.7
  12.4 0.0 collective-permute-done.4.early_x_ref
  12.4 0.0 collective-permute-done.2.lon_x_ref
  12.4 1.7 %collective-permute-done.3.lon_y_ref = bf16[64,256]{1,0:T(8,128)(2,1)S(1)} collective-permute-done((bf16[64,256]{1,0:T(8,128)(2,1)S(1)}, bf16[64,256]{1,0:T(8,128)(2,1)S(1)}, u32[]{:S(2)}, u32[]{:S(2)}) %collective-permute-start.3) | collective-permute-done | bytes 32800 | tf_op jit(solution)/shard_map/ppermute | solution.py:557
  14.2 0.9 %collective-permute-start.5 = (bf16[80,256]{1,0:T(8,128)(2,1)S(1)}, bf16[80,256]{1,0:T(8,128)(2,1)S(1)}, u32[]{:S(2)}, u32[]{:S(2)}) collective-permute-start(bf16[80,256]{1,0:T(8,128)(2,1)S(1)} %get-tuple-element.38), channel_id=1, source_target_pairs={{0,1},{4,5},{8,9},{12,13},{16,17},{20,21},{24,25},{28,29},{1,0},{5... | collective-permute-start | bytes 122888 | tf_op jit(solution)/shard_map/ppermute | solution.py:561
  15.1 0.0 collective-permute-start.6
  15.1 0.0 collective-permute-done.7.early_y_ref
  15.1 2.4 %interior.1 = (f32[9,2,3,96,128]{4,3,2,1,0:T(8,128)S(1)}, f32[9,3,3,96,128]{4,3,2,1,0:T(8,128)S(1)}, f32[2,3,96,128]{3,2,1,0:T(8,128)S(1)}, f32[2,3,96,128]{3,2,...) custom-call(f32[9,64,256]{2,1,0:T(8,128)S(1)} %get-tuple-element.29.fields_ref, ...), custom_call_target="tpu_custom_call" | custom-call | flops 7864320 | bytes 4194304 | tf_op jit(solution)/shard_map/interior/pallas_call | solution.py:705
  17.6 0.7 %collective-permute-done.5.args_0_ = bf16[80,256]{1,0:T(8,128)(2,1)S(1)} collective-permute-done((bf16[80,256]{1,0:T(8,128)(2,1)S(1)}, bf16[80,256]{1,0:T(8,128)(2,1)S(1)}, u32[]{:S(2)}, u32[]{:S(2)}) %collective-permute-start.5) | collective-permute-done | bytes 40992 | tf_op jit(solution)/shard_map/ppermute | solution.py:561
  18.2 0.0 collective-permute-done.6.args_1_
  18.3 2.7 %rim.1 = (f32[2,64,256]{2,1,0:T(8,128)}, f32[3,64,256]{2,1,0:T(8,128)}, f32[9,2,3,96,128]{4,3,2,1,0:T(8,128)S(1)}, f32[9,3,3,96,128]{4,3,2,1,0:T(8,128)S(1)}, f3...) custom-call(bf16[80,256]{1,0:T(8,128)(2,1)S(1)} %collective-permute-, ...), custom_call_target="tpu_custom_call", output_to_operand_aliasing={{2}: (2, {}), {3}: (3, {}), {4}: (4, {}), {5}: (5, {}), {6}... | custom-call | tf_op jit(solution)/shard_map/rim/pallas_call | solution.py:717
  (1 shorter events, 0.0 us)
Async XLA Ops:
  0.6 8.7 %collective-permute-start.1 = (bf16[2,2,64,256]{3,2,1,0:T(8,128)(2,1)}, bf16[2,2,64,256]{3,2,1,0:T(8,128)(2,1)S(1)}, u32[]{:S(2)}, u32[]{:S(2)}) collective-permute-start(bf16[2,2,64,256]{3,2,1,0:T(8,128)(2,1)} %ocean_hbm.1), channel_id=1, source_target_pairs={{0,1},{4,5},{8,9},{12,13},{16,17},{20,21},{24,25},{28,29},{1,0},{5... | collective-permute-start | bytes 393224 | tf_op jit(solution)/shard_map/ppermute | solution.py:561
  3.7 5.7 %collective-permute-start = (bf16[2,2,64,256]{3,2,1,0:T(8,128)(2,1)}, bf16[2,2,64,256]{3,2,1,0:T(8,128)(2,1)S(1)}, u32[]{:S(2)}, u32[]{:S(2)}) collective-permute-start(bf16[2,2,64,256]{3,2,1,0:T(8,128)(2,1)} %ocean_hbm.1), channel_id=1, source_target_pairs={{0,4},{4,0},{8,12},{12,8},{16,20},{20,16},{24,28},{28,24},{1,2},{5... | collective-permute-start | bytes 393224 | tf_op jit(solution)/shard_map/ppermute | solution.py:561
  6.1 6.4 %collective-permute-start.4 = (bf16[128,256]{1,0:T(8,128)(2,1)S(1)}, bf16[128,256]{1,0:T(8,128)(2,1)S(1)}, u32[]{:S(2)}, u32[]{:S(2)}) collective-permute-start(bf16[128,256]{1,0:T(8,128)(2,1)S(1)} %get-tuple-element.37), channel_id=1, source_target_pairs={{0,1},{4,5},{8,9},{12,13},{16,17},{20,21},{24,25},{28,29},{1,0},{5... | collective-permute-start | bytes 196616 | tf_op jit(solution)/shard_map/ppermute | solution.py:561
  9.8 2.6 %collective-permute-start.2 = (bf16[64,256]{1,0:T(8,128)(2,1)S(1)}, bf16[64,256]{1,0:T(8,128)(2,1)S(1)}, u32[]{:S(2)}, u32[]{:S(2)}) collective-permute-start(bf16[64,256]{1,0:T(8,128)(2,1)S(1)} %get-tuple-element.35), channel_id=1, source_target_pairs={{0,4},{8,12},{16,20},{24,28},{4,0},{12,8},{20,16},{28,24},{1,5},{9... | collective-permute-start | bytes 98312 | tf_op jit(solution)/shard_map/ppermute | solution.py:557
  9.9 4.3 %collective-permute-start.3 = (bf16[64,256]{1,0:T(8,128)(2,1)S(1)}, bf16[64,256]{1,0:T(8,128)(2,1)S(1)}, u32[]{:S(2)}, u32[]{:S(2)}) collective-permute-start(bf16[64,256]{1,0:T(8,128)(2,1)S(1)} %get-tuple-element.36), channel_id=1, source_target_pairs={{4,8},{12,16},{20,24},{28,0},{8,4},{16,12},{24,20},{0,28},{5,9},{1... | collective-permute-start | bytes 98312 | tf_op jit(solution)/shard_map/ppermute | solution.py:557
  12.4 2.7 %collective-permute-start.7 = (bf16[128,256]{1,0:T(8,128)(2,1)S(1)}, bf16[128,256]{1,0:T(8,128)(2,1)S(1)}, u32[]{:S(2)}, u32[]{:S(2)}) collective-permute-start(bf16[128,256]{1,0:T(8,128)(2,1)S(1)} %get-tuple-element.41), channel_id=1, source_target_pairs={{0,4},{4,0},{8,12},{12,8},{16,20},{20,16},{24,28},{28,24},{1,2},{5... | collective-permute-start | bytes 196616 | tf_op jit(solution)/shard_map/ppermute | solution.py:561
  14.2 4.1 %collective-permute-start.5 = (bf16[80,256]{1,0:T(8,128)(2,1)S(1)}, bf16[80,256]{1,0:T(8,128)(2,1)S(1)}, u32[]{:S(2)}, u32[]{:S(2)}) collective-permute-start(bf16[80,256]{1,0:T(8,128)(2,1)S(1)} %get-tuple-element.38), channel_id=1, source_target_pairs={{0,1},{4,5},{8,9},{12,13},{16,17},{20,21},{24,25},{28,29},{1,0},{5... | collective-permute-start | bytes 122888 | tf_op jit(solution)/shard_map/ppermute | solution.py:561
  15.1 3.1 %collective-permute-start.6 = (bf16[80,256]{1,0:T(8,128)(2,1)S(1)}, bf16[80,256]{1,0:T(8,128)(2,1)S(1)}, u32[]{:S(2)}, u32[]{:S(2)}) collective-permute-start(bf16[80,256]{1,0:T(8,128)(2,1)S(1)} %get-tuple-element.39), channel_id=1, source_target_pairs={{0,4},{4,0},{8,12},{12,8},{16,20},{20,16},{24,28},{28,24},{1,2},{5... | collective-permute-start | bytes 122888 | tf_op jit(solution)/shard_map/ppermute | solution.py:561

commit v10 on v9

--- a/solution.py
+++ b/solution.py
@@ -365,10 +365,10 @@
     ]
 
 
-def stress_rows(refs, step, window, row):
+def stress_rows(refs, step, window, row, height=GROUP):
     velocity, stress, strength, _, _, _ = refs
     every = range(velocity.shape[2])
-    at, north, south = pl.ds(row, 8), pl.ds(row + 1, 8), pl.ds(row - 1, 8)
+    at, north, south = (pl.ds(row + shift, height) for shift in (0, 1, -1))
     u_x = across([velocity[step, 0, j, at, :] for j in every])
     v_x = across([velocity[step, 1, j, at, :] for j in every])
     for j in every:
@@ -388,10 +388,10 @@
         stress[step + 1, 2, j, at, :] = old[2] + kr * shear4
 
 
-def velocity_rows(refs, step, window, row):
+def velocity_rows(refs, step, window, row, height=GROUP):
     velocity, stress, _, keep, push, force = refs
     every = range(velocity.shape[2])
-    at, north, south = pl.ds(row, 8), pl.ds(row + 1, 8), pl.ds(row - 1, 8)
+    at, north, south = (pl.ds(row + shift, height) for shift in (0, 1, -1))
     now = step + 1
     p_x = across([stress[now, 0, j, at, :] for j in every])
     t_x = across([stress[now, 2, j, at, :] for j in every])
@@ -474,7 +474,7 @@
     place_rows(refs, early, range(early), margin, rows, lat_count, early_x_ref, early_y_ref)
     for window in range(windows):
         lost = 2 * SUB * window
-        row_list = range(margin + lost, margin + rows - lost, 8)
+        row_list = range(margin + lost, margin + rows - lost, GROUP)
 
         def subcycle(number, carry):
             step = window * SUB + number
@@ -511,7 +511,7 @@
     def half_step(step, half):
         done = 2 * step + 1 + half
         rows_now = velocity_rows if half else stress_rows
-        for first in range(0, margin, 8):
+        for first in range(0, margin, GROUP):
             rows_now(refs, step, step // SUB, done + first)
             rows_now(refs, step, step // SUB, bottom - done + first)
 

time: 21.1 us -> 21.1 us (level)
  transfers between devices with their start and end apart: 8 -> 8, of which waited for: 2 -> 2; matrix products, arithmetic and copies ran while one was open for 0% -> 0% of each run, Pallas kernels for 25% -> 26%
where the time goes in v10:
time: 21.1 us; the launch traced here: 21 us
  starting transfers between devices  9.85 us (47%)
  Pallas kernels  8.08 us (38%)
  waiting for transfers between devices  2.35 us (11%)
  between operations  0.69 us (3%)
    ppermute x6, starting transfers between devices, lat_exchange(): return lax.ppermute(x, ('lon', 'lat'), lat_swaps(first))  7.23 us
    pallas_call x1, Pallas kernels, local(): pl.pallas_call(functools.partial(rim_kernel, margin, early, count, lax.ax...  2.71 us
    ppermute x1, starting transfers between devices, lon_exchange(): lax.ppermute(y, 'lon', lon_swaps(1))  2.55 us
    pallas_call x1, Pallas kernels, local(): pl.pallas_call(functools.partial(interior_kernel, margin, lax.axis_size('...  2.54 us
    pallas_call x1, Pallas kernels, local(): pl.pallas_call(functools.partial(local_kernel, margin), out_shape=(shape(...  2.34 us
    ppermute x1, waiting for transfers between devices, lon_exchange(): lax.ppermute(y, 'lon', lon_swaps(1))  1.74 us
    ppermute x6, waiting for transfers between devices, lat_exchange(): return lax.ppermute(x, ('lon', 'lat'), lat_swaps(first))  0.6 us
  transfers between devices with their start and end apart: 8, of which 2 were waited for; matrix products, arithmetic and copies ran while one was open for 0% of the time, Pallas kernels for 26%

profile of v10, /device:TPU:0, one launch (start us, length us, event | category | flops | bytes accessed | tf_op | source)
XLA Modules:
  0.0 21.0 jit_solution(11961849908485312672)
XLA Ops:
  0.6 3.1 %collective-permute-start.1 = (bf16[2,2,64,256]{3,2,1,0:T(8,128)(2,1)}, bf16[2,2,64,256]{3,2,1,0:T(8,128)(2,1)S(1)}, u32[]{:S(2)}, u32[]{:S(2)}) collective-permute-start(bf16[2,2,64,256]{3,2,1,0:T(8,128)(2,1)} %ocean_hbm.1), channel_id=1, source_target_pairs={{0,1},{4,5},{8,9},{12,13},{16,17},{20,21},{24,25},{28,29},{1,0},{5... | collective-permute-start | bytes 393224 | tf_op jit(solution)/shard_map/ppermute | solution.py:561
  3.7 0.0 collective-permute-start
  3.7 2.3 %local.1 = (f32[6,64,256]{2,1,0:T(8,128)}, f32[9,64,256]{2,1,0:T(8,128)S(1)}, f32[2,2,64,256]{3,2,1,0:T(8,128)S(1)}, bf16[64,128]{1,0:T(8,128)(2,1)S(1)}, bf16[6...) custom-call(s32[1,16]{1,0:T(1,128)} %covered_hbm.1, ...), custom_call_target="tpu_custom_call" | custom-call | flops 9830400 | bytes 1179648 | tf_op jit(solution)/shard_map/local/pallas_call | solution.py:597
  6.1 3.2 %collective-permute-start.4 = (bf16[128,256]{1,0:T(8,128)(2,1)S(1)}, bf16[128,256]{1,0:T(8,128)(2,1)S(1)}, u32[]{:S(2)}, u32[]{:S(2)}) collective-permute-start(bf16[128,256]{1,0:T(8,128)(2,1)S(1)} %get-tuple-element.37), channel_id=1, source_target_pairs={{0,1},{4,5},{8,9},{12,13},{16,17},{20,21},{24,25},{28,29},{1,0},{5... | collective-permute-start | bytes 196616 | tf_op jit(solution)/shard_map/ppermute | solution.py:561
  9.3 0.0 collective-permute-done.1.tile_ref
  9.3 0.2 side.1.current_ref
  9.5 0.0 collective-permute-done.tile_ref
  9.5 0.3 %force.1 = (f32[4,64,256]{2,1,0:T(8,128)S(1)}, bf16[64,256]{1,0:T(8,128)(2,1)S(1)}, bf16[64,256]{1,0:T(8,128)(2,1)S(1)}, bf16[48,256]{1,0:T(8,128)(2,1)S(1)}, bf...) custom-call(bf16[64,128]{1,0:T(8,128)(2,1)S(1)} %get-tuple-element.27.side_ref, ...), custom_call_target="tpu_custom_call" | custom-call | flops 1 | bytes 1 | tf_op jit(solution)/shard_map/force/pallas_call | solution.py:660
  9.8 0.1 collective-permute-start.2
  9.9 2.5 %collective-permute-start.3 = (bf16[64,256]{1,0:T(8,128)(2,1)S(1)}, bf16[64,256]{1,0:T(8,128)(2,1)S(1)}, u32[]{:S(2)}, u32[]{:S(2)}) collective-permute-start(bf16[64,256]{1,0:T(8,128)(2,1)S(1)} %get-tuple-element.36), channel_id=1, source_target_pairs={{4,8},{12,16},{20,24},{28,0},{8,4},{16,12},{24,20},{0,28},{5,9},{1... | collective-permute-start | bytes 98312 | tf_op jit(solution)/shard_map/ppermute | solution.py:557
  12.4 0.0 collective-permute-start.7
  12.4 0.0 collective-permute-done.4.early_x_ref
  12.4 0.0 collective-permute-done.2.lon_x_ref
  12.4 1.7 %collective-permute-done.3.lon_y_ref = bf16[64,256]{1,0:T(8,128)(2,1)S(1)} collective-permute-done((bf16[64,256]{1,0:T(8,128)(2,1)S(1)}, bf16[64,256]{1,0:T(8,128)(2,1)S(1)}, u32[]{:S(2)}, u32[]{:S(2)}) %collective-permute-start.3) | collective-permute-done | bytes 32800 | tf_op jit(solution)/shard_map/ppermute | solution.py:557
  14.2 0.9 %collective-permute-start.5 = (bf16[80,256]{1,0:T(8,128)(2,1)S(1)}, bf16[80,256]{1,0:T(8,128)(2,1)S(1)}, u32[]{:S(2)}, u32[]{:S(2)}) collective-permute-start(bf16[80,256]{1,0:T(8,128)(2,1)S(1)} %get-tuple-element.38), channel_id=1, source_target_pairs={{0,1},{4,5},{8,9},{12,13},{16,17},{20,21},{24,25},{28,29},{1,0},{5... | collective-permute-start | bytes 122888 | tf_op jit(solution)/shard_map/ppermute | solution.py:561
  15.1 0.0 collective-permute-start.6
  15.1 0.0 collective-permute-done.7.early_y_ref
  15.1 2.5 %interior.1 = (f32[9,2,3,96,128]{4,3,2,1,0:T(8,128)S(1)}, f32[9,3,3,96,128]{4,3,2,1,0:T(8,128)S(1)}, f32[2,3,96,128]{3,2,1,0:T(8,128)S(1)}, f32[2,3,96,128]{3,2,...) custom-call(f32[9,64,256]{2,1,0:T(8,128)S(1)} %get-tuple-element.29.fields_ref, ...), custom_call_target="tpu_custom_call" | custom-call | flops 7864320 | bytes 4194304 | tf_op jit(solution)/shard_map/interior/pallas_call | solution.py:705
  17.7 0.6 %collective-permute-done.5.args_0_ = bf16[80,256]{1,0:T(8,128)(2,1)S(1)} collective-permute-done((bf16[80,256]{1,0:T(8,128)(2,1)S(1)}, bf16[80,256]{1,0:T(8,128)(2,1)S(1)}, u32[]{:S(2)}, u32[]{:S(2)}) %collective-permute-start.5) | collective-permute-done | bytes 40992 | tf_op jit(solution)/shard_map/ppermute | solution.py:561
  18.2 0.0 collective-permute-done.6.args_1_
  18.3 2.7 %rim.1 = (f32[2,64,256]{2,1,0:T(8,128)}, f32[3,64,256]{2,1,0:T(8,128)}, f32[9,2,3,96,128]{4,3,2,1,0:T(8,128)S(1)}, f32[9,3,3,96,128]{4,3,2,1,0:T(8,128)S(1)}, f3...) custom-call(bf16[80,256]{1,0:T(8,128)(2,1)S(1)} %collective-permute-, ...), custom_call_target="tpu_custom_call", output_to_operand_aliasing={{2}: (2, {}), {3}: (3, {}), {4}: (4, {}), {5}: (5, {}), {6}... | custom-call | tf_op jit(solution)/shard_map/rim/pallas_call | solution.py:717
  (1 shorter events, 0.0 us)
Async XLA Ops:
  0.6 8.7 %collective-permute-start.1 = (bf16[2,2,64,256]{3,2,1,0:T(8,128)(2,1)}, bf16[2,2,64,256]{3,2,1,0:T(8,128)(2,1)S(1)}, u32[]{:S(2)}, u32[]{:S(2)}) collective-permute-start(bf16[2,2,64,256]{3,2,1,0:T(8,128)(2,1)} %ocean_hbm.1), channel_id=1, source_target_pairs={{0,1},{4,5},{8,9},{12,13},{16,17},{20,21},{24,25},{28,29},{1,0},{5... | collective-permute-start | bytes 393224 | tf_op jit(solution)/shard_map/ppermute | solution.py:561
  3.7 5.7 %collective-permute-start = (bf16[2,2,64,256]{3,2,1,0:T(8,128)(2,1)}, bf16[2,2,64,256]{3,2,1,0:T(8,128)(2,1)S(1)}, u32[]{:S(2)}, u32[]{:S(2)}) collective-permute-start(bf16[2,2,64,256]{3,2,1,0:T(8,128)(2,1)} %ocean_hbm.1), channel_id=1, source_target_pairs={{0,4},{4,0},{8,12},{12,8},{16,20},{20,16},{24,28},{28,24},{1,2},{5... | collective-permute-start | bytes 393224 | tf_op jit(solution)/shard_map/ppermute | solution.py:561
  6.1 6.4 %collective-permute-start.4 = (bf16[128,256]{1,0:T(8,128)(2,1)S(1)}, bf16[128,256]{1,0:T(8,128)(2,1)S(1)}, u32[]{:S(2)}, u32[]{:S(2)}) collective-permute-start(bf16[128,256]{1,0:T(8,128)(2,1)S(1)} %get-tuple-element.37), channel_id=1, source_target_pairs={{0,1},{4,5},{8,9},{12,13},{16,17},{20,21},{24,25},{28,29},{1,0},{5... | collective-permute-start | bytes 196616 | tf_op jit(solution)/shard_map/ppermute | solution.py:561
  9.8 2.6 %collective-permute-start.2 = (bf16[64,256]{1,0:T(8,128)(2,1)S(1)}, bf16[64,256]{1,0:T(8,128)(2,1)S(1)}, u32[]{:S(2)}, u32[]{:S(2)}) collective-permute-start(bf16[64,256]{1,0:T(8,128)(2,1)S(1)} %get-tuple-element.35), channel_id=1, source_target_pairs={{0,4},{8,12},{16,20},{24,28},{4,0},{12,8},{20,16},{28,24},{1,5},{9... | collective-permute-start | bytes 98312 | tf_op jit(solution)/shard_map/ppermute | solution.py:557
  9.9 4.3 %collective-permute-start.3 = (bf16[64,256]{1,0:T(8,128)(2,1)S(1)}, bf16[64,256]{1,0:T(8,128)(2,1)S(1)}, u32[]{:S(2)}, u32[]{:S(2)}) collective-permute-start(bf16[64,256]{1,0:T(8,128)(2,1)S(1)} %get-tuple-element.36), channel_id=1, source_target_pairs={{4,8},{12,16},{20,24},{28,0},{8,4},{16,12},{24,20},{0,28},{5,9},{1... | collective-permute-start | bytes 98312 | tf_op jit(solution)/shard_map/ppermute | solution.py:557
  12.4 2.7 %collective-permute-start.7 = (bf16[128,256]{1,0:T(8,128)(2,1)S(1)}, bf16[128,256]{1,0:T(8,128)(2,1)S(1)}, u32[]{:S(2)}, u32[]{:S(2)}) collective-permute-start(bf16[128,256]{1,0:T(8,128)(2,1)S(1)} %get-tuple-element.41), channel_id=1, source_target_pairs={{0,4},{4,0},{8,12},{12,8},{16,20},{20,16},{24,28},{28,24},{1,2},{5... | collective-permute-start | bytes 196616 | tf_op jit(solution)/shard_map/ppermute | solution.py:561
  14.2 4.1 %collective-permute-start.5 = (bf16[80,256]{1,0:T(8,128)(2,1)S(1)}, bf16[80,256]{1,0:T(8,128)(2,1)S(1)}, u32[]{:S(2)}, u32[]{:S(2)}) collective-permute-start(bf16[80,256]{1,0:T(8,128)(2,1)S(1)} %get-tuple-element.38), channel_id=1, source_target_pairs={{0,1},{4,5},{8,9},{12,13},{16,17},{20,21},{24,25},{28,29},{1,0},{5... | collective-permute-start | bytes 122888 | tf_op jit(solution)/shard_map/ppermute | solution.py:561
  15.1 3.1 %collective-permute-start.6 = (bf16[80,256]{1,0:T(8,128)(2,1)S(1)}, bf16[80,256]{1,0:T(8,128)(2,1)S(1)}, u32[]{:S(2)}, u32[]{:S(2)}) collective-permute-start(bf16[80,256]{1,0:T(8,128)(2,1)S(1)} %get-tuple-element.39), channel_id=1, source_target_pairs={{0,4},{4,0},{8,12},{12,8},{16,20},{20,16},{24,28},{28,24},{1,2},{5... | collective-permute-start | bytes 122888 | tf_op jit(solution)/shard_map/ppermute | solution.py:561

commit v11 on v10

--- a/solution.py
+++ b/solution.py
@@ -253,13 +253,13 @@
     fields_ref,
     lon_x_in,
     lon_y_in,
-    early_y_in,
+    early_x_in,
     force_ref,
     lon_x_ref,
     lon_y_ref,
     lat_x_ref,
     lat_y_ref,
-    early_y_ref,
+    early_x_ref,
 ):
     windows, _, rows, cols = current_ref.shape
     weights = side_ref[:, rows:]
@@ -294,11 +294,11 @@
 
     for ref, north in ((lat_x_ref, northward), (lat_y_ref, jnp.logical_not(northward))):
         pack_rows(ref, 0, groups, depths, value_of, north, rows)
-    early_y_ref[...] = early_y_in[...]
+    early_x_ref[...] = early_x_in[...]
 
 
 def corner_kernel(
-    margin, rows, lat_x_in, lat_y_in, lon_x_ref, lon_y_ref, early_x_ref, lat_x_ref, lat_y_ref
+    margin, rows, lat_x_in, lat_y_in, lon_x_ref, lon_y_ref, early_y_ref, lat_x_ref, lat_y_ref
 ):
     for old_ref, ref, north in (
         (lat_x_in, lat_x_ref, even("lat")),
@@ -647,7 +647,7 @@
         )
     )
 
-    early_x = lat_exchange(lat_x, 0)
+    early_y = lat_exchange(lat_y, 1)
     current = pl.pallas_call(
         side_kernel,
         out_shape=shape(wind_stress.shape),
@@ -657,7 +657,7 @@
         cost_estimate=pl.CostEstimate(flops=1, bytes_accessed=1, transcendentals=0),
         name="side",
     )(side, tile_x, current)
-    force, lon_x, lon_y, late_x, late_y, lat_y = pl.pallas_call(
+    force, lon_x, lon_y, late_x, late_y, lat_x = pl.pallas_call(
         functools.partial(force_kernel, margin, early),
         out_shape=(
             shape((2 * windows, rows, cols)),
@@ -672,10 +672,10 @@
         compiler_params=params(),
         cost_estimate=pl.CostEstimate(flops=1, bytes_accessed=1, transcendentals=0),
         name="force",
-    )(side, tile_y, current, fields, lon_x, lon_y, lat_y)
+    )(side, tile_y, current, fields, lon_x, lon_y, lat_x)
 
     lon_x, lon_y = lon_exchange(lon_x, lon_y)
-    early_y = lat_exchange(lat_y, 1)
+    early_x = lat_exchange(lat_x, 0)
     message = shape((late_rows + 2 * margin, cols), bf16)
     late_x, late_y = pl.pallas_call(
         functools.partial(corner_kernel, margin, rows),
@@ -685,7 +685,7 @@
         compiler_params=params(),
         cost_estimate=pl.CostEstimate(flops=1, bytes_accessed=1, transcendentals=0),
         name="corner",
-    )(late_x, late_y, lon_x, lon_y, early_x)
+    )(late_x, late_y, lon_x, lon_y, early_y)
     late_x, late_y = lat_exchange(late_x, 0), lat_exchange(late_y, 1)
 
     steps = SUB * windows

time: 21.1 us -> 21 us (level)
  waiting for transfers between devices: 2.35 us -> 1.21 us
  starting transfers between devices: 9.85 us -> 10.8 us
    ppermute x1, waiting for transfers between devices: 1.74 us -> 0.01 us  [lon_exchange(): lax.ppermute(y, 'lon', lon_swaps(1))]
    ppermute x6, starting transfers between devices: 7.23 us -> 8 us  [lat_exchange(): return lax.ppermute(x, ('lon', 'lat'), lat_swaps(first))]
    ppermute x6, waiting for transfers between devices: 0.6 us -> 1.21 us  [lat_exchange(): return lax.ppermute(x, ('lon', 'lat'), lat_swaps(first))]
where the time goes in v11:
time: 21 us; the launch traced here: 20.8 us
  starting transfers between devices  10.8 us (51%)
  Pallas kernels  8.11 us (39%)
  waiting for transfers between devices  1.21 us (6%)
  between operations  0.71 us (3%)
    ppermute x6, starting transfers between devices, lat_exchange(): return lax.ppermute(x, ('lon', 'lat'), lat_swaps(first))  8 us
    pallas_call x1, Pallas kernels, local(): pl.pallas_call(functools.partial(rim_kernel, margin, early, count, lax.ax...  2.73 us
    ppermute x1, starting transfers between devices, lon_exchange(): lax.ppermute(y, 'lon', lon_swaps(1))  2.71 us
    pallas_call x1, Pallas kernels, local(): pl.pallas_call(functools.partial(interior_kernel, margin, lax.axis_size('...  2.54 us
    pallas_call x1, Pallas kernels, local(): pl.pallas_call(functools.partial(local_kernel, margin), out_shape=(shape(...  2.34 us
    ppermute x6, waiting for transfers between devices, lat_exchange(): return lax.ppermute(x, ('lon', 'lat'), lat_swaps(first))  1.21 us
  transfers between devices with their start and end apart: 8, of which 2 were waited for; matrix products, arithmetic and copies ran while one was open for 0% of the time, Pallas kernels for 26%

profile of v11, /device:TPU:0, one launch (start us, length us, event | category | flops | bytes accessed | tf_op | source)
XLA Modules:
  0.0 20.8 jit_solution(8048776680421234546)
XLA Ops:
  0.6 3.1 %collective-permute-start.1 = (bf16[2,2,64,256]{3,2,1,0:T(8,128)(2,1)}, bf16[2,2,64,256]{3,2,1,0:T(8,128)(2,1)S(1)}, u32[]{:S(2)}, u32[]{:S(2)}) collective-permute-start(bf16[2,2,64,256]{3,2,1,0:T(8,128)(2,1)} %ocean_hbm.1), channel_id=1, source_target_pairs={{0,1},{4,5},{8,9},{12,13},{16,17},{20,21},{24,25},{28,29},{1,0},{5... | collective-permute-start | bytes 393224 | tf_op jit(solution)/shard_map/ppermute | solution.py:561
  3.7 0.0 collective-permute-start
  3.7 2.3 %local.1 = (f32[6,64,256]{2,1,0:T(8,128)}, f32[9,64,256]{2,1,0:T(8,128)S(1)}, f32[2,2,64,256]{3,2,1,0:T(8,128)S(1)}, bf16[64,128]{1,0:T(8,128)(2,1)S(1)}, bf16[6...) custom-call(s32[1,16]{1,0:T(1,128)} %covered_hbm.1, ...), custom_call_target="tpu_custom_call" | custom-call | flops 9830400 | bytes 1179648 | tf_op jit(solution)/shard_map/local/pallas_call | solution.py:597
  6.1 0.6 %collective-permute-start.4 = (bf16[128,256]{1,0:T(8,128)(2,1)S(1)}, bf16[128,256]{1,0:T(8,128)(2,1)S(1)}, u32[]{:S(2)}, u32[]{:S(2)}) collective-permute-start(bf16[128,256]{1,0:T(8,128)(2,1)S(1)} %get-tuple-element.37), channel_id=1, source_target_pairs={{0,4},{4,0},{8,12},{12,8},{16,20},{20,16},{24,28},{28,24},{1,2},{5... | collective-permute-start | bytes 196616 | tf_op jit(solution)/shard_map/ppermute | solution.py:561
  6.6 0.8 %collective-permute-done.1.tile_ref = bf16[2,2,64,256]{3,2,1,0:T(8,128)(2,1)S(1)} collective-permute-done((bf16[2,2,64,256]{3,2,1,0:T(8,128)(2,1)}, bf16[2,2,64,256]{3,2,1,0:T(8,128)(2,1)S(1)}, u32[]{:S(2)}, u32[]{:S(2)}) %collective-permute-start.1) | collective-permute-done | bytes 131104 | tf_op jit(solution)/shard_map/ppermute | solution.py:561
  7.4 0.2 side.1.current_ref
  7.6 0.0 collective-permute-done.tile_ref
  7.6 0.3 %force.1 = (f32[4,64,256]{2,1,0:T(8,128)S(1)}, bf16[64,256]{1,0:T(8,128)(2,1)S(1)}, bf16[64,256]{1,0:T(8,128)(2,1)S(1)}, bf16[48,256]{1,0:T(8,128)(2,1)S(1)}, bf...) custom-call(bf16[64,128]{1,0:T(8,128)(2,1)S(1)} %get-tuple-element.27.side_ref, ...), custom_call_target="tpu_custom_call" | custom-call | flops 1 | bytes 1 | tf_op jit(solution)/shard_map/force/pallas_call | solution.py:660
  7.9 0.1 collective-permute-start.2
  8.0 2.7 %collective-permute-start.3 = (bf16[64,256]{1,0:T(8,128)(2,1)S(1)}, bf16[64,256]{1,0:T(8,128)(2,1)S(1)}, u32[]{:S(2)}, u32[]{:S(2)}) collective-permute-start(bf16[64,256]{1,0:T(8,128)(2,1)S(1)} %get-tuple-element.36), channel_id=1, source_target_pairs={{4,8},{12,16},{20,24},{28,0},{8,4},{16,12},{24,20},{0,28},{5,9},{1... | collective-permute-start | bytes 98312 | tf_op jit(solution)/shard_map/ppermute | solution.py:557
  10.7 2.6 %collective-permute-start.7 = (bf16[128,256]{1,0:T(8,128)(2,1)S(1)}, bf16[128,256]{1,0:T(8,128)(2,1)S(1)}, u32[]{:S(2)}, u32[]{:S(2)}) collective-permute-start(bf16[128,256]{1,0:T(8,128)(2,1)S(1)} %get-tuple-element.41), channel_id=1, source_target_pairs={{0,1},{4,5},{8,9},{12,13},{16,17},{20,21},{24,25},{28,29},{1,0},{5... | collective-permute-start | bytes 196616 | tf_op jit(solution)/shard_map/ppermute | solution.py:561
  13.3 0.0 collective-permute-done.4.early_y_ref
  13.3 0.0 collective-permute-done.2.lon_x_ref
  13.3 0.0 collective-permute-done.3.lon_y_ref
  13.3 1.8 %collective-permute-start.5 = (bf16[80,256]{1,0:T(8,128)(2,1)S(1)}, bf16[80,256]{1,0:T(8,128)(2,1)S(1)}, u32[]{:S(2)}, u32[]{:S(2)}) collective-permute-start(bf16[80,256]{1,0:T(8,128)(2,1)S(1)} %get-tuple-element.38), channel_id=1, source_target_pairs={{0,1},{4,5},{8,9},{12,13},{16,17},{20,21},{24,25},{28,29},{1,0},{5... | collective-permute-start | bytes 122888 | tf_op jit(solution)/shard_map/ppermute | solution.py:561
  15.1 0.0 collective-permute-start.6
  15.1 0.4 %collective-permute-done.7.early_x_ref = bf16[128,256]{1,0:T(8,128)(2,1)S(1)} collective-permute-done((bf16[128,256]{1,0:T(8,128)(2,1)S(1)}, bf16[128,256]{1,0:T(8,128)(2,1)S(1)}, u32[]{:S(2)}, u32[]{:S(2)}) %collective-permute-start.7) | collective-permute-done | bytes 65568 | tf_op jit(solution)/shard_map/ppermute | solution.py:561
  15.5 2.5 %interior.1 = (f32[9,2,3,96,128]{4,3,2,1,0:T(8,128)S(1)}, f32[9,3,3,96,128]{4,3,2,1,0:T(8,128)S(1)}, f32[2,3,96,128]{3,2,1,0:T(8,128)S(1)}, f32[2,3,96,128]{3,2,...) custom-call(f32[9,64,256]{2,1,0:T(8,128)S(1)} %get-tuple-element.29.fields_ref, ...), custom_call_target="tpu_custom_call" | custom-call | flops 7864320 | bytes 4194304 | tf_op jit(solution)/shard_map/interior/pallas_call | solution.py:705
  18.1 0.0 collective-permute-done.5.args_0_
  18.1 0.0 collective-permute-done.6.args_1_
  18.1 2.7 %rim.1 = (f32[2,64,256]{2,1,0:T(8,128)}, f32[3,64,256]{2,1,0:T(8,128)}, f32[9,2,3,96,128]{4,3,2,1,0:T(8,128)S(1)}, f32[9,3,3,96,128]{4,3,2,1,0:T(8,128)S(1)}, f3...) custom-call(bf16[80,256]{1,0:T(8,128)(2,1)S(1)} %collective-permute-, ...), custom_call_target="tpu_custom_call", output_to_operand_aliasing={{2}: (2, {}), {3}: (3, {}), {4}: (4, {}), {5}: (5, {}), {6}... | custom-call | tf_op jit(solution)/shard_map/rim/pallas_call | solution.py:717
  (1 shorter events, 0.0 us)
Async XLA Ops:
  0.6 6.8 %collective-permute-start.1 = (bf16[2,2,64,256]{3,2,1,0:T(8,128)(2,1)}, bf16[2,2,64,256]{3,2,1,0:T(8,128)(2,1)S(1)}, u32[]{:S(2)}, u32[]{:S(2)}) collective-permute-start(bf16[2,2,64,256]{3,2,1,0:T(8,128)(2,1)} %ocean_hbm.1), channel_id=1, source_target_pairs={{0,1},{4,5},{8,9},{12,13},{16,17},{20,21},{24,25},{28,29},{1,0},{5... | collective-permute-start | bytes 393224 | tf_op jit(solution)/shard_map/ppermute | solution.py:561
  3.7 3.9 %collective-permute-start = (bf16[2,2,64,256]{3,2,1,0:T(8,128)(2,1)}, bf16[2,2,64,256]{3,2,1,0:T(8,128)(2,1)S(1)}, u32[]{:S(2)}, u32[]{:S(2)}) collective-permute-start(bf16[2,2,64,256]{3,2,1,0:T(8,128)(2,1)} %ocean_hbm.1), channel_id=1, source_target_pairs={{0,4},{4,0},{8,12},{12,8},{16,20},{20,16},{24,28},{28,24},{1,2},{5... | collective-permute-start | bytes 393224 | tf_op jit(solution)/shard_map/ppermute | solution.py:561
  6.1 7.2 %collective-permute-start.4 = (bf16[128,256]{1,0:T(8,128)(2,1)S(1)}, bf16[128,256]{1,0:T(8,128)(2,1)S(1)}, u32[]{:S(2)}, u32[]{:S(2)}) collective-permute-start(bf16[128,256]{1,0:T(8,128)(2,1)S(1)} %get-tuple-element.37), channel_id=1, source_target_pairs={{0,4},{4,0},{8,12},{12,8},{16,20},{20,16},{24,28},{28,24},{1,2},{5... | collective-permute-start | bytes 196616 | tf_op jit(solution)/shard_map/ppermute | solution.py:561
  7.9 5.3 %collective-permute-start.2 = (bf16[64,256]{1,0:T(8,128)(2,1)S(1)}, bf16[64,256]{1,0:T(8,128)(2,1)S(1)}, u32[]{:S(2)}, u32[]{:S(2)}) collective-permute-start(bf16[64,256]{1,0:T(8,128)(2,1)S(1)} %get-tuple-element.35), channel_id=1, source_target_pairs={{0,4},{8,12},{16,20},{24,28},{4,0},{12,8},{20,16},{28,24},{1,5},{9... | collective-permute-start | bytes 98312 | tf_op jit(solution)/shard_map/ppermute | solution.py:557
  8.0 5.3 %collective-permute-start.3 = (bf16[64,256]{1,0:T(8,128)(2,1)S(1)}, bf16[64,256]{1,0:T(8,128)(2,1)S(1)}, u32[]{:S(2)}, u32[]{:S(2)}) collective-permute-start(bf16[64,256]{1,0:T(8,128)(2,1)S(1)} %get-tuple-element.36), channel_id=1, source_target_pairs={{4,8},{12,16},{20,24},{28,0},{8,4},{16,12},{24,20},{0,28},{5,9},{1... | collective-permute-start | bytes 98312 | tf_op jit(solution)/shard_map/ppermute | solution.py:557
  10.7 4.8 %collective-permute-start.7 = (bf16[128,256]{1,0:T(8,128)(2,1)S(1)}, bf16[128,256]{1,0:T(8,128)(2,1)S(1)}, u32[]{:S(2)}, u32[]{:S(2)}) collective-permute-start(bf16[128,256]{1,0:T(8,128)(2,1)S(1)} %get-tuple-element.41), channel_id=1, source_target_pairs={{0,1},{4,5},{8,9},{12,13},{16,17},{20,21},{24,25},{28,29},{1,0},{5... | collective-permute-start | bytes 196616 | tf_op jit(solution)/shard_map/ppermute | solution.py:561
  13.3 4.8 %collective-permute-start.5 = (bf16[80,256]{1,0:T(8,128)(2,1)S(1)}, bf16[80,256]{1,0:T(8,128)(2,1)S(1)}, u32[]{:S(2)}, u32[]{:S(2)}) collective-permute-start(bf16[80,256]{1,0:T(8,128)(2,1)S(1)} %get-tuple-element.38), channel_id=1, source_target_pairs={{0,1},{4,5},{8,9},{12,13},{16,17},{20,21},{24,25},{28,29},{1,0},{5... | collective-permute-start | bytes 122888 | tf_op jit(solution)/shard_map/ppermute | solution.py:561
  15.1 3.0 %collective-permute-start.6 = (bf16[80,256]{1,0:T(8,128)(2,1)S(1)}, bf16[80,256]{1,0:T(8,128)(2,1)S(1)}, u32[]{:S(2)}, u32[]{:S(2)}) collective-permute-start(bf16[80,256]{1,0:T(8,128)(2,1)S(1)} %get-tuple-element.39), channel_id=1, source_target_pairs={{0,4},{4,0},{8,12},{12,8},{16,20},{20,16},{24,28},{28,24},{1,2},{5... | collective-permute-start | bytes 122888 | tf_op jit(solution)/shard_map/ppermute | solution.py:561

commit v12 on v11

--- a/solution.py
+++ b/solution.py
@@ -474,14 +474,14 @@
     place_rows(refs, early, range(early), margin, rows, lat_count, early_x_ref, early_y_ref)
     for window in range(windows):
         lost = 2 * SUB * window
-        row_list = range(margin + lost, margin + rows - lost, GROUP)
+        row_list = range(margin + lost, margin + rows - lost, 8)
 
         def subcycle(number, carry):
             step = window * SUB + number
             for row in row_list:
-                stress_rows(refs, step, window, row)
+                stress_rows(refs, step, window, row, 8)
             for row in row_list:
-                velocity_rows(refs, step, window, row)
+                velocity_rows(refs, step, window, row, 8)
             return carry
 
         lax.fori_loop(0, SUB, subcycle, 0)

time: 21 us -> 20.9 us (level)
  transfers between devices with their start and end apart: 8 -> 8, of which waited for: 2 -> 2; matrix products, arithmetic and copies ran while one was open for 0% -> 0% of each run, Pallas kernels for 26% -> 25%
where the time goes in v12:
time: 20.9 us; the launch traced here: 20.7 us
  starting transfers between devices  10.8 us (52%)
  Pallas kernels  8.01 us (38%)
  waiting for transfers between devices  1.21 us (6%)
  between operations  0.71 us (3%)
    ppermute x6, starting transfers between devices, lat_exchange(): return lax.ppermute(x, ('lon', 'lat'), lat_swaps(first))  8 us
    pallas_call x1, Pallas kernels, local(): pl.pallas_call(functools.partial(rim_kernel, margin, early, count, lax.ax...  2.73 us
    ppermute x1, starting transfers between devices, lon_exchange(): lax.ppermute(y, 'lon', lon_swaps(1))  2.71 us
    pallas_call x1, Pallas kernels, local(): pl.pallas_call(functools.partial(interior_kernel, margin, lax.axis_size('...  2.43 us
    pallas_call x1, Pallas kernels, local(): pl.pallas_call(functools.partial(local_kernel, margin), out_shape=(shape(...  2.34 us
    ppermute x6, waiting for transfers between devices, lat_exchange(): return lax.ppermute(x, ('lon', 'lat'), lat_swaps(first))  1.21 us
  transfers between devices with their start and end apart: 8, of which 2 were waited for; matrix products, arithmetic and copies ran while one was open for 0% of the time, Pallas kernels for 25%

profile of v12, /device:TPU:0, one launch (start us, length us, event | category | flops | bytes accessed | tf_op | source)
XLA Modules:
  0.0 20.7 jit_solution(5982270651437031279)
XLA Ops:
  0.6 3.1 %collective-permute-start.1 = (bf16[2,2,64,256]{3,2,1,0:T(8,128)(2,1)}, bf16[2,2,64,256]{3,2,1,0:T(8,128)(2,1)S(1)}, u32[]{:S(2)}, u32[]{:S(2)}) collective-permute-start(bf16[2,2,64,256]{3,2,1,0:T(8,128)(2,1)} %ocean_hbm.1), channel_id=1, source_target_pairs={{0,1},{4,5},{8,9},{12,13},{16,17},{20,21},{24,25},{28,29},{1,0},{5... | collective-permute-start | bytes 393224 | tf_op jit(solution)/shard_map/ppermute | solution.py:561
  3.7 0.0 collective-permute-start
  3.7 2.3 %local.1 = (f32[6,64,256]{2,1,0:T(8,128)}, f32[9,64,256]{2,1,0:T(8,128)S(1)}, f32[2,2,64,256]{3,2,1,0:T(8,128)S(1)}, bf16[64,128]{1,0:T(8,128)(2,1)S(1)}, bf16[6...) custom-call(s32[1,16]{1,0:T(1,128)} %covered_hbm.1, ...), custom_call_target="tpu_custom_call" | custom-call | flops 9830400 | bytes 1179648 | tf_op jit(solution)/shard_map/local/pallas_call | solution.py:597
  6.1 0.6 %collective-permute-start.4 = (bf16[128,256]{1,0:T(8,128)(2,1)S(1)}, bf16[128,256]{1,0:T(8,128)(2,1)S(1)}, u32[]{:S(2)}, u32[]{:S(2)}) collective-permute-start(bf16[128,256]{1,0:T(8,128)(2,1)S(1)} %get-tuple-element.37), channel_id=1, source_target_pairs={{0,4},{4,0},{8,12},{12,8},{16,20},{20,16},{24,28},{28,24},{1,2},{5... | collective-permute-start | bytes 196616 | tf_op jit(solution)/shard_map/ppermute | solution.py:561
  6.6 0.8 %collective-permute-done.1.tile_ref = bf16[2,2,64,256]{3,2,1,0:T(8,128)(2,1)S(1)} collective-permute-done((bf16[2,2,64,256]{3,2,1,0:T(8,128)(2,1)}, bf16[2,2,64,256]{3,2,1,0:T(8,128)(2,1)S(1)}, u32[]{:S(2)}, u32[]{:S(2)}) %collective-permute-start.1) | collective-permute-done | bytes 131104 | tf_op jit(solution)/shard_map/ppermute | solution.py:561
  7.4 0.2 side.1.current_ref
  7.6 0.0 collective-permute-done.tile_ref
  7.6 0.3 %force.1 = (f32[4,64,256]{2,1,0:T(8,128)S(1)}, bf16[64,256]{1,0:T(8,128)(2,1)S(1)}, bf16[64,256]{1,0:T(8,128)(2,1)S(1)}, bf16[48,256]{1,0:T(8,128)(2,1)S(1)}, bf...) custom-call(bf16[64,128]{1,0:T(8,128)(2,1)S(1)} %get-tuple-element.27.side_ref, ...), custom_call_target="tpu_custom_call" | custom-call | flops 1 | bytes 1 | tf_op jit(solution)/shard_map/force/pallas_call | solution.py:660
  7.9 0.1 collective-permute-start.2
  8.0 2.7 %collective-permute-start.3 = (bf16[64,256]{1,0:T(8,128)(2,1)S(1)}, bf16[64,256]{1,0:T(8,128)(2,1)S(1)}, u32[]{:S(2)}, u32[]{:S(2)}) collective-permute-start(bf16[64,256]{1,0:T(8,128)(2,1)S(1)} %get-tuple-element.36), channel_id=1, source_target_pairs={{4,8},{12,16},{20,24},{28,0},{8,4},{16,12},{24,20},{0,28},{5,9},{1... | collective-permute-start | bytes 98312 | tf_op jit(solution)/shard_map/ppermute | solution.py:557
  10.7 2.6 %collective-permute-start.7 = (bf16[128,256]{1,0:T(8,128)(2,1)S(1)}, bf16[128,256]{1,0:T(8,128)(2,1)S(1)}, u32[]{:S(2)}, u32[]{:S(2)}) collective-permute-start(bf16[128,256]{1,0:T(8,128)(2,1)S(1)} %get-tuple-element.41), channel_id=1, source_target_pairs={{0,1},{4,5},{8,9},{12,13},{16,17},{20,21},{24,25},{28,29},{1,0},{5... | collective-permute-start | bytes 196616 | tf_op jit(solution)/shard_map/ppermute | solution.py:561
  13.3 0.0 collective-permute-done.4.early_y_ref
  13.3 0.0 collective-permute-done.2.lon_x_ref
  13.3 0.0 collective-permute-done.3.lon_y_ref
  13.3 1.8 %collective-permute-start.5 = (bf16[80,256]{1,0:T(8,128)(2,1)S(1)}, bf16[80,256]{1,0:T(8,128)(2,1)S(1)}, u32[]{:S(2)}, u32[]{:S(2)}) collective-permute-start(bf16[80,256]{1,0:T(8,128)(2,1)S(1)} %get-tuple-element.38), channel_id=1, source_target_pairs={{0,1},{4,5},{8,9},{12,13},{16,17},{20,21},{24,25},{28,29},{1,0},{5... | collective-permute-start | bytes 122888 | tf_op jit(solution)/shard_map/ppermute | solution.py:561
  15.1 0.0 collective-permute-start.6
  15.1 0.4 %collective-permute-done.7.early_x_ref = bf16[128,256]{1,0:T(8,128)(2,1)S(1)} collective-permute-done((bf16[128,256]{1,0:T(8,128)(2,1)S(1)}, bf16[128,256]{1,0:T(8,128)(2,1)S(1)}, u32[]{:S(2)}, u32[]{:S(2)}) %collective-permute-start.7) | collective-permute-done | bytes 65568 | tf_op jit(solution)/shard_map/ppermute | solution.py:561
  15.5 2.4 %interior.1 = (f32[9,2,3,96,128]{4,3,2,1,0:T(8,128)S(1)}, f32[9,3,3,96,128]{4,3,2,1,0:T(8,128)S(1)}, f32[2,3,96,128]{3,2,1,0:T(8,128)S(1)}, f32[2,3,96,128]{3,2,...) custom-call(f32[9,64,256]{2,1,0:T(8,128)S(1)} %get-tuple-element.29.fields_ref, ...), custom_call_target="tpu_custom_call" | custom-call | flops 7864320 | bytes 4194304 | tf_op jit(solution)/shard_map/interior/pallas_call | solution.py:705
  18.0 0.0 collective-permute-done.5.args_0_
  18.0 0.0 collective-permute-done.6.args_1_
  18.0 2.7 %rim.1 = (f32[2,64,256]{2,1,0:T(8,128)}, f32[3,64,256]{2,1,0:T(8,128)}, f32[9,2,3,96,128]{4,3,2,1,0:T(8,128)S(1)}, f32[9,3,3,96,128]{4,3,2,1,0:T(8,128)S(1)}, f3...) custom-call(bf16[80,256]{1,0:T(8,128)(2,1)S(1)} %collective-permute-, ...), custom_call_target="tpu_custom_call", output_to_operand_aliasing={{2}: (2, {}), {3}: (3, {}), {4}: (4, {}), {5}: (5, {}), {6}... | custom-call | tf_op jit(solution)/shard_map/rim/pallas_call | solution.py:717
  (1 shorter events, 0.0 us)
Async XLA Ops:
  0.6 6.8 %collective-permute-start.1 = (bf16[2,2,64,256]{3,2,1,0:T(8,128)(2,1)}, bf16[2,2,64,256]{3,2,1,0:T(8,128)(2,1)S(1)}, u32[]{:S(2)}, u32[]{:S(2)}) collective-permute-start(bf16[2,2,64,256]{3,2,1,0:T(8,128)(2,1)} %ocean_hbm.1), channel_id=1, source_target_pairs={{0,1},{4,5},{8,9},{12,13},{16,17},{20,21},{24,25},{28,29},{1,0},{5... | collective-permute-start | bytes 393224 | tf_op jit(solution)/shard_map/ppermute | solution.py:561
  3.7 3.9 %collective-permute-start = (bf16[2,2,64,256]{3,2,1,0:T(8,128)(2,1)}, bf16[2,2,64,256]{3,2,1,0:T(8,128)(2,1)S(1)}, u32[]{:S(2)}, u32[]{:S(2)}) collective-permute-start(bf16[2,2,64,256]{3,2,1,0:T(8,128)(2,1)} %ocean_hbm.1), channel_id=1, source_target_pairs={{0,4},{4,0},{8,12},{12,8},{16,20},{20,16},{24,28},{28,24},{1,2},{5... | collective-permute-start | bytes 393224 | tf_op jit(solution)/shard_map/ppermute | solution.py:561
  6.1 7.2 %collective-permute-start.4 = (bf16[128,256]{1,0:T(8,128)(2,1)S(1)}, bf16[128,256]{1,0:T(8,128)(2,1)S(1)}, u32[]{:S(2)}, u32[]{:S(2)}) collective-permute-start(bf16[128,256]{1,0:T(8,128)(2,1)S(1)} %get-tuple-element.37), channel_id=1, source_target_pairs={{0,4},{4,0},{8,12},{12,8},{16,20},{20,16},{24,28},{28,24},{1,2},{5... | collective-permute-start | bytes 196616 | tf_op jit(solution)/shard_map/ppermute | solution.py:561
  7.9 5.3 %collective-permute-start.2 = (bf16[64,256]{1,0:T(8,128)(2,1)S(1)}, bf16[64,256]{1,0:T(8,128)(2,1)S(1)}, u32[]{:S(2)}, u32[]{:S(2)}) collective-permute-start(bf16[64,256]{1,0:T(8,128)(2,1)S(1)} %get-tuple-element.35), channel_id=1, source_target_pairs={{0,4},{8,12},{16,20},{24,28},{4,0},{12,8},{20,16},{28,24},{1,5},{9... | collective-permute-start | bytes 98312 | tf_op jit(solution)/shard_map/ppermute | solution.py:557
  8.0 5.3 %collective-permute-start.3 = (bf16[64,256]{1,0:T(8,128)(2,1)S(1)}, bf16[64,256]{1,0:T(8,128)(2,1)S(1)}, u32[]{:S(2)}, u32[]{:S(2)}) collective-permute-start(bf16[64,256]{1,0:T(8,128)(2,1)S(1)} %get-tuple-element.36), channel_id=1, source_target_pairs={{4,8},{12,16},{20,24},{28,0},{8,4},{16,12},{24,20},{0,28},{5,9},{1... | collective-permute-start | bytes 98312 | tf_op jit(solution)/shard_map/ppermute | solution.py:557
  10.7 4.8 %collective-permute-start.7 = (bf16[128,256]{1,0:T(8,128)(2,1)S(1)}, bf16[128,256]{1,0:T(8,128)(2,1)S(1)}, u32[]{:S(2)}, u32[]{:S(2)}) collective-permute-start(bf16[128,256]{1,0:T(8,128)(2,1)S(1)} %get-tuple-element.41), channel_id=1, source_target_pairs={{0,1},{4,5},{8,9},{12,13},{16,17},{20,21},{24,25},{28,29},{1,0},{5... | collective-permute-start | bytes 196616 | tf_op jit(solution)/shard_map/ppermute | solution.py:561
  13.3 4.6 %collective-permute-start.5 = (bf16[80,256]{1,0:T(8,128)(2,1)S(1)}, bf16[80,256]{1,0:T(8,128)(2,1)S(1)}, u32[]{:S(2)}, u32[]{:S(2)}) collective-permute-start(bf16[80,256]{1,0:T(8,128)(2,1)S(1)} %get-tuple-element.38), channel_id=1, source_target_pairs={{0,1},{4,5},{8,9},{12,13},{16,17},{20,21},{24,25},{28,29},{1,0},{5... | collective-permute-start | bytes 122888 | tf_op jit(solution)/shard_map/ppermute | solution.py:561
  15.1 2.9 %collective-permute-start.6 = (bf16[80,256]{1,0:T(8,128)(2,1)S(1)}, bf16[80,256]{1,0:T(8,128)(2,1)S(1)}, u32[]{:S(2)}, u32[]{:S(2)}) collective-permute-start(bf16[80,256]{1,0:T(8,128)(2,1)S(1)} %get-tuple-element.39), channel_id=1, source_target_pairs={{0,4},{4,0},{8,12},{12,8},{16,20},{20,16},{24,28},{28,24},{1,2},{5... | collective-permute-start | bytes 122888 | tf_op jit(solution)/shard_map/ppermute | solution.py:561
